TPU v7x, 512 devices: a whole 4x8x8 slice. The times are simulated.
512 devices in a mesh: uly: 32 (over z_hi, x, core), blk: 16 (over y, z_lo).
Axes of the slice: x: 4, y: 8, z: 8 (z_hi: 4, z_lo: 2; z = z_hi * 2 + z_lo), core: 2. Of those that a mesh axis runs over, the one named last changes fastest.
Arguments:
- packed_queries: bfloat16 [65536, 4096], P(('blk', 'uly')), may hold values from -8 to 8
- packed_keys: bfloat16 [65536, 256], P(('blk', 'uly')), may hold values from -8 to 8
- packed_values: bfloat16 [65536, 256], P(('blk', 'uly')), may hold values from -6 to 6
- output_cotangent: bfloat16 [65536, 4096], P(('blk', 'uly')), may hold values from -6 to 6
- doc_offsets: int32 [130], replicated, may hold values from 0 to 65536, as said below
Outputs:
- attended: bfloat16 [65536, 4096], P(('blk', 'uly'))
- grad_queries: bfloat16 [65536, 4096], P(('blk', 'uly'))
- keys_gradient: bfloat16 [65536, 256], P(('blk', 'uly'))
- values_gradient: bfloat16 [65536, 256], P(('blk', 'uly'))
Inputs may be any that keep to these rules, and one draw needn't show every extreme that they name: doc_offsets never fall; the first is 0 and the last 65536; each document, from one offset to the next, is 256 to 1024 tokens long and starts at a multiple of 128; some document is exactly 1024 long.
All inputs are finite; a program needn't handle non-finite values.
Results may differ from a plain program's by a relative error of at most 0.04.
Values may be sent and summed in bfloat16 or wider, within the bound.
No kernel may reach another device: no remote copies, remote signals or barrier semaphores. Data moves between devices by JAX's collectives and lax.ppermute only.
A program may use at most 64 MiB of HBM per device.

v0:
```python
import math

import jax
import jax.numpy as jnp
from jax import lax
from jax.sharding import PartitionSpec as P

HEAD_SIZE = 128


def from_behind(block, axis, distance):
    devices = range(lax.axis_size(axis))
    route = [(i - distance, i) for i in devices if i - distance in devices]
    return lax.ppermute(block, axis, route)


def doc_starts(doc_offsets, positions):
    return jnp.max(
        jnp.where(doc_offsets[None, :] <= positions[:, None], doc_offsets[None, :], 0), axis=1
    )


def allowed(query_pos, key_pos, starts):
    return (key_pos[None, :] <= query_pos[:, None]) & (key_pos[None, :] >= starts[:, None])


def attend_block(query_blk, key_win, value_win, visible, cot_blk, score_scale):
    scores = (
        jnp.einsum("tcgd,wcd->cgtw", query_blk, key_win, preferred_element_type=jnp.float32)
        * score_scale
    )
    scores = jnp.where(visible[None, None], scores, -jnp.inf)
    row_max = jnp.max(scores, axis=-1, keepdims=True)
    row_sum = jnp.sum(jnp.exp(scores - row_max), axis=-1, keepdims=True)
    log_total = row_max + jnp.log(row_sum)
    weights = jnp.exp(scores - log_total)
    weights_low = weights.astype(jnp.bfloat16)
    attended_b = jnp.einsum(
        "cgtw,wcd->tcgd", weights_low, value_win, preferred_element_type=jnp.float32
    ).astype(jnp.bfloat16)
    row_delta = jnp.einsum(
        "tcgd,tcgd->cgt", cot_blk, attended_b, preferred_element_type=jnp.float32
    )
    value_grad = jnp.einsum(
        "cgtw,tcgd->wcd", weights_low, cot_blk, preferred_element_type=jnp.float32
    )
    grad_probs = jnp.einsum(
        "tcgd,wcd->cgtw", cot_blk, value_win, preferred_element_type=jnp.float32
    )
    grad_scores = (weights * (grad_probs - row_delta[..., None])).astype(jnp.bfloat16)
    query_grad = (
        jnp.einsum("cgtw,wcd->tcgd", grad_scores, key_win, preferred_element_type=jnp.float32)
        * score_scale
    ).astype(jnp.bfloat16)
    key_grad = (
        jnp.einsum("cgtw,tcgd->wcd", grad_scores, query_blk, preferred_element_type=jnp.float32)
        * score_scale
    )
    return (attended_b, query_grad, key_grad, value_grad)


def shards(packed_queries, packed_keys, packed_values, output_cotangent, doc_offsets):
    head_dim = HEAD_SIZE
    lane_count = lax.axis_size("uly")
    cycle_pos = lax.axis_index("blk")
    tok_dev = packed_queries.shape[0]
    heads_all = packed_queries.shape[1] // head_dim
    kv_all = packed_keys.shape[1] // head_dim
    region = tok_dev * lane_count
    longest = 8 * (region // 32)
    score_scale = 1.0 / math.sqrt(head_dim)
    per_dev = heads_all // lane_count
    copies = lane_count // kv_all

    def to_slots(states):
        spread = jnp.broadcast_to(
            states.reshape(tok_dev, kv_all, 1, head_dim), (tok_dev, kv_all, copies, head_dim)
        )
        return spread.reshape(tok_dev, lane_count * head_dim)

    query_heads, key_own, value_own, cot_heads = (
        lax.all_to_all(packed_queries, "uly", split_axis=1, concat_axis=0, tiled=True),
        lax.all_to_all(to_slots(packed_keys), "uly", split_axis=1, concat_axis=0, tiled=True),
        lax.all_to_all(to_slots(packed_values), "uly", split_axis=1, concat_axis=0, tiled=True),
        lax.all_to_all(output_cotangent, "uly", split_axis=1, concat_axis=0, tiled=True),
    )
    tail_k, tail_v = from_behind(
        (key_own[region - longest :], value_own[region - longest :]), "blk", 1
    )
    key_ext = jnp.concatenate([tail_k, key_own], 0).reshape(longest + region, 1, head_dim)
    value_ext = jnp.concatenate([tail_v, value_own], 0).reshape(longest + region, 1, head_dim)
    queries_parted = query_heads.reshape(region, 1, per_dev, head_dim)
    cotangent_parted = cot_heads.reshape(region, 1, per_dev, head_dim)
    block_rows = min(512, region)
    window_rows = block_rows + longest
    pos_base = cycle_pos * region

    def one_block(running, step_num):
        key_gradient_part, value_gradient_part = running
        row_start = step_num * block_rows
        query_blk = lax.dynamic_slice_in_dim(queries_parted, row_start, block_rows, 0)
        cot_blk = lax.dynamic_slice_in_dim(cotangent_parted, row_start, block_rows, 0)
        key_win = lax.dynamic_slice_in_dim(key_ext, row_start, window_rows, 0)
        value_win = lax.dynamic_slice_in_dim(value_ext, row_start, window_rows, 0)
        query_pos = pos_base + row_start + jnp.arange(block_rows, dtype=jnp.int32)
        key_pos = pos_base + row_start - longest + jnp.arange(window_rows, dtype=jnp.int32)
        visible = allowed(query_pos, key_pos, doc_starts(doc_offsets, query_pos))
        attended_b, query_grad, key_grad, value_grad = attend_block(
            query_blk, key_win, value_win, visible, cot_blk, score_scale
        )
        key_gradient_part = lax.dynamic_update_slice_in_dim(
            key_gradient_part,
            lax.dynamic_slice_in_dim(key_gradient_part, row_start, window_rows, 0) + key_grad,
            row_start,
            0,
        )
        value_gradient_part = lax.dynamic_update_slice_in_dim(
            value_gradient_part,
            lax.dynamic_slice_in_dim(value_gradient_part, row_start, window_rows, 0) + value_grad,
            row_start,
            0,
        )
        return ((key_gradient_part, value_gradient_part), (attended_b, query_grad))

    empty_gradients = jnp.zeros((longest + region, 1, head_dim), jnp.float32)
    (key_gradient_part, value_gradient_part), (attended_all, query_all) = lax.scan(
        one_block,
        (empty_gradients, empty_gradients),
        jnp.arange(region // block_rows, dtype=jnp.int32),
    )
    attended, grad_queries = (
        lax.all_to_all(
            attended_all.reshape(region, per_dev * head_dim),
            "uly",
            split_axis=0,
            concat_axis=1,
            tiled=True,
        ),
        lax.all_to_all(
            query_all.reshape(region, per_dev * head_dim),
            "uly",
            split_axis=0,
            concat_axis=1,
            tiled=True,
        ),
    )
    back_k, back_v = (
        from_behind(key_gradient_part[:longest, 0].astype(jnp.bfloat16), "blk", -1).astype(
            jnp.float32
        ),
        from_behind(value_gradient_part[:longest, 0].astype(jnp.bfloat16), "blk", -1).astype(
            jnp.float32
        ),
    )
    own_k = key_gradient_part[longest:, 0].at[region - longest :].add(back_k)
    own_v = value_gradient_part[longest:, 0].at[region - longest :].add(back_v)
    lane_k, lane_v = (
        lax.all_to_all(
            own_k.astype(jnp.bfloat16), "uly", split_axis=0, concat_axis=1, tiled=True
        ).astype(own_k.dtype),
        lax.all_to_all(
            own_v.astype(jnp.bfloat16), "uly", split_axis=0, concat_axis=1, tiled=True
        ).astype(own_v.dtype),
    )
    keys_gradient = (
        lane_k.reshape(tok_dev, kv_all, copies, head_dim)
        .sum(2)
        .reshape(tok_dev, kv_all * head_dim)
        .astype(jnp.bfloat16)
    )
    values_gradient = (
        lane_v.reshape(tok_dev, kv_all, copies, head_dim)
        .sum(2)
        .reshape(tok_dev, kv_all * head_dim)
        .astype(jnp.bfloat16)
    )
    return (attended, grad_queries, keys_gradient, values_gradient)


def solution(mesh):
    in_specs = (
        P(("blk", "uly"), None),
        P(("blk", "uly"), None),
        P(("blk", "uly"), None),
        P(("blk", "uly"), None),
        P(),
    )
    out_specs = (
        P(("blk", "uly"), None),
        P(("blk", "uly"), None),
        P(("blk", "uly"), None),
        P(("blk", "uly"), None),
    )
    return jax.shard_map(shards, mesh=mesh, in_specs=in_specs, out_specs=out_specs, check_vma=False)
```

profile of v0, /device:TPU:56, one launch (start us, length us, event | category | flops | bytes accessed | tf_op | source)
XLA Modules:
  0.0 505.9 jit_solution(16817914548120629789)
XLA Ops:
  2.7 13.3 %all-to-all-start.2 = ((bf16[128,32,128]{2,0,1:T(8,128)(2,1)}), bf16[128,32,128]{2,0,1:T(8,128)(2,1)S(1)}, u32[]{:S(2)}, u32[]{:S(2)}) async-start(bf16[128,32,128]{2,0,1:T(8,128)(2,1)} %bitcast.31), calls=%async_computation.2 | async-start | bytes 2097152 | tf_op jit(solution)/shard_map/all_to_all | solution.py:84
  16.0 24.5 %all-to-all-done.2 = bf16[128,32,128]{2,0,1:T(8,128)(2,1)S(1)} async-done(((bf16[128,32,128]{2,0,1:T(8,128)(2,1)}), bf16[128,32,128]{2,0,1:T(8,128)(2,1)S(1)}, u32[]{:S(2)}, u32[]{:S(2)}) %all-to-all-start.2) | async-done | bytes 1048608 | tf_op jit(solution)/shard_map/all_to_all | solution.py:84
  41.7 9.4 %all-to-all-start.1 = ((bf16[128,32,128]{2,0,1:T(8,128)(2,1)}), bf16[128,32,128]{2,0,1:T(8,128)(2,1)S(1)}, u32[]{:S(2)}, u32[]{:S(2)}) async-start(bf16[128,32,128]{2,0,1:T(8,128)(2,1)} %bitcast.26), calls=%async_computation.1 | async-start | bytes 2097152 | tf_op jit(solution)/shard_map/all_to_all | solution.py:83
  52.4 23.5 %all-to-all-done.1 = bf16[128,32,128]{2,0,1:T(8,128)(2,1)S(1)} async-done(((bf16[128,32,128]{2,0,1:T(8,128)(2,1)}), bf16[128,32,128]{2,0,1:T(8,128)(2,1)S(1)}, u32[]{:S(2)}, u32[]{:S(2)}) %all-to-all-start.1) | async-done | bytes 1048608 | tf_op jit(solution)/shard_map/all_to_all | solution.py:83
  75.9 9.2 %all-to-all-start = ((bf16[128,32,128]{0,2,1:T(8,128)(2,1)}), bf16[128,32,128]{0,2,1:T(8,128)(2,1)S(1)}, u32[]{:S(2)}, u32[]{:S(2)}) async-start(bf16[128,32,128]{0,2,1:T(8,128)(2,1)} %bitcast.207), calls=%async_computation | async-start | bytes 2097152 | tf_op jit(solution)/shard_map/all_to_all | solution.py:82
  87.3 22.8 %all-to-all-done = bf16[128,32,128]{0,2,1:T(8,128)(2,1)S(1)} async-done(((bf16[128,32,128]{0,2,1:T(8,128)(2,1)}), bf16[128,32,128]{0,2,1:T(8,128)(2,1)S(1)}, u32[]{:S(2)}, u32[]{:S(2)}) %all-to-all-start) | async-done | bytes 1048608 | tf_op jit(solution)/shard_map/all_to_all | solution.py:82
  110.1 9.0 %all-to-all-start.3 = ((bf16[128,32,128]{0,2,1:T(8,128)(2,1)}), bf16[128,32,128]{0,2,1:T(8,128)(2,1)}, u32[]{:S(2)}, u32[]{:S(2)}) async-start(bf16[128,32,128]{0,2,1:T(8,128)(2,1)} %bitcast.206), calls=%async_computation.3 | async-start | bytes 2097152 | tf_op jit(solution)/shard_map/all_to_all | solution.py:85
  119.8 3.8 collective-permute-start.1
  127.7 21.1 %all-to-all-done.3 = bf16[128,32,128]{0,2,1:T(8,128)(2,1)} async-done(((bf16[128,32,128]{0,2,1:T(8,128)(2,1)}), bf16[128,32,128]{0,2,1:T(8,128)(2,1)}, u32[]{:S(2)}, u32[]{:S(2)}) %all-to-all-start.3) | async-done | bytes 1048608 | tf_op jit(solution)/shard_map/all_to_all | solution.py:85
  159.1 187.7 %while.20 = (s32[]{:T(128)}, f32[5120,1,128]{2,0,1:T(8,128)}, f32[5120,1,128]{2,0,1:T(8,128)}, bf16[8,512,1,1,128]{4,1,0,3,2:T(8,128)(2,1)}, bf16[8,512,1,1,128]...) while((s32[]{:T(128)}, f32[5120,1,128]{2,0,1:T(8,128)}, ...), condition=%wide.region_4.5_spmd, body=%wide.region_0.4_spmd.sunk | while | flops 1221791232 | bytes 47100820 | solution.py:126
  172.2 2.8 fusion.68
  195.7 2.8 fusion.68
  219.1 2.8 fusion.68
  242.6 2.8 fusion.68
  289.5 2.8 fusion.68
  346.8 34.1 %all_to_all.134 = bf16[32,128,128]{2,1,0:T(8,128)(2,1)S(1)} all-to-all(bf16[32,128,128]{2,1,0:T(8,128)(2,1)} %bitcast.214), channel_id=1, replica_groups=mesh['uly'=32,'blk'=16] {'uly'}, dimensions={0} | all-to-all | bytes 2097152 | tf_op jit(solution)/shard_map/all_to_all | solution.py:132
  380.9 9.5 %all-to-all-start.5 = ((bf16[32,128,128]{2,1,0:T(8,128)(2,1)}), bf16[32,128,128]{2,1,0:T(8,128)(2,1)S(1)}, u32[]{:S(2)}, u32[]{:S(2)}) async-start(bf16[32,128,128]{2,1,0:T(8,128)(2,1)} %bitcast.213), calls=%async_computation.5 | async-start | bytes 2097152 | tf_op jit(solution)/shard_map/all_to_all | solution.py:139
  391.5 5.8 %collective-permute-start.2 = (bf16[1024,128]{1,0:T(8,128)(2,1)S(1)}, bf16[1024,128]{1,0:T(8,128)(2,1)S(1)}, u32[]{:S(2)}, u32[]{:S(2)}) collective-permute-start(bf16[1024,128]{1,0:T(8,128)(2,1)S(1)} %fusion.39), channel_id=1, source_target_pairs={{1,0},{2,1},{3,2},{4,3},{5,4},{6,5},{7,6},{8,7},{9,8},{10,9},{11,1... | collective-permute-start | bytes 786440 | tf_op jit(solution)/shard_map/ppermute | solution.py:14
  397.3 3.5 slice_bitcast_fusion
  400.8 21.5 %collective-permute-done.2 = bf16[1024,128]{1,0:T(8,128)(2,1)S(1)} collective-permute-done((bf16[1024,128]{1,0:T(8,128)(2,1)S(1)}, bf16[1024,128]{1,0:T(8,128)(2,1)S(1)}, u32[]{:S(2)}, u32[]{:S(2)}) %collective-permute-start.2) | collective-permute-done | bytes 262176 | tf_op jit(solution)/shard_map/ppermute | solution.py:14
  424.7 7.7 %all-to-all-start.6 = ((bf16[32,128,128]{1,2,0:T(8,128)(2,1)}), bf16[32,128,128]{1,2,0:T(8,128)(2,1)S(1)}, u32[]{:S(2)}, u32[]{:S(2)}) async-start(bf16[32,128,128]{1,2,0:T(8,128)(2,1)} %copy.82), calls=%async_computation.6 | async-start | bytes 2097152 | tf_op jit(solution)/shard_map/all_to_all | solution.py:158
  435.8 25.6 %collective-permute-done.3 = bf16[1024,128]{1,0:T(8,128)(2,1)S(1)} collective-permute-done((bf16[1024,128]{1,0:T(8,128)(2,1)S(1)}, bf16[1024,128]{1,0:T(8,128)(2,1)S(1)}, u32[]{:S(2)}, u32[]{:S(2)}) %collective-permute-start.3) | collective-permute-done | bytes 262176 | tf_op jit(solution)/shard_map/ppermute | solution.py:14
  465.4 9.7 %all-to-all-start.7 = ((bf16[32,128,128]{1,2,0:T(8,128)(2,1)}), bf16[32,128,128]{1,2,0:T(8,128)(2,1)}, u32[]{:S(2)}, u32[]{:S(2)}) async-start(bf16[32,128,128]{1,2,0:T(8,128)(2,1)} %copy.88), calls=%async_computation.7 | async-start | bytes 2097152 | tf_op jit(solution)/shard_map/all_to_all | solution.py:161
  481.6 22.2 %all-to-all-done.7 = bf16[32,128,128]{1,2,0:T(8,128)(2,1)} async-done(((bf16[32,128,128]{1,2,0:T(8,128)(2,1)}), bf16[32,128,128]{1,2,0:T(8,128)(2,1)}, u32[]{:S(2)}, u32[]{:S(2)}) %all-to-all-start.7) | async-done | bytes 1048608 | tf_op jit(solution)/shard_map/all_to_all | solution.py:161
  (264 shorter events, 208.5 us)
Async XLA Ops:
  0.6 15.3 %copy-start.4 = (bf16[128,256]{1,0:T(8,128)(2,1)S(1)}, bf16[128,256]{1,0:T(8,128)(2,1)}, u32[]{:S(2)}) copy-start(bf16[128,256]{1,0:T(8,128)(2,1)} %param.12) | copy-start | bytes 196612
  2.7 48.4 %copy-start.3 = (bf16[128,4096]{1,0:T(8,128)(2,1)S(1)}, bf16[128,4096]{1,0:T(8,128)(2,1)}, u32[]{:S(2)}) copy-start(bf16[128,4096]{1,0:T(8,128)(2,1)} %param.11) | copy-start | bytes 3145732
  2.7 37.8 %all-to-all-start.2 = ((bf16[128,32,128]{2,0,1:T(8,128)(2,1)}), bf16[128,32,128]{2,0,1:T(8,128)(2,1)S(1)}, u32[]{:S(2)}, u32[]{:S(2)}) async-start(bf16[128,32,128]{2,0,1:T(8,128)(2,1)} %bitcast.31), calls=%async_computation.2 | async-start | bytes 2097152 | tf_op jit(solution)/shard_map/all_to_all | solution.py:84
  41.7 34.2 %all-to-all-start.1 = ((bf16[128,32,128]{2,0,1:T(8,128)(2,1)}), bf16[128,32,128]{2,0,1:T(8,128)(2,1)S(1)}, u32[]{:S(2)}, u32[]{:S(2)}) async-start(bf16[128,32,128]{2,0,1:T(8,128)(2,1)} %bitcast.26), calls=%async_computation.1 | async-start | bytes 2097152 | tf_op jit(solution)/shard_map/all_to_all | solution.py:83
  75.9 34.2 %all-to-all-start = ((bf16[128,32,128]{0,2,1:T(8,128)(2,1)}), bf16[128,32,128]{0,2,1:T(8,128)(2,1)S(1)}, u32[]{:S(2)}, u32[]{:S(2)}) async-start(bf16[128,32,128]{0,2,1:T(8,128)(2,1)} %bitcast.207), calls=%async_computation | async-start | bytes 2097152 | tf_op jit(solution)/shard_map/all_to_all | solution.py:82
  110.1 38.7 %all-to-all-start.3 = ((bf16[128,32,128]{0,2,1:T(8,128)(2,1)}), bf16[128,32,128]{0,2,1:T(8,128)(2,1)}, u32[]{:S(2)}, u32[]{:S(2)}) async-start(bf16[128,32,128]{0,2,1:T(8,128)(2,1)} %bitcast.206), calls=%async_computation.3 | async-start | bytes 2097152 | tf_op jit(solution)/shard_map/all_to_all | solution.py:85
  119.8 31.2 %collective-permute-start.1 = (bf16[1024,128]{1,0:T(8,128)(2,1)}, bf16[1024,128]{1,0:T(8,128)(2,1)S(1)}, u32[]{:S(2)}, u32[]{:S(2)}) collective-permute-start(bf16[1024,128]{1,0:T(8,128)(2,1)} %bitcast.33), channel_id=1, source_target_pairs={{0,1},{1,2},{2,3},{3,4},{4,5},{5,6},{6,7},{7,8},{8,9},{9,10},{10,1... | collective-permute-start | bytes 786440 | tf_op jit(solution)/shard_map/ppermute | solution.py:14
  124.4 29.2 %collective-permute-start = (bf16[1024,128]{1,0:T(8,128)(2,1)}, bf16[1024,128]{1,0:T(8,128)(2,1)}, u32[]{:S(2)}, u32[]{:S(2)}) collective-permute-start(bf16[1024,128]{1,0:T(8,128)(2,1)} %bitcast.28), channel_id=1, source_target_pairs={{0,1},{1,2},{2,3},{3,4},{4,5},{5,6},{6,7},{7,8},{8,9},{9,10},{10,1... | collective-permute-start | bytes 786440 | tf_op jit(solution)/shard_map/ppermute | solution.py:14
  155.7 3.4 copy-start.5
  178.4 1.9 copy-start.1
  198.5 1.8 copy-start.2
  201.9 1.9 copy-start.1
  225.3 1.9 copy-start.1
  245.4 1.8 copy-start.2
  248.8 1.9 copy-start.1
  272.2 1.9 copy-start.1
  295.7 1.9 copy-start.1
  319.2 1.9 copy-start.1
  342.7 1.9 copy-start.1
  380.9 43.8 %all-to-all-start.5 = ((bf16[32,128,128]{2,1,0:T(8,128)(2,1)}), bf16[32,128,128]{2,1,0:T(8,128)(2,1)S(1)}, u32[]{:S(2)}, u32[]{:S(2)}) async-start(bf16[32,128,128]{2,1,0:T(8,128)(2,1)} %bitcast.213), calls=%async_computation.5 | async-start | bytes 2097152 | tf_op jit(solution)/shard_map/all_to_all | solution.py:139
  391.5 30.8 %collective-permute-start.2 = (bf16[1024,128]{1,0:T(8,128)(2,1)S(1)}, bf16[1024,128]{1,0:T(8,128)(2,1)S(1)}, u32[]{:S(2)}, u32[]{:S(2)}) collective-permute-start(bf16[1024,128]{1,0:T(8,128)(2,1)S(1)} %fusion.39), channel_id=1, source_target_pairs={{1,0},{2,1},{3,2},{4,3},{5,4},{6,5},{7,6},{8,7},{9,8},{10,9},{11,1... | collective-permute-start | bytes 786440 | tf_op jit(solution)/shard_map/ppermute | solution.py:14
  424.7 40.7 %all-to-all-start.6 = ((bf16[32,128,128]{1,2,0:T(8,128)(2,1)}), bf16[32,128,128]{1,2,0:T(8,128)(2,1)S(1)}, u32[]{:S(2)}, u32[]{:S(2)}) async-start(bf16[32,128,128]{1,2,0:T(8,128)(2,1)} %copy.82), calls=%async_computation.6 | async-start | bytes 2097152 | tf_op jit(solution)/shard_map/all_to_all | solution.py:158
  433.5 27.8 %collective-permute-start.3 = (bf16[1024,128]{1,0:T(8,128)(2,1)S(1)}, bf16[1024,128]{1,0:T(8,128)(2,1)S(1)}, u32[]{:S(2)}, u32[]{:S(2)}) collective-permute-start(bf16[1024,128]{1,0:T(8,128)(2,1)S(1)} %fusion.40), channel_id=1, source_target_pairs={{1,0},{2,1},{3,2},{4,3},{5,4},{6,5},{7,6},{8,7},{9,8},{10,9},{11,1... | collective-permute-start | bytes 786440 | tf_op jit(solution)/shard_map/ppermute | solution.py:14
  465.4 38.4 %all-to-all-start.7 = ((bf16[32,128,128]{1,2,0:T(8,128)(2,1)}), bf16[32,128,128]{1,2,0:T(8,128)(2,1)}, u32[]{:S(2)}, u32[]{:S(2)}) async-start(bf16[32,128,128]{1,2,0:T(8,128)(2,1)} %copy.88), calls=%async_computation.7 | async-start | bytes 2097152 | tf_op jit(solution)/shard_map/all_to_all | solution.py:161
  (7 other events, 11.6 us)
where the time goes:
time: 510 us; the launch traced here: 506 us
  waiting for transfers between devices  162 us (32%)
  local copies, waits for them, and re-layouts  105 us (21%)
  matrix products  95.7 us (19%)
  starting transfers between devices  81.6 us (16%)
  blocking collectives  34.1 us (7%)
  other arithmetic  20.2 us (4%)
  loops' own time  6.49 us (1%)
    ppermute x4, waiting for transfers between devices, from_behind(): return lax.ppermute(block, axis, route)  48.4 us
    all_to_all x1, blocking collectives, shards(): lax.all_to_all(attended_all.reshape(region, per_dev * head_dim), 'uly', s...  34.1 us
    all_to_all x1, waiting for transfers between devices, shards(): lax.all_to_all(to_slots(packed_values), 'uly', split_axis=1, concat_axis=...  24.5 us
    all_to_all x1, waiting for transfers between devices, shards(): lax.all_to_all(to_slots(packed_keys), 'uly', split_axis=1, concat_axis=0,...  23.5 us
    all_to_all x1, waiting for transfers between devices, shards(): lax.all_to_all(packed_queries, 'uly', split_axis=1, concat_axis=0, tiled=...  22.8 us
    dot_general x8, matrix products, attend_block(): jnp.einsum('cgtw,tcgd->wcd', weights_low, cot_blk, preferred_element_type...  22.4 us
    all_to_all x1, waiting for transfers between devices, shards(): lax.all_to_all(own_v.astype(jnp.bfloat16), 'uly', split_axis=0, concat_ax...  22.2 us
    all_to_all x1, waiting for transfers between devices, shards(): lax.all_to_all(output_cotangent, 'uly', split_axis=1, concat_axis=0, tile...  21.1 us
  transfers between devices with their start and end apart: 11, of which 8 were waited for; matrix products, arithmetic and copies ran while one was open for 6% of the time, Pallas kernels for 0%

commit v1 on v0

v1 whole, which is shorter than its diff:
```python
import functools
import math

import jax
import jax.numpy as jnp
from jax import lax
from jax.experimental import pallas as pl
from jax.experimental.pallas import tpu as pltpu
from jax.sharding import PartitionSpec as P

HEAD = 128
TOK = 128
RING = 8
KEYS = RING * TOK
SCALE = 1.0 / math.sqrt(HEAD)
SCALE2 = SCALE * math.log2(math.e)
F32 = jnp.float32
BF16 = jnp.bfloat16
HEADS_PER_STEP = 4


def dot(a, b, ca, cb):
    return lax.dot_general(a, b, (((ca,), (cb,)), ((), ())), preferred_element_type=F32)


def attention_kernel(
    where_ref, q_ref, do_ref, k_ref, v_ref, o_ref, dq_ref, dk_ref, dv_ref, bias, dk_acc, dv_acc, *, steps
):
    step = pl.program_id(0)
    part = lax.rem(step, steps)

    @pl.when(step == 0)
    def _():
        position, before = where_ref[0], where_ref[1]
        row = lax.broadcasted_iota(jnp.int32, (TOK, TOK), 0)
        col = lax.broadcasted_iota(jnp.int32, (TOK, TOK), 1)
        for slot in range(RING):
            behind = lax.rem(position - slot + RING, RING)
            seen = ((behind == 0) & (col <= row)) | ((behind > 0) & (behind <= before))
            bias[:, slot * TOK : (slot + 1) * TOK] = jnp.where(seen, 0.0, -1e30).astype(F32)

    k, v = k_ref[...], v_ref[...]
    heads = HEADS_PER_STEP
    q = jnp.concatenate([q_ref[:, r * HEAD : (r + 1) * HEAD] for r in range(heads)], 0)
    do = jnp.concatenate([do_ref[:, r * HEAD : (r + 1) * HEAD] for r in range(heads)], 0)
    s = dot(q, k, 1, 1) + jnp.concatenate([bias[...]] * heads, 0)
    top = jnp.max(s, axis=1, keepdims=True)
    p = jnp.exp2(s * SCALE2 - top * SCALE2)
    inv = 1.0 / jnp.sum(p, axis=1, keepdims=True)
    p_low = p.astype(BF16)
    o = (dot(p_low, v, 1, 0) * inv).astype(BF16)
    do_wide = do.astype(F32)
    delta = jnp.sum(do_wide * o.astype(F32), axis=1, keepdims=True) * inv
    do_norm = (do_wide * inv).astype(BF16)
    ds = (p * (dot(do_norm, v, 1, 1) - delta)).astype(BF16)
    dq = (dot(ds, k, 1, 0) * SCALE).astype(BF16)
    for r in range(heads):
        o_ref[:, r * HEAD : (r + 1) * HEAD] = o[r * TOK : (r + 1) * TOK]
        dq_ref[:, r * HEAD : (r + 1) * HEAD] = dq[r * TOK : (r + 1) * TOK]
    dk = dot(q.T, ds, 1, 0)
    dv = dot(do_norm.T, p_low, 1, 0)

    @pl.when(part == 0)
    def _():
        dk_acc[...] = dk
        dv_acc[...] = dv

    @pl.when(part != 0)
    def _():
        dk_acc[...] += dk
        dv_acc[...] += dv

    @pl.when(part == steps - 1)
    def _():
        dk_ref[...] = (dk_acc[...] * SCALE).T.astype(BF16)
        dv_ref[...] = dv_acc[...].T.astype(BF16)


def attention(where, q, do, k, v):
    kv_heads = k.shape[1] // HEAD
    width = HEADS_PER_STEP * HEAD
    total = q.shape[1] // width
    steps = total // kv_heads
    rows = pl.BlockSpec((TOK, width), lambda i, w: (0, i))
    keys = pl.BlockSpec((KEYS, HEAD), lambda i, w: (0, i // steps))
    return pl.pallas_call(
        functools.partial(attention_kernel, steps=steps),
        grid_spec=pltpu.PrefetchScalarGridSpec(
            num_scalar_prefetch=1,
            grid=(total,),
            in_specs=[rows, rows, keys, keys],
            out_specs=[rows, rows, keys, keys],
            scratch_shapes=[
                pltpu.VMEM((TOK, KEYS), F32),
                pltpu.VMEM((HEAD, KEYS), F32),
                pltpu.VMEM((HEAD, KEYS), F32),
            ],
        ),
        out_shape=[jax.ShapeDtypeStruct(q.shape, BF16)] * 2 + [jax.ShapeDtypeStruct(k.shape, BF16)] * 2,
        compiler_params=pltpu.CompilerParams(
            vmem_limit_bytes=48 << 20, dimension_semantics=("arbitrary",)
        ),
        cost_estimate=pl.CostEstimate(
            flops=12 * TOK * KEYS * q.shape[1],
            bytes_accessed=8 * q.size + 8 * k.size,
            transcendentals=TOK * KEYS * q.shape[1] // HEAD,
        ),
    )(where, q, do, k, v)


def ring_shift(block, rings):
    lanes, regions = lax.axis_size("uly"), lax.axis_size("blk")
    tokens = lanes * regions

    def device(place):
        return (place % lanes) * regions + place // lanes

    route = [
        (device(i), device(i + rings * RING)) for i in range(tokens) if 0 <= i + rings * RING < tokens
    ]
    return lax.ppermute(block, ("uly", "blk"), route)


def within_ring(blocks):
    lanes = lax.axis_size("uly")
    groups = [list(range(r, r + RING)) for r in range(0, lanes, RING)]
    return lax.all_to_all(blocks, "uly", 0, 0, axis_index_groups=groups, tiled=True)


def shards(queries, keys, values, cotangent, doc_offsets):
    lane = lax.axis_index("uly")
    position = lane % RING
    first = (lax.axis_index("blk") * lax.axis_size("uly") + lane) * TOK
    start = jnp.max(jnp.where(doc_offsets <= first, doc_offsets, 0))
    where = jnp.stack([position, (first - start) // TOK]).astype(jnp.int32)
    slot = jnp.arange(RING)[:, None, None]

    own = jnp.concatenate([keys, values], 1)
    behind = ring_shift(own, 1)
    seen = within_ring(jnp.where(slot >= position, own[None], behind[None]))
    width = keys.shape[1]
    seen = seen.reshape(KEYS, 2 * width)
    attended, grad_q, grad_k, grad_v = attention(
        where, queries, cotangent, seen[:, :width], seen[:, width:]
    )
    terms = within_ring(jnp.concatenate([grad_k, grad_v], 1).reshape(RING, TOK, 2 * width)).astype(F32)
    mine = jnp.sum(jnp.where(slot >= position, terms, 0.0), 0)
    theirs = jnp.sum(jnp.where(slot >= position, 0.0, terms), 0).astype(BF16)
    total = (mine + ring_shift(theirs, -1).astype(F32)).astype(BF16)
    return attended, grad_q, total[:, :width], total[:, width:]


def solution(mesh):
    split = P(("blk", "uly"), None)
    return jax.shard_map(
        shards,
        mesh=mesh,
        in_specs=(split, split, split, split, P()),
        out_specs=(split, split, split, split),
        check_vma=False,
    )
```

time: 510 us -> 92.5 us (0.18)
  waiting for transfers between devices: 162 us -> 29.2 us
  local copies, waits for them, and re-layouts: 105 us -> 3.89 us
  matrix products: 95.7 us -> 0 us
  starting transfers between devices: 81.6 us -> 16 us
  Pallas kernels: 0 us -> 20.4 us
  other arithmetic: 20.2 us -> 2.38 us
  blocking collectives: 34.1 us -> 18.5 us
  loops' own time: 6.49 us -> 0 us
    all_to_all x7 -> x1, waiting for transfers between devices: 114 us -> 14.6 us  [within_ring(): lax.all_to_all(blocks, 'uly', 0, 0, axis_index_groups=groups, tiled=True)]
    dot_general x48 -> x0, matrix products: 95.7 us -> none  [the longest x8 22.4 us: attend_block(): jnp.einsum('cgtw,tcgd->wcd', weights_low, cot_blk, preferred_element_type...]
    all_to_all x7 -> x1, starting transfers between devices: 67.8 us -> 4.43 us  [within_ring(): lax.all_to_all(blocks, 'uly', 0, 0, axis_index_groups=groups, tiled=True)]
    dynamic_slice x40 -> x0, local copies, waits for them, and re-layouts: 42.8 us -> none  [the longest x16 18.9 us: one_block(): lax.dynamic_slice_in_dim(key_gradient_part, row_start, window_rows, 0)]
    ppermute x4 -> x2, waiting for transfers between devices: 48.4 us -> 14.6 us  [ring_shift(): return lax.ppermute(block, ('uly', 'blk'), route)]
    dynamic_update_slice x48 -> x0, local copies, waits for them, and re-layouts: 29.1 us -> none  [the longest x24 14.9 us: shards(): lax.scan(one_block, (empty_gradients, empty_gradients), jnp.arange(region...]
    pallas_call x0 -> x1, Pallas kernels: none -> 20.4 us  [attention(): pl.pallas_call(functools.partial(attention_kernel, steps=steps), grid_spe...]
    all_to_all x1, blocking collectives: 34.1 us -> 18.5 us  [within_ring(): lax.all_to_all(blocks, 'uly', 0, 0, axis_index_groups=groups, tiled=True)]
  transfers between devices with their start and end apart: 11 -> 3, of which waited for: 8 -> 3; matrix products, arithmetic and copies ran while one was open for 6% -> 1% of each run, Pallas kernels for 0% -> 0%
where the time goes in v1:
time: 92.5 us; the launch traced here: 91.7 us
  waiting for transfers between devices  29.2 us (32%)
  Pallas kernels  20.4 us (22%)
  blocking collectives  18.5 us (20%)
  starting transfers between devices  16 us (17%)
  local copies, waits for them, and re-layouts  3.89 us (4%)
  other arithmetic  2.38 us (3%)
  between operations  1.37 us (1%)
    pallas_call x1, Pallas kernels, attention(): pl.pallas_call(functools.partial(attention_kernel, steps=steps), grid_spe...  20.4 us
    all_to_all x1, blocking collectives, within_ring(): lax.all_to_all(blocks, 'uly', 0, 0, axis_index_groups=groups, tiled=True)  18.5 us
    ppermute x2, waiting for transfers between devices, ring_shift(): return lax.ppermute(block, ('uly', 'blk'), route)  14.6 us
    all_to_all x1, waiting for transfers between devices, within_ring(): lax.all_to_all(blocks, 'uly', 0, 0, axis_index_groups=groups, tiled=True)  14.6 us
    ppermute x2, starting transfers between devices, ring_shift(): return lax.ppermute(block, ('uly', 'blk'), route)  11.5 us
    all_to_all x1, starting transfers between devices, within_ring(): lax.all_to_all(blocks, 'uly', 0, 0, axis_index_groups=groups, tiled=True)  4.43 us
    unnamed x7, local copies, waits for them, and re-layouts  2.32 us
  transfers between devices with their start and end apart: 3, of which 3 were waited for; matrix products, arithmetic and copies ran while one was open for 1% of the time, Pallas kernels for 0%

profile of v1, /device:TPU:56, one launch (start us, length us, event | category | flops | bytes accessed | tf_op | source)
XLA Modules:
  0.0 91.7 jit_solution(3025506663638933583)
XLA Ops:
  0.6 0.8 constant_dynamic-update-slice_fusion.1
  1.5 0.8 constant_dynamic-update-slice_fusion
  2.3 6.1 %collective-permute-start = (bf16[128,512]{1,0:T(8,128)(2,1)S(1)}, bf16[128,512]{1,0:T(8,128)(2,1)S(1)}, u32[]{:S(2)}, u32[]{:S(2)}) collective-permute-start(bf16[128,512]{1,0:T(8,128)(2,1)S(1)} %constant_dynamic-update-slice_fusion), channel_id=1, source_target_pairs={{0,128},{16,144},{32,160},{48,176},{64,192},{80,208},{96,224},{112... | collective-permute-start | bytes 393224 | tf_op jit(solution)/shard_map/ppermute | solution.py:121
  8.4 11.0 %collective-permute-done = bf16[128,512]{1,0:T(8,128)(2,1)S(1)} collective-permute-done((bf16[128,512]{1,0:T(8,128)(2,1)S(1)}, bf16[128,512]{1,0:T(8,128)(2,1)S(1)}, u32[]{:S(2)}, u32[]{:S(2)}) %collective-permute-start) | collective-permute-done | bytes 131104 | tf_op jit(solution)/shard_map/ppermute | solution.py:121
  19.5 1.1 %broadcast_select_fusion = bf16[8,128,512]{2,1,0:T(8,128)(2,1)} fusion(pred[8]{0:T(512)(128)(4,1)S(1)} %iota_compare_fusion, bf16[128,512]{1,0:T(8,128)(2,1)S(1)} %collective-permute-done, bf16[128,512]{1,0:T(8,128)(2,1)S(1)} %constant_dynamic-update-slice_fusion), kind=kLoop, calls=%fused_computation.5 | loop fusion | flops 524288 | bytes 1310728 | tf_op jit(solution)/shard_map/jit(_where)/select_n | solution.py:140
  20.6 0.0 copy-start.2
  20.6 4.4 %all-to-all-start = ((bf16[8,128,512]{2,1,0:T(8,128)(2,1)}), bf16[8,128,512]{2,1,0:T(8,128)(2,1)S(1)}, u32[]{:S(2)}, u32[]{:S(2)}) async-start(bf16[8,128,512]{2,1,0:T(8,128)(2,1)} %broadcast_select_fusion), calls=%async_computation | async-start | bytes 2097152 | tf_op jit(solution)/shard_map/all_to_all | solution.py:127
  25.0 0.0 copy-done.2
  25.0 0.6 fusion.2
  26.3 0.1 pad_add_fusion.where_ref
  26.4 14.6 %all-to-all-done = bf16[8,128,512]{2,1,0:T(8,128)(2,1)S(1)} async-done(((bf16[8,128,512]{2,1,0:T(8,128)(2,1)}), bf16[8,128,512]{2,1,0:T(8,128)(2,1)S(1)}, u32[]{:S(2)}, u32[]{:S(2)}) %all-to-all-start) | async-done | bytes 1048608 | tf_op jit(solution)/shard_map/all_to_all | solution.py:127
  41.0 0.0 copy-start
  41.0 0.0 copy-start.1
  41.0 0.1 fusion.3
  41.1 1.1 %copy-done = bf16[128,4096]{1,0:T(8,128)(2,1)S(1)} copy-done((bf16[128,4096]{1,0:T(8,128)(2,1)S(1)}, bf16[128,4096]{1,0:T(8,128)(2,1)}, u32[]{:S(2)}) %copy-start) | copy-done | bytes 1048600
  42.2 0.3 copy-done.1
  42.5 20.4 %shard_map.84 = (bf16[128,4096]{1,0:T(8,128)(2,1)}, bf16[128,4096]{1,0:T(8,128)(2,1)}, bf16[1024,256]{1,0:T(8,128)(2,1)S(1)}, bf16[1024,256]{1,0:T(8,128)(2,1)S(1)}) custom-call(s32[2]{0:T(128)S(1)} %pad_add_fusion.where_ref, bf16[128,4096]{1,0:T(8,128)(2,1)S(1)} %copy-done, bf16[128,4096]{1,0:T(8,128)(2,1)S(1)} %copy-done.1, ...), custom_call_target="tpu_custom_call" | custom-call | flops 6442450944 | bytes 6291456 | tf_op jit(solution)/shard_map/pallas_call | solution.py:86
  62.9 0.1 pad_maximum_fusion
  63.0 18.5 %all_to_all.10 = bf16[8,128,512]{2,1,0:T(8,128)(2,1)S(1)} all-to-all(bf16[8,128,512]{2,1,0:T(8,128)(2,1)S(1)} %bitcast.5), channel_id=1, replica_groups={{0,16,32,48,64,80,96,112},{128,144,160,176,192,208,224,240},{256,272,28..., dimensions={0} | all-to-all | bytes 2097152 | tf_op jit(solution)/shard_map/all_to_all | solution.py:127
  81.5 0.4 fusion.1
  82.0 5.4 %collective-permute-start.1 = (bf16[128,512]{1,0:T(8,128)(2,1)S(1)}, bf16[128,512]{1,0:T(8,128)(2,1)S(1)}, u32[]{:S(2)}, u32[]{:S(2)}) collective-permute-start(bf16[128,512]{1,0:T(8,128)(2,1)S(1)} %get-tuple-element.12), channel_id=1, source_target_pairs={{128,0},{144,16},{160,32},{176,48},{192,64},{208,80},{224,96},{240... | collective-permute-start | bytes 393224 | tf_op jit(solution)/shard_map/ppermute | solution.py:121
  87.4 3.6 %collective-permute-done.1 = bf16[128,512]{1,0:T(8,128)(2,1)S(1)} collective-permute-done((bf16[128,512]{1,0:T(8,128)(2,1)S(1)}, bf16[128,512]{1,0:T(8,128)(2,1)S(1)}, u32[]{:S(2)}, u32[]{:S(2)}) %collective-permute-start.1) | collective-permute-done | bytes 131104 | tf_op jit(solution)/shard_map/ppermute | solution.py:121
  91.0 0.7 fusion.4
  (2 shorter events, 0.0 us)
Async XLA Ops:
  2.3 17.2 %collective-permute-start = (bf16[128,512]{1,0:T(8,128)(2,1)S(1)}, bf16[128,512]{1,0:T(8,128)(2,1)S(1)}, u32[]{:S(2)}, u32[]{:S(2)}) collective-permute-start(bf16[128,512]{1,0:T(8,128)(2,1)S(1)} %constant_dynamic-update-slice_fusion), channel_id=1, source_target_pairs={{0,128},{16,144},{32,160},{48,176},{64,192},{80,208},{96,224},{112... | collective-permute-start | bytes 393224 | tf_op jit(solution)/shard_map/ppermute | solution.py:121
  20.6 4.4 %copy-start.2 = (s32[130]{0:T(256)S(1)}, s32[130]{0:T(256)}, u32[]{:S(2)}) copy-start(s32[130]{0:T(256)} %param.9) | copy-start | bytes 1564
  20.6 20.4 %all-to-all-start = ((bf16[8,128,512]{2,1,0:T(8,128)(2,1)}), bf16[8,128,512]{2,1,0:T(8,128)(2,1)S(1)}, u32[]{:S(2)}, u32[]{:S(2)}) async-start(bf16[8,128,512]{2,1,0:T(8,128)(2,1)} %broadcast_select_fusion), calls=%async_computation | async-start | bytes 2097152 | tf_op jit(solution)/shard_map/all_to_all | solution.py:127
  41.0 1.2 %copy-start = (bf16[128,4096]{1,0:T(8,128)(2,1)S(1)}, bf16[128,4096]{1,0:T(8,128)(2,1)}, u32[]{:S(2)}) copy-start(bf16[128,4096]{1,0:T(8,128)(2,1)} %q_ref.1) | copy-start | bytes 3145732
  41.0 1.5 %copy-start.1 = (bf16[128,4096]{1,0:T(8,128)(2,1)S(1)}, bf16[128,4096]{1,0:T(8,128)(2,1)}, u32[]{:S(2)}) copy-start(bf16[128,4096]{1,0:T(8,128)(2,1)} %do_ref.1) | copy-start | bytes 3145732
  82.0 9.0 %collective-permute-start.1 = (bf16[128,512]{1,0:T(8,128)(2,1)S(1)}, bf16[128,512]{1,0:T(8,128)(2,1)S(1)}, u32[]{:S(2)}, u32[]{:S(2)}) collective-permute-start(bf16[128,512]{1,0:T(8,128)(2,1)S(1)} %get-tuple-element.12), channel_id=1, source_target_pairs={{128,0},{144,16},{160,32},{176,48},{192,64},{208,80},{224,96},{240... | collective-permute-start | bytes 393224 | tf_op jit(solution)/shard_map/ppermute | solution.py:121

commit v2 on v1

v2 whole, which is shorter than its diff:
```python
import math

import jax
import jax.numpy as jnp
from jax import lax
from jax.experimental import pallas as pl
from jax.experimental.pallas import tpu as pltpu
from jax.sharding import PartitionSpec as P

HEAD = 128
TOK = 128
RING = 8
KEYS = RING * TOK
SPAN = KEYS + TOK
SCALE = 1.0 / math.sqrt(HEAD)
SCALE2 = SCALE * math.log2(math.e)
F32 = jnp.float32
BF16 = jnp.bfloat16


def dot(a, b, ca, cb):
    return lax.dot_general(a, b, (((ca,), (cb,)), ((), ())), preferred_element_type=F32)


def stacked(ref):
    return jnp.concatenate([ref[:, r * HEAD : (r + 1) * HEAD] for r in range(ref.shape[1] // HEAD)], 0)


def attention_kernel(
    where_ref,
    offsets_ref,
    q_here_ref,
    do_here_ref,
    q_there_ref,
    do_there_ref,
    seen_ref,
    own_here_ref,
    own_there_ref,
    o_here_ref,
    dq_here_ref,
    there_ref,
    terms_ref,
    mine_here_ref,
    q_now,
    do_now,
    own_now,
    first_own,
    k_fill,
    k_zero,
    v_zero,
    o_now,
    dq_now,
    dk_acc,
    dv_acc,
):
    core, chip = where_ref[0], where_ref[1]
    side = pl.program_id(0)
    index = lax.rem(core + side, 2)
    half = q_now.shape[1]
    first_token = where_ref[2] + index * TOK
    offsets = offsets_ref[...]
    start = jnp.max(jnp.where(offsets <= first_token, offsets, 0))
    before = lax.shift_right_logical(first_token - start, 7)

    def slot(m):
        return lax.rem(2 * chip + 1 + m, RING)

    @pl.when(side == 0)
    def _():
        mine = pl.ds(pl.multiple_of(core * half, half), half)
        q_now[...] = q_here_ref[:, mine]
        do_now[...] = do_here_ref[:, mine]
        own_now[...] = own_here_ref[...]
        dk_acc[...] = jnp.zeros_like(dk_acc)
        dv_acc[...] = jnp.zeros_like(dv_acc)

    @pl.when(side == 1)
    def _():
        q_now[...] = q_there_ref[...]
        do_now[...] = do_there_ref[...]
        own_now[...] = own_there_ref[...]

    @pl.when(core == 0)
    def _():
        first_own[...] = own_here_ref[...]

    @pl.when(core == 1)
    def _():
        first_own[...] = own_there_ref[...]

    first = jnp.broadcast_to(own_now[0:1, :HEAD], (TOK, HEAD))
    zero = jnp.zeros((TOK, HEAD), BF16)
    for w in range(RING - 1):
        at = slice(w * TOK, (w + 1) * TOK)
        block = seen_ref[slot(w + index)]
        if w == RING - 2:
            block = jnp.where(index == 1, first_own[...], block)
        shown = RING - 1 - w <= before
        k_fill[at] = jnp.where(shown, block[:, :HEAD], first)
        k_zero[at] = jnp.where(shown, block[:, :HEAD], zero)
        v_zero[at] = jnp.where(shown, block[:, HEAD:], zero)
    last = slice(KEYS - TOK, KEYS)
    k_fill[last] = own_now[:, :HEAD]
    k_zero[last] = own_now[:, :HEAD]
    v_zero[last] = own_now[:, HEAD:]
    hidden = RING - 1 - before

    heads = half // HEAD
    q, do = stacked(q_now), stacked(do_now)
    k, v = k_fill[...], v_zero[...]
    row = lax.broadcasted_iota(jnp.int32, (TOK, TOK), 0)
    col = lax.broadcasted_iota(jnp.int32, (TOK, TOK), 1)
    causal = jnp.where(col <= row, 0.0, -1e30).astype(F32)
    s = dot(q, k, 1, 1)
    s = jnp.concatenate([s[:, : KEYS - TOK], s[:, KEYS - TOK :] + jnp.concatenate([causal] * heads, 0)], 1)
    top = jnp.max(s, axis=1, keepdims=True)
    p = jnp.exp2(s * SCALE2 - top * SCALE2)
    p_low = p.astype(BF16)
    wide = p[:, :TOK]
    for w in range(1, RING):
        wide = wide + p[:, w * TOK : (w + 1) * TOK]
    total = jnp.sum(wide - hidden.astype(F32) * p[:, :TOK], axis=1, keepdims=True)
    inv = 1.0 / total
    o = (dot(p_low, v, 1, 0) * inv).astype(BF16)
    do_wide = do.astype(F32)
    delta = jnp.sum(do_wide * o.astype(F32), axis=1, keepdims=True) * inv
    do_norm = (do_wide * inv).astype(BF16)
    ds = p_low * (dot(do_norm, v, 1, 1) - delta).astype(BF16)
    dq = (dot(ds, k_zero[...], 1, 0) * SCALE).astype(BF16)
    for r in range(heads):
        o_now[:, r * HEAD : (r + 1) * HEAD] = o[r * TOK : (r + 1) * TOK]
        dq_now[:, r * HEAD : (r + 1) * HEAD] = dq[r * TOK : (r + 1) * TOK]
    place = lax.broadcasted_iota(jnp.int32, (HEAD, KEYS), 1)
    shown = place >= hidden * TOK
    window = pl.ds(pl.multiple_of(index * TOK, TOK), KEYS)
    dk_acc[:, window] += jnp.where(shown, dot(q.T, ds, 1, 0), 0.0)
    dv_acc[:, window] += jnp.where(shown, dot(do_norm.T, p_low, 1, 0), 0.0)

    @pl.when(side == 0)
    def _():
        o_here_ref[...] = o_now[...]
        dq_here_ref[...] = dq_now[...]

    @pl.when(side == 1)
    def _():
        there_ref[:, :half] = o_now[...]
        there_ref[:, half : 2 * half] = dq_now[...]

        def block(m):
            cols = slice(m * TOK, (m + 1) * TOK)
            return (dk_acc[:, cols] * SCALE).T.astype(BF16), dv_acc[:, cols].T.astype(BF16)

        for m in range(RING - 1):
            terms_ref[slot(m), :, :HEAD], terms_ref[slot(m), :, HEAD:] = block(m)
        terms_ref[2 * chip] = jnp.zeros((TOK, 2 * HEAD), BF16)
        even_k, even_v = block(RING - 1)
        odd_k, odd_v = block(RING)
        swap = core == 1
        mine_here_ref[:, :HEAD] = jnp.where(swap, odd_k, even_k)
        mine_here_ref[:, HEAD:] = jnp.where(swap, odd_v, even_v)
        there_ref[:, 2 * half : 2 * half + HEAD] = jnp.where(swap, even_k, odd_k)
        there_ref[:, 2 * half + HEAD :] = jnp.where(swap, even_v, odd_v)


def attention(where, offsets, queries, cotangent, q_there, do_there, seen, own_here, own_there):
    half = q_there.shape
    rows = half[1] // HEAD * TOK
    own = own_here.shape
    there = (TOK, 2 * half[1] + own[1])
    vmem = pl.BlockSpec(memory_space=pltpu.VMEM)
    return pl.pallas_call(
        attention_kernel,
        grid_spec=pltpu.PrefetchScalarGridSpec(
            num_scalar_prefetch=1,
            grid=(2,),
            in_specs=[vmem] * 8,
            out_specs=[vmem] * 5,
            scratch_shapes=[
                pltpu.VMEM(half, BF16),
                pltpu.VMEM(half, BF16),
                pltpu.VMEM(own, BF16),
                pltpu.VMEM(own, BF16),
                pltpu.VMEM((KEYS, HEAD), BF16),
                pltpu.VMEM((KEYS, HEAD), BF16),
                pltpu.VMEM((KEYS, HEAD), BF16),
                pltpu.VMEM(half, BF16),
                pltpu.VMEM(half, BF16),
                pltpu.VMEM((HEAD, SPAN), F32),
                pltpu.VMEM((HEAD, SPAN), F32),
            ],
        ),
        out_shape=[
            jax.ShapeDtypeStruct(half, BF16),
            jax.ShapeDtypeStruct(half, BF16),
            jax.ShapeDtypeStruct(there, BF16),
            jax.ShapeDtypeStruct(seen.shape, BF16),
            jax.ShapeDtypeStruct(own, BF16),
        ],
        compiler_params=pltpu.CompilerParams(
            vmem_limit_bytes=44 << 20, dimension_semantics=("arbitrary",)
        ),
        cost_estimate=pl.CostEstimate(
            flops=24 * rows * KEYS * HEAD,
            bytes_accessed=16 * rows * HEAD,
            transcendentals=2 * rows * KEYS,
        ),
    )(where, offsets, queries, cotangent, q_there, do_there, seen, own_here, own_there)


def ring_shift(block, rings):
    lanes, regions = lax.axis_size("uly"), lax.axis_size("blk")
    tokens = lanes * regions

    def device(place):
        return (place % lanes) * regions + place // lanes

    route = [
        (device(i), device(i + rings * RING)) for i in range(tokens) if 0 <= i + rings * RING < tokens
    ]
    return lax.ppermute(block, ("uly", "blk"), route)


def within_ring(blocks):
    lanes = lax.axis_size("uly")
    groups = [list(range(r, r + RING)) for r in range(0, lanes, RING)]
    return lax.all_to_all(blocks, "uly", 0, 0, axis_index_groups=groups, tiled=True)


def to_sibling(block):
    lanes = lax.axis_size("uly")
    return lax.ppermute(block, "uly", [(i, i ^ 1) for i in range(lanes)])


def to_sibling(block):
    lanes = lax.axis_size("uly")
    return lax.ppermute(block, "uly", [(i, i ^ 1) for i in range(lanes)])


def shards(queries, keys, values, cotangent, doc_offsets):
    lane = lax.axis_index("uly")
    core, chip = lane & 1, (lane >> 1) & (RING // 2 - 1)
    first = (lax.axis_index("blk") * lax.axis_size("uly") + lane - core) * TOK
    where = jnp.stack([core, chip, first]).astype(jnp.int32)
    slot_chip = (jnp.arange(RING) // 2)[:, None, None]

    def heads_of(block, group):
        width = block.shape[1] // 2
        return lax.dynamic_slice_in_dim(block, group * width, width, 1)

    def by_slot(block):
        return jnp.broadcast_to(
            block.reshape(1, TOK, 2, 2 * HEAD).transpose(0, 2, 1, 3), (RING // 2, 2, TOK, 2 * HEAD)
        ).reshape(RING, TOK, 2 * HEAD)

    kv = jnp.concatenate([keys[:, :HEAD], values[:, :HEAD], keys[:, HEAD:], values[:, HEAD:]], 1)
    behind = ring_shift(kv, 1)
    send = jnp.where(slot_chip > chip, by_slot(kv), by_slot(behind))
    halves = [heads_of(a, 1 - core) for a in (queries, cotangent, kv)]
    where, *halves = lax.optimization_barrier((where, *halves))
    seen = within_ring(send)
    q_there, do_there, own_there = [to_sibling(a) for a in halves]
    offsets = doc_offsets.reshape(1, -1)
    o_here, dq_here, there, terms, mine_here = attention(
        where, offsets, queries, cotangent, q_there, do_there, seen, heads_of(kv, core), own_there
    )

    terms = within_ring(terms).reshape(RING // 2, 2, TOK, 2 * HEAD)

    def picked(after):
        return sum(
            jnp.where((j > chip) == after, terms[j], jnp.zeros_like(terms[j])).astype(F32)
            for j in range(RING // 2)
        )

    shifted = ring_shift(picked(False).astype(BF16), -1)
    back = to_sibling(there)
    half = o_here.shape[1]

    def joined(a, b):
        return jnp.where(core == 0, jnp.concatenate([a, b], 1), jnp.concatenate([b, a], 1))

    attended, grad_q = joined(o_here, back[:, :half]), joined(dq_here, back[:, half : 2 * half])
    local = jnp.where(
        core == 0,
        jnp.stack([mine_here, back[:, 2 * half :]]),
        jnp.stack([back[:, 2 * half :], mine_here]),
    )
    ours = picked(True) + local.astype(F32)
    ours, attended, grad_q = lax.optimization_barrier((ours, attended, grad_q))
    total = (ours + shifted.astype(F32)).astype(BF16)
    grad_k = jnp.concatenate([total[0, :, :HEAD], total[1, :, :HEAD]], 1)
    grad_v = jnp.concatenate([total[0, :, HEAD:], total[1, :, HEAD:]], 1)
    return attended, grad_q, grad_k, grad_v


def solution(mesh):
    split = P(("blk", "uly"), None)
    return jax.shard_map(
        shards,
        mesh=mesh,
        in_specs=(split, split, split, split, P()),
        out_specs=(split, split, split, split),
        check_vma=False,
    )
```

time: 92.5 us -> 81.4 us (0.88)
  blocking collectives: 18.5 us -> 0 us
  starting transfers between devices: 16 us -> 28 us
  waiting for transfers between devices: 29.2 us -> 21.7 us
  local copies, waits for them, and re-layouts: 3.89 us -> 8.44 us
  Pallas kernels: 20.4 us -> 16.9 us
  other arithmetic: 2.38 us -> 4.97 us
    all_to_all x1 -> x0, blocking collectives: 18.5 us -> none  [within_ring(): lax.all_to_all(blocks, 'uly', 0, 0, axis_index_groups=groups, tiled=True)]
    ppermute x2, waiting for transfers between devices: 14.6 us -> 4.26 us  [ring_shift(): return lax.ppermute(block, ('uly', 'blk'), route)]
    ppermute x0 -> x4, starting transfers between devices: none -> 8.63 us  [to_sibling(): return lax.ppermute(block, 'uly', [(i, i ^ 1) for i in range(lanes)])]
    pallas_call x1, Pallas kernels: 20.4 us -> 16.9 us  [attention(): pl.pallas_call(attention_kernel, grid_spec=pltpu.PrefetchScalarGridSpec(n...]
    all_to_all x1 -> x2, starting transfers between devices: 4.43 us -> 7.81 us  [within_ring(): lax.all_to_all(blocks, 'uly', 0, 0, axis_index_groups=groups, tiled=True)]
    dynamic_slice x0 -> x2, local copies, waits for them, and re-layouts: none -> 2.3 us  [heads_of(): return lax.dynamic_slice_in_dim(block, group * width, width, 1)]
    select_n x1 -> x3, other arithmetic: 1.11 us -> 3.33 us  [the longest x2 2.43 us: joined(): jnp.where(core == 0, jnp.concatenate([a, b], 1), jnp.concatenate([b, a], 1))]
    all_to_all x1 -> x2, waiting for transfers between devices: 14.6 us -> 16.5 us  [within_ring(): lax.all_to_all(blocks, 'uly', 0, 0, axis_index_groups=groups, tiled=True)]
  transfers between devices with their start and end apart: 3 -> 8, of which waited for: 3 -> 4; matrix products, arithmetic and copies ran while one was open for 1% -> 10% of each run, Pallas kernels for 0% -> 0%
where the time goes in v2:
time: 81.4 us; the launch traced here: 80.7 us
  starting transfers between devices  28 us (34%)
  waiting for transfers between devices  21.7 us (27%)
  Pallas kernels  16.9 us (21%)
  local copies, waits for them, and re-layouts  8.44 us (10%)
  other arithmetic  4.97 us (6%)
  between operations  0.83 us (1%)
    pallas_call x1, Pallas kernels, attention(): pl.pallas_call(attention_kernel, grid_spec=pltpu.PrefetchScalarGridSpec(n...  16.9 us
    all_to_all x2, waiting for transfers between devices, within_ring(): lax.all_to_all(blocks, 'uly', 0, 0, axis_index_groups=groups, tiled=True)  16.5 us
    ppermute x2, starting transfers between devices, ring_shift(): return lax.ppermute(block, ('uly', 'blk'), route)  11.5 us
    ppermute x4, starting transfers between devices, to_sibling(): return lax.ppermute(block, 'uly', [(i, i ^ 1) for i in range(lanes)])  8.63 us
    all_to_all x2, starting transfers between devices, within_ring(): lax.all_to_all(blocks, 'uly', 0, 0, axis_index_groups=groups, tiled=True)  7.81 us
    ppermute x2, waiting for transfers between devices, ring_shift(): return lax.ppermute(block, ('uly', 'blk'), route)  4.26 us
    unnamed x10, local copies, waits for them, and re-layouts  3.07 us
    select_n x2, other arithmetic, joined(): jnp.where(core == 0, jnp.concatenate([a, b], 1), jnp.concatenate([b, a], 1))  2.43 us
  transfers between devices with their start and end apart: 8, of which 4 were waited for; matrix products, arithmetic and copies ran while one was open for 10% of the time, Pallas kernels for 0%

profile of v2, /device:TPU:56, one launch (start us, length us, event | category | flops | bytes accessed | tf_op | source)
XLA Modules:
  0.0 80.7 jit_solution(7473278010581457798)
XLA Ops:
  0.6 0.8 %fusion.2 = (bf16[128,128]{1,0:T(8,128)(2,1)S(1)}, bf16[128,128]{1,0:T(8,128)(2,1)S(1)}, bf16[128,128]{1,0:T(8,128)(2,1)S(1)}, bf16[128,128]{1,0:T(8,128)(2,1)S(1)}) fusion(bf16[128,256]{1,0:T(8,128)(2,1)} %param.6, bf16[128,256]{1,0:T(8,128)(2,1)} %param.7), kind=kLoop, calls=%fused_computation.26 | loop fusion | bytes 262144 | tf_op jit(solution)/shard_map/slice | solution.py:255
  1.5 6.1 %collective-permute-start.2 = (bf16[128,512]{1,0:T(8,128)(2,1)S(1)}, bf16[128,512]{1,0:T(8,128)(2,1)S(1)}, u32[]{:S(2)}, u32[]{:S(2)}) collective-permute-start(bf16[128,512]{1,0:T(8,128)(2,1)S(1)} %pad_maximum_fusion), channel_id=1, source_target_pairs={{0,128},{16,144},{32,160},{48,176},{64,192},{80,208},{96,224},{112... | collective-permute-start | bytes 393224 | tf_op jit(solution)/shard_map/ppermute | solution.py:220
  7.6 2.3 %constant_dynamic-slice_fusion.2 = (bf16[128,2048]{1,0:T(8,128)(2,1)}, bf16[128,2048]{1,0:T(8,128)(2,1)}) fusion(bf16[128,4096]{1,0:T(8,128)(2,1)} %do_here_ref.1, s32[]{:T(128)S(6)} %select_n.92, bf16[128,4096]{1,0:T(8,128)(2,1)} %q_here_ref.1), kind=kLoop, calls=%fused_computation.21 | loop fusion | bytes 2097156 | tf_op jit(solution)/shard_map/dynamic_slice | solution.py:248
  10.0 1.9 %collective-permute-start = (bf16[128,2048]{1,0:T(8,128)(2,1)}, bf16[128,2048]{1,0:T(8,128)(2,1)S(1)}, u32[]{:S(2)}, u32[]{:S(2)}) collective-permute-start(bf16[128,2048]{1,0:T(8,128)(2,1)} %get-tuple-element.17), channel_id=1, source_target_pairs={{0,16},{16,0},{32,48},{48,32},{64,80},{80,64},{96,112},{112,96},{1... | collective-permute-start | bytes 1572872 | tf_op jit(solution)/shard_map/ppermute | solution.py:236
  11.9 2.4 %collective-permute-start.1 = (bf16[128,2048]{1,0:T(8,128)(2,1)}, bf16[128,2048]{1,0:T(8,128)(2,1)S(1)}, u32[]{:S(2)}, u32[]{:S(2)}) collective-permute-start(bf16[128,2048]{1,0:T(8,128)(2,1)} %get-tuple-element.18), channel_id=1, source_target_pairs={{0,16},{16,0},{32,48},{48,32},{64,80},{80,64},{96,112},{112,96},{1... | collective-permute-start | bytes 1572872 | tf_op jit(solution)/shard_map/ppermute | solution.py:236
  14.4 4.3 %collective-permute-done.2 = bf16[128,512]{1,0:T(8,128)(2,1)S(1)} collective-permute-done((bf16[128,512]{1,0:T(8,128)(2,1)S(1)}, bf16[128,512]{1,0:T(8,128)(2,1)S(1)}, u32[]{:S(2)}, u32[]{:S(2)}) %collective-permute-start.2) | collective-permute-done | bytes 131104 | tf_op jit(solution)/shard_map/ppermute | solution.py:220
  18.7 0.9 %bitcast_select_fusion = bf16[8,128,256]{2,1,0:T(8,128)(2,1)} fusion(pred[8]{0:T(512)(128)(4,1)S(1)} %fusion, bf16[2,128,256]{2,1,0:T(8,128)(2,1)S(1)} %copy.10, bf16[2,128,256]{2,1,0:T(8,128)(2,1)S(1)} %copy.9), kind=kLoop, calls=%fused_computation.2 | loop fusion | flops 262144 | bytes 786440 | tf_op jit(solution)/shard_map/jit(_where)/select_n | solution.py:257
  19.6 4.3 %all-to-all-start = ((bf16[8,128,256]{2,1,0:T(8,128)(2,1)}), bf16[8,128,256]{2,1,0:T(8,128)(2,1)S(1)}, u32[]{:S(2)}, u32[]{:S(2)}) async-start(bf16[8,128,256]{2,1,0:T(8,128)(2,1)} %bitcast_select_fusion), calls=%async_computation | async-start | bytes 1048576 | tf_op jit(solution)/shard_map/all_to_all | solution.py:226
  23.9 2.4 %collective-permute-start.3 = (bf16[128,256]{1,0:T(8,128)(2,1)S(1)}, bf16[128,256]{1,0:T(8,128)(2,1)S(1)}, u32[]{:S(2)}, u32[]{:S(2)}) collective-permute-start(bf16[128,256]{1,0:T(8,128)(2,1)S(1)} %get-tuple-element.19), channel_id=1, source_target_pairs={{0,16},{16,0},{32,48},{48,32},{64,80},{80,64},{96,112},{112,96},{1... | collective-permute-start | bytes 196616 | tf_op jit(solution)/shard_map/ppermute | solution.py:236
  26.3 0.9 %collective-permute-done.3.own_there_ref = bf16[128,256]{1,0:T(8,128)(2,1)S(1)} collective-permute-done((bf16[128,256]{1,0:T(8,128)(2,1)S(1)}, bf16[128,256]{1,0:T(8,128)(2,1)S(1)}, u32[]{:S(2)}, u32[]{:S(2)}) %collective-permute-start.3) | collective-permute-done | bytes 65568 | tf_op jit(solution)/shard_map/ppermute | solution.py:236
  27.2 0.8 copy-done.2
  28.0 6.3 %all-to-all-done.seen_ref = bf16[8,128,256]{2,1,0:T(8,128)(2,1)S(1)} async-done(((bf16[8,128,256]{2,1,0:T(8,128)(2,1)}), bf16[8,128,256]{2,1,0:T(8,128)(2,1)S(1)}, u32[]{:S(2)}, u32[]{:S(2)}) %all-to-all-start) | async-done | bytes 524320 | tf_op jit(solution)/shard_map/all_to_all | solution.py:226
  34.3 1.2 %copy-done.1 = bf16[128,4096]{1,0:T(8,128)(2,1)S(1)} copy-done((bf16[128,4096]{1,0:T(8,128)(2,1)S(1)}, bf16[128,4096]{1,0:T(8,128)(2,1)}, u32[]{:S(2)}) %copy-start.1) | copy-done | bytes 1048600
  35.5 1.0 %copy-done.3 = bf16[128,2048]{1,0:T(8,128)(2,1)S(1)} copy-done((bf16[128,2048]{1,0:T(8,128)(2,1)S(1)}, bf16[128,2048]{1,0:T(8,128)(2,1)}, u32[]{:S(2)}) %copy-start.3) | copy-done | bytes 524312
  36.6 16.9 %shard_map.84 = (bf16[128,2048]{1,0:T(8,128)(2,1)S(1)}, bf16[128,2048]{1,0:T(8,128)(2,1)S(1)}, bf16[128,4352]{1,0:T(8,128)(2,1)}, bf16[8,128,256]{2,1,0:T(8,128)(2,1)}, bf16[128,256]{1,0:T(8,128)(2,1)S(1)}) custom-call(s32[3]{0:T(128)S(1)} %pad_add_fusion.where_ref, s32[1,130]{1,0:T(1,128)S(1)} %bitcast.26, bf16[128,4096]{1,0:T(8,128)(2,1)S(1)} %copy-done, ...), custom_call_target="tpu_custom_call" | custom-call | flops 6442450944 | bytes 4194304 | tf_op jit(solution)/shard_map/pallas_call | solution.py:171
  53.4 1.9 %collective-permute-start.4 = (bf16[128,4352]{1,0:T(8,128)(2,1)}, bf16[128,4352]{1,0:T(8,128)(2,1)}, u32[]{:S(2)}, u32[]{:S(2)}) collective-permute-start(bf16[128,4352]{1,0:T(8,128)(2,1)} %get-tuple-element.22), channel_id=1, source_target_pairs={{0,16},{16,0},{32,48},{48,32},{64,80},{80,64},{96,112},{112,96},{1... | collective-permute-start | bytes 3342344 | tf_op jit(solution)/shard_map/ppermute | solution.py:236
  55.3 3.5 %all-to-all-start.1 = ((bf16[8,128,256]{2,1,0:T(8,128)(2,1)}), bf16[8,128,256]{2,1,0:T(8,128)(2,1)S(1)}, u32[]{:S(2)}, u32[]{:S(2)}) async-start(bf16[8,128,256]{2,1,0:T(8,128)(2,1)} %get-tuple-element.20), calls=%async_computation.1 | async-start | bytes 1048576 | tf_op jit(solution)/shard_map/all_to_all | solution.py:226
  58.9 10.2 %all-to-all-done.1 = bf16[8,128,256]{2,1,0:T(8,128)(2,1)S(1)} async-done(((bf16[8,128,256]{2,1,0:T(8,128)(2,1)}), bf16[8,128,256]{2,1,0:T(8,128)(2,1)S(1)}, u32[]{:S(2)}, u32[]{:S(2)}) %all-to-all-start.1) | async-done | bytes 524320 | tf_op jit(solution)/shard_map/all_to_all | solution.py:226
  69.2 5.4 %collective-permute-start.5 = (bf16[2,128,256]{2,1,0:T(8,128)(2,1)S(1)}, bf16[2,128,256]{2,1,0:T(8,128)(2,1)S(1)}, u32[]{:S(2)}, u32[]{:S(2)}) collective-permute-start(bf16[2,128,256]{2,1,0:T(8,128)(2,1)S(1)} %add_convert_fusion.1), channel_id=1, source_target_pairs={{128,0},{144,16},{160,32},{176,48},{192,64},{208,80},{224,96},{240... | collective-permute-start | bytes 393224 | tf_op jit(solution)/shard_map/ppermute | solution.py:220
  74.7 1.3 %fusion.1 = (bf16[128,2048]{1,0:T(8,128)(2,1)S(1)}, bf16[128,2048]{1,0:T(8,128)(2,1)S(1)}) fusion(bf16[128,4352]{1,0:T(8,128)(2,1)} %collective-permute-done.4), kind=kLoop, calls=%fused_computation.25 | loop fusion | bytes 2097152 | tf_op jit(solution)/shard_map/slice | solution.py:282
  76.0 1.2 %maximum_select_fusion = bf16[128,4096]{1,0:T(8,128)(2,1)} fusion(bf16[128,2048]{1,0:T(8,128)(2,1)S(1)} %get-tuple-element.29, bf16[128,2048]{1,0:T(8,128)(2,1)S(1)} %get-tuple-element.23, pred[]{:T(512)S(6)} %eq.17), kind=kLoop, calls=%fused_computation | loop fusion | flops 4718592 | bytes 2097153 | tf_op jit(solution)/shard_map/jit(_where)/select_n | solution.py:280
  77.2 1.2 %maximum_select_fusion.1 = bf16[128,4096]{1,0:T(8,128)(2,1)} fusion(bf16[128,2048]{1,0:T(8,128)(2,1)S(1)} %get-tuple-element.28, bf16[128,2048]{1,0:T(8,128)(2,1)S(1)} %get-tuple-element.24, pred[]{:T(512)S(6)} %eq.17), kind=kLoop, calls=%fused_computation.1 | loop fusion | flops 4718592 | bytes 2097153 | tf_op jit(solution)/shard_map/jit(_where)/select_n | solution.py:280
  78.4 0.8 %slice_bitcast_fusion = bf16[1,128,256]{2,1,0:T(8,128)(2,1)S(1)} fusion(bf16[128,4352]{1,0:T(8,128)(2,1)} %collective-permute-done.4), kind=kLoop, calls=%fused_computation.8 | loop fusion | bytes 131072 | tf_op jit(solution)/shard_map/stack | solution.py:285
  79.4 0.6 pad_maximum_fusion.1
  (24 shorter events, 1.2 us)
Async XLA Ops:
  1.5 17.2 %collective-permute-start.2 = (bf16[128,512]{1,0:T(8,128)(2,1)S(1)}, bf16[128,512]{1,0:T(8,128)(2,1)S(1)}, u32[]{:S(2)}, u32[]{:S(2)}) collective-permute-start(bf16[128,512]{1,0:T(8,128)(2,1)S(1)} %pad_maximum_fusion), channel_id=1, source_target_pairs={{0,128},{16,144},{32,160},{48,176},{64,192},{80,208},{96,224},{112... | collective-permute-start | bytes 393224 | tf_op jit(solution)/shard_map/ppermute | solution.py:220
  10.0 17.2 %collective-permute-start = (bf16[128,2048]{1,0:T(8,128)(2,1)}, bf16[128,2048]{1,0:T(8,128)(2,1)S(1)}, u32[]{:S(2)}, u32[]{:S(2)}) collective-permute-start(bf16[128,2048]{1,0:T(8,128)(2,1)} %get-tuple-element.17), channel_id=1, source_target_pairs={{0,16},{16,0},{32,48},{48,32},{64,80},{80,64},{96,112},{112,96},{1... | collective-permute-start | bytes 1572872 | tf_op jit(solution)/shard_map/ppermute | solution.py:236
  11.9 15.3 %collective-permute-start.1 = (bf16[128,2048]{1,0:T(8,128)(2,1)}, bf16[128,2048]{1,0:T(8,128)(2,1)S(1)}, u32[]{:S(2)}, u32[]{:S(2)}) collective-permute-start(bf16[128,2048]{1,0:T(8,128)(2,1)} %get-tuple-element.18), channel_id=1, source_target_pairs={{0,16},{16,0},{32,48},{48,32},{64,80},{80,64},{96,112},{112,96},{1... | collective-permute-start | bytes 1572872 | tf_op jit(solution)/shard_map/ppermute | solution.py:236
  18.7 15.6 %copy-start = (bf16[128,4096]{1,0:T(8,128)(2,1)S(1)}, bf16[128,4096]{1,0:T(8,128)(2,1)}, u32[]{:S(2)}) copy-start(bf16[128,4096]{1,0:T(8,128)(2,1)} %q_here_ref.1) | copy-start | bytes 3145732
  18.7 15.6 %copy-start.4 = (s32[130]{0:T(256)S(1)}, s32[130]{0:T(256)}, u32[]{:S(2)}) copy-start(s32[130]{0:T(256)} %param.9) | copy-start | bytes 1564
  19.6 14.6 %all-to-all-start = ((bf16[8,128,256]{2,1,0:T(8,128)(2,1)}), bf16[8,128,256]{2,1,0:T(8,128)(2,1)S(1)}, u32[]{:S(2)}, u32[]{:S(2)}) async-start(bf16[8,128,256]{2,1,0:T(8,128)(2,1)} %bitcast_select_fusion), calls=%async_computation | async-start | bytes 1048576 | tf_op jit(solution)/shard_map/all_to_all | solution.py:226
  23.9 3.3 %collective-permute-start.3 = (bf16[128,256]{1,0:T(8,128)(2,1)S(1)}, bf16[128,256]{1,0:T(8,128)(2,1)S(1)}, u32[]{:S(2)}, u32[]{:S(2)}) collective-permute-start(bf16[128,256]{1,0:T(8,128)(2,1)S(1)} %get-tuple-element.19), channel_id=1, source_target_pairs={{0,16},{16,0},{32,48},{48,32},{64,80},{80,64},{96,112},{112,96},{1... | collective-permute-start | bytes 196616 | tf_op jit(solution)/shard_map/ppermute | solution.py:236
  27.2 0.8 copy-start.2
  34.3 1.2 %copy-start.1 = (bf16[128,4096]{1,0:T(8,128)(2,1)S(1)}, bf16[128,4096]{1,0:T(8,128)(2,1)}, u32[]{:S(2)}) copy-start(bf16[128,4096]{1,0:T(8,128)(2,1)} %do_here_ref.1) | copy-start | bytes 3145732
  35.5 1.0 %copy-start.3 = (bf16[128,2048]{1,0:T(8,128)(2,1)S(1)}, bf16[128,2048]{1,0:T(8,128)(2,1)}, u32[]{:S(2)}) copy-start(bf16[128,2048]{1,0:T(8,128)(2,1)} %copy-done.2) | copy-start | bytes 1572868
  53.4 21.3 %collective-permute-start.4 = (bf16[128,4352]{1,0:T(8,128)(2,1)}, bf16[128,4352]{1,0:T(8,128)(2,1)}, u32[]{:S(2)}, u32[]{:S(2)}) collective-permute-start(bf16[128,4352]{1,0:T(8,128)(2,1)} %get-tuple-element.22), channel_id=1, source_target_pairs={{0,16},{16,0},{32,48},{48,32},{64,80},{80,64},{96,112},{112,96},{1... | collective-permute-start | bytes 3342344 | tf_op jit(solution)/shard_map/ppermute | solution.py:236
  55.3 13.8 %all-to-all-start.1 = ((bf16[8,128,256]{2,1,0:T(8,128)(2,1)}), bf16[8,128,256]{2,1,0:T(8,128)(2,1)S(1)}, u32[]{:S(2)}, u32[]{:S(2)}) async-start(bf16[8,128,256]{2,1,0:T(8,128)(2,1)} %get-tuple-element.20), calls=%async_computation.1 | async-start | bytes 1048576 | tf_op jit(solution)/shard_map/all_to_all | solution.py:226
  69.2 10.1 %collective-permute-start.5 = (bf16[2,128,256]{2,1,0:T(8,128)(2,1)S(1)}, bf16[2,128,256]{2,1,0:T(8,128)(2,1)S(1)}, u32[]{:S(2)}, u32[]{:S(2)}) collective-permute-start(bf16[2,128,256]{2,1,0:T(8,128)(2,1)S(1)} %add_convert_fusion.1), channel_id=1, source_target_pairs={{128,0},{144,16},{160,32},{176,48},{192,64},{208,80},{224,96},{240... | collective-permute-start | bytes 393224 | tf_op jit(solution)/shard_map/ppermute | solution.py:220

commit v3 on v2

--- a/solution.py
+++ b/solution.py
@@ -1,3 +1,4 @@
+import functools
 import math
 
 import jax
@@ -41,8 +42,8 @@
     there_ref,
     terms_ref,
     mine_here_ref,
-    q_now,
-    do_now,
+    q_side,
+    do_side,
     own_now,
     first_own,
     k_fill,
@@ -52,11 +53,12 @@
     dq_now,
     dk_acc,
     dv_acc,
+    sems,
 ):
     core, chip = where_ref[0], where_ref[1]
     side = pl.program_id(0)
     index = lax.rem(core + side, 2)
-    half = q_now.shape[1]
+    half = o_now.shape[1]
     first_token = where_ref[2] + index * TOK
     offsets = offsets_ref[...]
     start = jnp.max(jnp.where(offsets <= first_token, offsets, 0))
@@ -65,19 +67,28 @@
     def slot(m):
         return lax.rem(2 * chip + 1 + m, RING)
 
+    mine = pl.ds(pl.multiple_of(core * half, half), half)
+    fetches = [
+        [
+            pltpu.make_async_copy(q_here_ref.at[:, mine], q_side.at[0], sems.at[0]),
+            pltpu.make_async_copy(do_here_ref.at[:, mine], do_side.at[0], sems.at[1]),
+        ],
+        [
+            pltpu.make_async_copy(q_there_ref, q_side.at[1], sems.at[2]),
+            pltpu.make_async_copy(do_there_ref, do_side.at[1], sems.at[3]),
+        ],
+    ]
+
     @pl.when(side == 0)
     def _():
-        mine = pl.ds(pl.multiple_of(core * half, half), half)
-        q_now[...] = q_here_ref[:, mine]
-        do_now[...] = do_here_ref[:, mine]
+        for fetch in fetches[0] + fetches[1]:
+            fetch.start()
         own_now[...] = own_here_ref[...]
         dk_acc[...] = jnp.zeros_like(dk_acc)
         dv_acc[...] = jnp.zeros_like(dv_acc)
 
     @pl.when(side == 1)
     def _():
-        q_now[...] = q_there_ref[...]
-        do_now[...] = do_there_ref[...]
         own_now[...] = own_there_ref[...]
 
     @pl.when(core == 0)
@@ -103,38 +114,55 @@
     k_fill[last] = own_now[:, :HEAD]
     k_zero[last] = own_now[:, :HEAD]
     v_zero[last] = own_now[:, HEAD:]
-    hidden = RING - 1 - before
-
-    heads = half // HEAD
-    q, do = stacked(q_now), stacked(do_now)
-    k, v = k_fill[...], v_zero[...]
-    row = lax.broadcasted_iota(jnp.int32, (TOK, TOK), 0)
-    col = lax.broadcasted_iota(jnp.int32, (TOK, TOK), 1)
-    causal = jnp.where(col <= row, 0.0, -1e30).astype(F32)
-    s = dot(q, k, 1, 1)
-    s = jnp.concatenate([s[:, : KEYS - TOK], s[:, KEYS - TOK :] + jnp.concatenate([causal] * heads, 0)], 1)
-    top = jnp.max(s, axis=1, keepdims=True)
-    p = jnp.exp2(s * SCALE2 - top * SCALE2)
-    p_low = p.astype(BF16)
-    wide = p[:, :TOK]
-    for w in range(1, RING):
-        wide = wide + p[:, w * TOK : (w + 1) * TOK]
-    total = jnp.sum(wide - hidden.astype(F32) * p[:, :TOK], axis=1, keepdims=True)
-    inv = 1.0 / total
-    o = (dot(p_low, v, 1, 0) * inv).astype(BF16)
-    do_wide = do.astype(F32)
-    delta = jnp.sum(do_wide * o.astype(F32), axis=1, keepdims=True) * inv
-    do_norm = (do_wide * inv).astype(BF16)
-    ds = p_low * (dot(do_norm, v, 1, 1) - delta).astype(BF16)
-    dq = (dot(ds, k_zero[...], 1, 0) * SCALE).astype(BF16)
-    for r in range(heads):
-        o_now[:, r * HEAD : (r + 1) * HEAD] = o[r * TOK : (r + 1) * TOK]
-        dq_now[:, r * HEAD : (r + 1) * HEAD] = dq[r * TOK : (r + 1) * TOK]
-    place = lax.broadcasted_iota(jnp.int32, (HEAD, KEYS), 1)
-    shown = place >= hidden * TOK
-    window = pl.ds(pl.multiple_of(index * TOK, TOK), KEYS)
-    dk_acc[:, window] += jnp.where(shown, dot(q.T, ds, 1, 0), 0.0)
-    dv_acc[:, window] += jnp.where(shown, dot(do_norm.T, p_low, 1, 0), 0.0)
+
+    @pl.when(side == 0)
+    def _():
+        for fetch in fetches[0]:
+            fetch.wait()
+
+    @pl.when(side == 1)
+    def _():
+        for fetch in fetches[1]:
+            fetch.wait()
+
+    def attend(tiles):
+        width = 2 * tiles * TOK
+        heads = half // HEAD
+        q, do = stacked(q_side.at[side]), stacked(do_side.at[side])
+        k, v = k_fill[KEYS - width :], v_zero[KEYS - width :]
+        hidden = 2 * tiles - 1 - before
+        row = lax.broadcasted_iota(jnp.int32, (TOK, TOK), 0)
+        col = lax.broadcasted_iota(jnp.int32, (TOK, TOK), 1)
+        causal = jnp.where(col <= row, 0.0, -1e30).astype(F32)
+        s = dot(q, k, 1, 1)
+        s = jnp.concatenate(
+            [s[:, : width - TOK], s[:, width - TOK :] + jnp.concatenate([causal] * heads, 0)], 1
+        )
+        top = jnp.max(s, axis=1, keepdims=True)
+        p = jnp.exp2(s * SCALE2 - top * SCALE2)
+        p_low = p.astype(BF16)
+        wide = p[:, :TOK]
+        for w in range(1, 2 * tiles):
+            wide = wide + p[:, w * TOK : (w + 1) * TOK]
+        total = jnp.sum(wide - hidden.astype(F32) * p[:, :TOK], axis=1, keepdims=True)
+        inv = 1.0 / total
+        o = (dot(p_low, v, 1, 0) * inv).astype(BF16)
+        do_wide = do.astype(F32)
+        delta = jnp.sum(do_wide * o.astype(F32), axis=1, keepdims=True) * inv
+        do_norm = (do_wide * inv).astype(BF16)
+        ds = p_low * (dot(do_norm, v, 1, 1) - delta).astype(BF16)
+        dq = (dot(ds, k_zero[KEYS - width :], 1, 0) * SCALE).astype(BF16)
+        for r in range(heads):
+            o_now[:, r * HEAD : (r + 1) * HEAD] = o[r * TOK : (r + 1) * TOK]
+            dq_now[:, r * HEAD : (r + 1) * HEAD] = dq[r * TOK : (r + 1) * TOK]
+        place = lax.broadcasted_iota(jnp.int32, (HEAD, width), 1)
+        shown = place >= hidden * TOK
+        window = pl.ds(pl.multiple_of(index * TOK + KEYS - width, TOK), width)
+        dk_acc[:, window] += jnp.where(shown, dot(q.T, ds, 1, 0), 0.0)
+        dv_acc[:, window] += jnp.where(shown, dot(do_norm.T, p_low, 1, 0), 0.0)
+
+    for tiles in range(1, RING // 2 + 1):
+        pl.when(lax.shift_right_logical(before, 1) == tiles - 1)(functools.partial(attend, tiles))
 
     @pl.when(side == 0)
     def _():
@@ -168,16 +196,17 @@
     own = own_here.shape
     there = (TOK, 2 * half[1] + own[1])
     vmem = pl.BlockSpec(memory_space=pltpu.VMEM)
+    anywhere = pl.BlockSpec(memory_space=pl.ANY)
     return pl.pallas_call(
         attention_kernel,
         grid_spec=pltpu.PrefetchScalarGridSpec(
             num_scalar_prefetch=1,
             grid=(2,),
-            in_specs=[vmem] * 8,
+            in_specs=[vmem] + [anywhere] * 4 + [vmem] * 3,
             out_specs=[vmem] * 5,
             scratch_shapes=[
-                pltpu.VMEM(half, BF16),
-                pltpu.VMEM(half, BF16),
+                pltpu.VMEM((2, *half), BF16),
+                pltpu.VMEM((2, *half), BF16),
                 pltpu.VMEM(own, BF16),
                 pltpu.VMEM(own, BF16),
                 pltpu.VMEM((KEYS, HEAD), BF16),
@@ -187,6 +216,7 @@
                 pltpu.VMEM(half, BF16),
                 pltpu.VMEM((HEAD, SPAN), F32),
                 pltpu.VMEM((HEAD, SPAN), F32),
+                pltpu.SemaphoreType.DMA((4,)),
             ],
         ),
         out_shape=[
@@ -272,7 +302,10 @@
             for j in range(RING // 2)
         )
 
-    shifted = ring_shift(picked(False).astype(BF16), -1)
+    def side_by_side(a):
+        return jnp.concatenate([a[0, :, :HEAD], a[1, :, :HEAD], a[0, :, HEAD:], a[1, :, HEAD:]], 1)
+
+    shifted = ring_shift(side_by_side(picked(False).astype(BF16)), -1)
     back = to_sibling(there)
     half = o_here.shape[1]
 
@@ -285,12 +318,10 @@
         jnp.stack([mine_here, back[:, 2 * half :]]),
         jnp.stack([back[:, 2 * half :], mine_here]),
     )
-    ours = picked(True) + local.astype(F32)
+    ours = side_by_side(picked(True) + local.astype(F32))
     ours, attended, grad_q = lax.optimization_barrier((ours, attended, grad_q))
     total = (ours + shifted.astype(F32)).astype(BF16)
-    grad_k = jnp.concatenate([total[0, :, :HEAD], total[1, :, :HEAD]], 1)
-    grad_v = jnp.concatenate([total[0, :, HEAD:], total[1, :, HEAD:]], 1)
-    return attended, grad_q, grad_k, grad_v
+    return attended, grad_q, total[:, : 2 * HEAD], total[:, 2 * HEAD :]
 
 
 def solution(mesh):

time: 81.4 us -> 80.2 us (0.985)
  Pallas kernels: 16.9 us -> 9.78 us
  waiting for transfers between devices: 21.7 us -> 25.7 us
  starting transfers between devices: 28 us -> 30 us
  other arithmetic: 4.97 us -> 3.75 us
    pallas_call x1, Pallas kernels: 16.9 us -> 9.78 us  [attention(): pl.pallas_call(attention_kernel, grid_spec=pltpu.PrefetchScalarGridSpec(n...]
    all_to_all x2, starting transfers between devices: 7.81 us -> 13.2 us  [within_ring(): lax.all_to_all(blocks, 'uly', 0, 0, axis_index_groups=groups, tiled=True)]
    ppermute x2, waiting for transfers between devices: 4.26 us -> 8.21 us  [ring_shift(): return lax.ppermute(block, ('uly', 'blk'), route)]
    ppermute x2, starting transfers between devices: 11.5 us -> 8.08 us  [ring_shift(): return lax.ppermute(block, ('uly', 'blk'), route)]
    concatenate x2, other arithmetic: 1.28 us -> 0.04 us  [side_by_side(): jnp.concatenate([a[0, :, :HEAD], a[1, :, :HEAD], a[0, :, HEAD:], a[1, :,...]
  transfers between devices with their start and end apart: 8 -> 8, of which waited for: 4 -> 5; matrix products, arithmetic and copies ran while one was open for 10% -> 10% of each run, Pallas kernels for 0% -> 0%
where the time goes in v3:
time: 80.2 us; the launch traced here: 79.1 us
  starting transfers between devices  30 us (37%)
  waiting for transfers between devices  25.7 us (32%)
  Pallas kernels  9.78 us (12%)
  local copies, waits for them, and re-layouts  9.12 us (11%)
  other arithmetic  3.75 us (5%)
  between operations  0.82 us (1%)
    all_to_all x2, waiting for transfers between devices, within_ring(): lax.all_to_all(blocks, 'uly', 0, 0, axis_index_groups=groups, tiled=True)  16.6 us
    all_to_all x2, starting transfers between devices, within_ring(): lax.all_to_all(blocks, 'uly', 0, 0, axis_index_groups=groups, tiled=True)  13.2 us
    pallas_call x1, Pallas kernels, attention(): pl.pallas_call(attention_kernel, grid_spec=pltpu.PrefetchScalarGridSpec(n...  9.78 us
    ppermute x4, starting transfers between devices, to_sibling(): return lax.ppermute(block, 'uly', [(i, i ^ 1) for i in range(lanes)])  8.64 us
    ppermute x2, waiting for transfers between devices, ring_shift(): return lax.ppermute(block, ('uly', 'blk'), route)  8.21 us
    ppermute x2, starting transfers between devices, ring_shift(): return lax.ppermute(block, ('uly', 'blk'), route)  8.08 us
    unnamed x10, local copies, waits for them, and re-layouts  3.07 us
    select_n x2, other arithmetic, joined(): jnp.where(core == 0, jnp.concatenate([a, b], 1), jnp.concatenate([b, a], 1))  2.43 us
  transfers between devices with their start and end apart: 8, of which 5 were waited for; matrix products, arithmetic and copies ran while one was open for 10% of the time, Pallas kernels for 0%

profile of v3, /device:TPU:56, one launch (start us, length us, event | category | flops | bytes accessed | tf_op | source)
XLA Modules:
  0.0 79.1 jit_solution(13398310070183790901)
XLA Ops:
  0.6 0.8 %fusion.3 = (bf16[128,128]{1,0:T(8,128)(2,1)S(1)}, bf16[128,128]{1,0:T(8,128)(2,1)S(1)}, bf16[128,128]{1,0:T(8,128)(2,1)S(1)}, bf16[128,128]{1,0:T(8,128)(2,1)S(1)}) fusion(bf16[128,256]{1,0:T(8,128)(2,1)} %param.6, bf16[128,256]{1,0:T(8,128)(2,1)} %param.7), kind=kLoop, calls=%fused_computation.31 | loop fusion | bytes 262144 | tf_op jit(solution)/shard_map/slice | solution.py:285
  1.5 6.1 %collective-permute-start.2 = (bf16[128,512]{1,0:T(8,128)(2,1)S(1)}, bf16[128,512]{1,0:T(8,128)(2,1)S(1)}, u32[]{:S(2)}, u32[]{:S(2)}) collective-permute-start(bf16[128,512]{1,0:T(8,128)(2,1)S(1)} %pad_maximum_fusion.1), channel_id=1, source_target_pairs={{0,128},{16,144},{32,160},{48,176},{64,192},{80,208},{96,224},{112... | collective-permute-start | bytes 393224 | tf_op jit(solution)/shard_map/ppermute | solution.py:250
  7.6 2.3 %constant_dynamic-slice_fusion.2 = (bf16[128,2048]{1,0:T(8,128)(2,1)}, bf16[128,2048]{1,0:T(8,128)(2,1)}) fusion(bf16[128,4096]{1,0:T(8,128)(2,1)} %do_here_ref.1, s32[]{:T(128)S(6)} %select_n.92, bf16[128,4096]{1,0:T(8,128)(2,1)} %q_here_ref.1), kind=kLoop, calls=%fused_computation.25 | loop fusion | bytes 2097156 | tf_op jit(solution)/shard_map/dynamic_slice | solution.py:278
  10.0 1.9 %collective-permute-start = (bf16[128,2048]{1,0:T(8,128)(2,1)}, bf16[128,2048]{1,0:T(8,128)(2,1)S(1)}, u32[]{:S(2)}, u32[]{:S(2)}) collective-permute-start(bf16[128,2048]{1,0:T(8,128)(2,1)} %get-tuple-element.17), channel_id=1, source_target_pairs={{0,16},{16,0},{32,48},{48,32},{64,80},{80,64},{96,112},{112,96},{1... | collective-permute-start | bytes 1572872 | tf_op jit(solution)/shard_map/ppermute | solution.py:266
  11.9 2.4 %collective-permute-start.1 = (bf16[128,2048]{1,0:T(8,128)(2,1)}, bf16[128,2048]{1,0:T(8,128)(2,1)S(1)}, u32[]{:S(2)}, u32[]{:S(2)}) collective-permute-start(bf16[128,2048]{1,0:T(8,128)(2,1)} %get-tuple-element.18), channel_id=1, source_target_pairs={{0,16},{16,0},{32,48},{48,32},{64,80},{80,64},{96,112},{112,96},{1... | collective-permute-start | bytes 1572872 | tf_op jit(solution)/shard_map/ppermute | solution.py:266
  14.4 4.3 %collective-permute-done.2 = bf16[128,512]{1,0:T(8,128)(2,1)S(1)} collective-permute-done((bf16[128,512]{1,0:T(8,128)(2,1)S(1)}, bf16[128,512]{1,0:T(8,128)(2,1)S(1)}, u32[]{:S(2)}, u32[]{:S(2)}) %collective-permute-start.2) | collective-permute-done | bytes 131104 | tf_op jit(solution)/shard_map/ppermute | solution.py:250
  18.7 0.9 %bitcast_select_fusion = bf16[8,128,256]{2,1,0:T(8,128)(2,1)} fusion(pred[8]{0:T(512)(128)(4,1)S(1)} %fusion, bf16[2,128,256]{2,1,0:T(8,128)(2,1)S(1)} %copy.10, bf16[2,128,256]{2,1,0:T(8,128)(2,1)S(1)} %copy.9), kind=kLoop, calls=%fused_computation.2 | loop fusion | flops 262144 | bytes 786440 | tf_op jit(solution)/shard_map/jit(_where)/select_n | solution.py:287
  19.6 4.3 %all-to-all-start = ((bf16[8,128,256]{2,1,0:T(8,128)(2,1)}), bf16[8,128,256]{2,1,0:T(8,128)(2,1)S(1)}, u32[]{:S(2)}, u32[]{:S(2)}) async-start(bf16[8,128,256]{2,1,0:T(8,128)(2,1)} %bitcast_select_fusion), calls=%async_computation | async-start | bytes 1048576 | tf_op jit(solution)/shard_map/all_to_all | solution.py:256
  23.9 2.4 %collective-permute-start.3 = (bf16[128,256]{1,0:T(8,128)(2,1)S(1)}, bf16[128,256]{1,0:T(8,128)(2,1)S(1)}, u32[]{:S(2)}, u32[]{:S(2)}) collective-permute-start(bf16[128,256]{1,0:T(8,128)(2,1)S(1)} %get-tuple-element.19), channel_id=1, source_target_pairs={{0,16},{16,0},{32,48},{48,32},{64,80},{80,64},{96,112},{112,96},{1... | collective-permute-start | bytes 196616 | tf_op jit(solution)/shard_map/ppermute | solution.py:266
  26.4 0.9 %collective-permute-done.3.own_there_ref = bf16[128,256]{1,0:T(8,128)(2,1)S(1)} collective-permute-done((bf16[128,256]{1,0:T(8,128)(2,1)S(1)}, bf16[128,256]{1,0:T(8,128)(2,1)S(1)}, u32[]{:S(2)}, u32[]{:S(2)}) %collective-permute-start.3) | collective-permute-done | bytes 65568 | tf_op jit(solution)/shard_map/ppermute | solution.py:266
  27.2 0.8 %copy-done.2 = bf16[128,2048]{1,0:T(8,128)(2,1)} copy-done((bf16[128,2048]{1,0:T(8,128)(2,1)}, bf16[128,2048]{1,0:T(8,128)(2,1)S(1)}, u32[]{:S(2)}) %copy-start.2) | copy-done | bytes 524312
  28.0 6.3 %all-to-all-done.seen_ref = bf16[8,128,256]{2,1,0:T(8,128)(2,1)S(1)} async-done(((bf16[8,128,256]{2,1,0:T(8,128)(2,1)}), bf16[8,128,256]{2,1,0:T(8,128)(2,1)S(1)}, u32[]{:S(2)}, u32[]{:S(2)}) %all-to-all-start) | async-done | bytes 524320 | tf_op jit(solution)/shard_map/all_to_all | solution.py:256
  34.3 1.2 %copy-done.1 = bf16[128,4096]{1,0:T(8,128)(2,1)S(1)} copy-done((bf16[128,4096]{1,0:T(8,128)(2,1)S(1)}, bf16[128,4096]{1,0:T(8,128)(2,1)}, u32[]{:S(2)}) %copy-start.1) | copy-done | bytes 1048600
  35.5 1.0 %copy-done.3 = bf16[128,2048]{1,0:T(8,128)(2,1)S(1)} copy-done((bf16[128,2048]{1,0:T(8,128)(2,1)S(1)}, bf16[128,2048]{1,0:T(8,128)(2,1)}, u32[]{:S(2)}) %copy-start.3) | copy-done | bytes 524312
  36.6 9.8 %shard_map.84 = (bf16[128,2048]{1,0:T(8,128)(2,1)S(1)}, bf16[128,2048]{1,0:T(8,128)(2,1)S(1)}, bf16[128,4352]{1,0:T(8,128)(2,1)}, bf16[8,128,256]{2,1,0:T(8,128)(2,1)}, bf16[128,256]{1,0:T(8,128)(2,1)S(1)}) custom-call(s32[3]{0:T(128)S(1)} %pad_add_fusion.where_ref, s32[1,130]{1,0:T(1,128)S(1)} %bitcast.34, bf16[128,4096]{1,0:T(8,128)(2,1)S(1)} %copy-done, ...), custom_call_target="tpu_custom_call" | custom-call | flops 6442450944 | bytes 4194304 | tf_op jit(solution)/shard_map/pallas_call | solution.py:200
  46.4 1.9 %collective-permute-start.4 = (bf16[128,4352]{1,0:T(8,128)(2,1)}, bf16[128,4352]{1,0:T(8,128)(2,1)}, u32[]{:S(2)}, u32[]{:S(2)}) collective-permute-start(bf16[128,4352]{1,0:T(8,128)(2,1)} %get-tuple-element.22), channel_id=1, source_target_pairs={{0,16},{16,0},{32,48},{48,32},{64,80},{80,64},{96,112},{112,96},{1... | collective-permute-start | bytes 3342344 | tf_op jit(solution)/shard_map/ppermute | solution.py:266
  48.3 8.9 %all-to-all-start.1 = ((bf16[8,128,256]{2,1,0:T(8,128)(2,1)}), bf16[8,128,256]{2,1,0:T(8,128)(2,1)S(1)}, u32[]{:S(2)}, u32[]{:S(2)}) async-start(bf16[8,128,256]{2,1,0:T(8,128)(2,1)} %get-tuple-element.20), calls=%async_computation.1 | async-start | bytes 1048576 | tf_op jit(solution)/shard_map/all_to_all | solution.py:256
  57.2 10.3 %all-to-all-done.1 = bf16[8,128,256]{2,1,0:T(8,128)(2,1)S(1)} async-done(((bf16[8,128,256]{2,1,0:T(8,128)(2,1)}), bf16[8,128,256]{2,1,0:T(8,128)(2,1)S(1)}, u32[]{:S(2)}, u32[]{:S(2)}) %all-to-all-start.1) | async-done | bytes 524320 | tf_op jit(solution)/shard_map/all_to_all | solution.py:256
  67.7 2.0 %collective-permute-start.5 = (bf16[128,512]{1,0:T(8,128)(2,1)S(1)}, bf16[128,512]{1,0:T(8,128)(2,1)S(1)}, u32[]{:S(2)}, u32[]{:S(2)}) collective-permute-start(bf16[128,512]{1,0:T(8,128)(2,1)S(1)} %pad_maximum_fusion.2), channel_id=1, source_target_pairs={{128,0},{144,16},{160,32},{176,48},{192,64},{208,80},{224,96},{240... | collective-permute-start | bytes 393224 | tf_op jit(solution)/shard_map/ppermute | solution.py:250
  69.7 1.3 %fusion.1 = (bf16[128,2048]{1,0:T(8,128)(2,1)S(1)}, bf16[128,2048]{1,0:T(8,128)(2,1)S(1)}) fusion(bf16[128,4352]{1,0:T(8,128)(2,1)} %collective-permute-done.4), kind=kLoop, calls=%fused_computation.29 | loop fusion | bytes 2097152 | tf_op jit(solution)/shard_map/slice | solution.py:315
  71.0 1.2 %maximum_select_fusion = bf16[128,4096]{1,0:T(8,128)(2,1)} fusion(bf16[128,2048]{1,0:T(8,128)(2,1)S(1)} %get-tuple-element.29, bf16[128,2048]{1,0:T(8,128)(2,1)S(1)} %get-tuple-element.23, pred[]{:T(512)S(6)} %eq.17), kind=kLoop, calls=%fused_computation | loop fusion | flops 4718592 | bytes 2097153 | tf_op jit(solution)/shard_map/jit(_where)/select_n | solution.py:313
  72.2 1.2 %maximum_select_fusion.1 = bf16[128,4096]{1,0:T(8,128)(2,1)} fusion(bf16[128,2048]{1,0:T(8,128)(2,1)S(1)} %get-tuple-element.28, bf16[128,2048]{1,0:T(8,128)(2,1)S(1)} %get-tuple-element.24, pred[]{:T(512)S(6)} %eq.17), kind=kLoop, calls=%fused_computation.1 | loop fusion | flops 4718592 | bytes 2097153 | tf_op jit(solution)/shard_map/jit(_where)/select_n | solution.py:313
  73.5 0.8 %slice_bitcast_fusion.4 = bf16[1,128,256]{2,1,0:T(8,128)(2,1)S(1)} fusion(bf16[128,4352]{1,0:T(8,128)(2,1)} %collective-permute-done.4), kind=kLoop, calls=%fused_computation.14 | loop fusion | bytes 131072 | tf_op jit(solution)/shard_map/stack | solution.py:318
  74.5 4.0 %collective-permute-done.5 = bf16[128,512]{1,0:T(8,128)(2,1)S(1)} collective-permute-done((bf16[128,512]{1,0:T(8,128)(2,1)S(1)}, bf16[128,512]{1,0:T(8,128)(2,1)S(1)}, u32[]{:S(2)}, u32[]{:S(2)}) %collective-permute-start.5) | collective-permute-done | bytes 131104 | tf_op jit(solution)/shard_map/ppermute | solution.py:250
  (26 shorter events, 1.3 us)
Async XLA Ops:
  1.5 17.2 %collective-permute-start.2 = (bf16[128,512]{1,0:T(8,128)(2,1)S(1)}, bf16[128,512]{1,0:T(8,128)(2,1)S(1)}, u32[]{:S(2)}, u32[]{:S(2)}) collective-permute-start(bf16[128,512]{1,0:T(8,128)(2,1)S(1)} %pad_maximum_fusion.1), channel_id=1, source_target_pairs={{0,128},{16,144},{32,160},{48,176},{64,192},{80,208},{96,224},{112... | collective-permute-start | bytes 393224 | tf_op jit(solution)/shard_map/ppermute | solution.py:250
  10.0 17.3 %collective-permute-start = (bf16[128,2048]{1,0:T(8,128)(2,1)}, bf16[128,2048]{1,0:T(8,128)(2,1)S(1)}, u32[]{:S(2)}, u32[]{:S(2)}) collective-permute-start(bf16[128,2048]{1,0:T(8,128)(2,1)} %get-tuple-element.17), channel_id=1, source_target_pairs={{0,16},{16,0},{32,48},{48,32},{64,80},{80,64},{96,112},{112,96},{1... | collective-permute-start | bytes 1572872 | tf_op jit(solution)/shard_map/ppermute | solution.py:266
  11.9 15.4 %collective-permute-start.1 = (bf16[128,2048]{1,0:T(8,128)(2,1)}, bf16[128,2048]{1,0:T(8,128)(2,1)S(1)}, u32[]{:S(2)}, u32[]{:S(2)}) collective-permute-start(bf16[128,2048]{1,0:T(8,128)(2,1)} %get-tuple-element.18), channel_id=1, source_target_pairs={{0,16},{16,0},{32,48},{48,32},{64,80},{80,64},{96,112},{112,96},{1... | collective-permute-start | bytes 1572872 | tf_op jit(solution)/shard_map/ppermute | solution.py:266
  18.7 15.6 %copy-start = (bf16[128,4096]{1,0:T(8,128)(2,1)S(1)}, bf16[128,4096]{1,0:T(8,128)(2,1)}, u32[]{:S(2)}) copy-start(bf16[128,4096]{1,0:T(8,128)(2,1)} %q_here_ref.1) | copy-start | bytes 3145732
  18.7 15.6 %copy-start.4 = (s32[130]{0:T(256)S(1)}, s32[130]{0:T(256)}, u32[]{:S(2)}) copy-start(s32[130]{0:T(256)} %param.9) | copy-start | bytes 1564
  19.6 14.6 %all-to-all-start = ((bf16[8,128,256]{2,1,0:T(8,128)(2,1)}), bf16[8,128,256]{2,1,0:T(8,128)(2,1)S(1)}, u32[]{:S(2)}, u32[]{:S(2)}) async-start(bf16[8,128,256]{2,1,0:T(8,128)(2,1)} %bitcast_select_fusion), calls=%async_computation | async-start | bytes 1048576 | tf_op jit(solution)/shard_map/all_to_all | solution.py:256
  23.9 3.3 %collective-permute-start.3 = (bf16[128,256]{1,0:T(8,128)(2,1)S(1)}, bf16[128,256]{1,0:T(8,128)(2,1)S(1)}, u32[]{:S(2)}, u32[]{:S(2)}) collective-permute-start(bf16[128,256]{1,0:T(8,128)(2,1)S(1)} %get-tuple-element.19), channel_id=1, source_target_pairs={{0,16},{16,0},{32,48},{48,32},{64,80},{80,64},{96,112},{112,96},{1... | collective-permute-start | bytes 196616 | tf_op jit(solution)/shard_map/ppermute | solution.py:266
  27.2 0.8 %copy-start.2 = (bf16[128,2048]{1,0:T(8,128)(2,1)}, bf16[128,2048]{1,0:T(8,128)(2,1)S(1)}, u32[]{:S(2)}) copy-start(bf16[128,2048]{1,0:T(8,128)(2,1)S(1)} %collective-permute-done.1.do_there_ref) | copy-start | bytes 1572868
  34.3 1.2 %copy-start.1 = (bf16[128,4096]{1,0:T(8,128)(2,1)S(1)}, bf16[128,4096]{1,0:T(8,128)(2,1)}, u32[]{:S(2)}) copy-start(bf16[128,4096]{1,0:T(8,128)(2,1)} %do_here_ref.1) | copy-start | bytes 3145732
  35.5 1.0 %copy-start.3 = (bf16[128,2048]{1,0:T(8,128)(2,1)S(1)}, bf16[128,2048]{1,0:T(8,128)(2,1)}, u32[]{:S(2)}) copy-start(bf16[128,2048]{1,0:T(8,128)(2,1)} %copy-done.2) | copy-start | bytes 1572868
  46.4 23.4 %collective-permute-start.4 = (bf16[128,4352]{1,0:T(8,128)(2,1)}, bf16[128,4352]{1,0:T(8,128)(2,1)}, u32[]{:S(2)}, u32[]{:S(2)}) collective-permute-start(bf16[128,4352]{1,0:T(8,128)(2,1)} %get-tuple-element.22), channel_id=1, source_target_pairs={{0,16},{16,0},{32,48},{48,32},{64,80},{80,64},{96,112},{112,96},{1... | collective-permute-start | bytes 3342344 | tf_op jit(solution)/shard_map/ppermute | solution.py:266
  48.3 19.3 %all-to-all-start.1 = ((bf16[8,128,256]{2,1,0:T(8,128)(2,1)}), bf16[8,128,256]{2,1,0:T(8,128)(2,1)S(1)}, u32[]{:S(2)}, u32[]{:S(2)}) async-start(bf16[8,128,256]{2,1,0:T(8,128)(2,1)} %get-tuple-element.20), calls=%async_computation.1 | async-start | bytes 1048576 | tf_op jit(solution)/shard_map/all_to_all | solution.py:256
  67.7 10.7 %collective-permute-start.5 = (bf16[128,512]{1,0:T(8,128)(2,1)S(1)}, bf16[128,512]{1,0:T(8,128)(2,1)S(1)}, u32[]{:S(2)}, u32[]{:S(2)}) collective-permute-start(bf16[128,512]{1,0:T(8,128)(2,1)S(1)} %pad_maximum_fusion.2), channel_id=1, source_target_pairs={{128,0},{144,16},{160,32},{176,48},{192,64},{208,80},{224,96},{240... | collective-permute-start | bytes 393224 | tf_op jit(solution)/shard_map/ppermute | solution.py:250

commit v4 on v3

--- a/solution.py
+++ b/solution.py
@@ -128,33 +128,48 @@
     def attend(tiles):
         width = 2 * tiles * TOK
         heads = half // HEAD
-        q, do = stacked(q_side.at[side]), stacked(do_side.at[side])
-        k, v = k_fill[KEYS - width :], v_zero[KEYS - width :]
         hidden = 2 * tiles - 1 - before
         row = lax.broadcasted_iota(jnp.int32, (TOK, TOK), 0)
         col = lax.broadcasted_iota(jnp.int32, (TOK, TOK), 1)
         causal = jnp.where(col <= row, 0.0, -1e30).astype(F32)
-        s = dot(q, k, 1, 1)
-        s = jnp.concatenate(
-            [s[:, : width - TOK], s[:, width - TOK :] + jnp.concatenate([causal] * heads, 0)], 1
-        )
-        top = jnp.max(s, axis=1, keepdims=True)
-        p = jnp.exp2(s * SCALE2 - top * SCALE2)
-        p_low = p.astype(BF16)
-        wide = p[:, :TOK]
-        for w in range(1, 2 * tiles):
-            wide = wide + p[:, w * TOK : (w + 1) * TOK]
-        total = jnp.sum(wide - hidden.astype(F32) * p[:, :TOK], axis=1, keepdims=True)
-        inv = 1.0 / total
-        o = (dot(p_low, v, 1, 0) * inv).astype(BF16)
-        do_wide = do.astype(F32)
-        delta = jnp.sum(do_wide * o.astype(F32), axis=1, keepdims=True) * inv
-        do_norm = (do_wide * inv).astype(BF16)
-        ds = p_low * (dot(do_norm, v, 1, 1) - delta).astype(BF16)
-        dq = (dot(ds, k_zero[KEYS - width :], 1, 0) * SCALE).astype(BF16)
-        for r in range(heads):
-            o_now[:, r * HEAD : (r + 1) * HEAD] = o[r * TOK : (r + 1) * TOK]
-            dq_now[:, r * HEAD : (r + 1) * HEAD] = dq[r * TOK : (r + 1) * TOK]
+        k, kz, v = k_fill[KEYS - width :], k_zero[KEYS - width :], v_zero[KEYS - width :]
+        group_size = 8
+        groups = range(0, heads, group_size)
+
+        def part(ref, g):
+            at = ref.at[side]
+            return jnp.concatenate([at[:, (g + r) * HEAD : (g + r + 1) * HEAD] for r in range(group_size)], 0)
+
+        qs = [part(q_side, g) for g in groups]
+        scores = [dot(q, k, 1, 1) for q in qs]
+        dss, ps, norms = [], [], []
+        for g, s in zip(groups, scores):
+            do = part(do_side, g)
+            s = jnp.concatenate(
+                [s[:, : width - TOK], s[:, width - TOK :] + jnp.concatenate([causal] * group_size, 0)], 1
+            )
+            top = jnp.max(s, axis=1, keepdims=True)
+            p = jnp.exp2(s * SCALE2 - top * SCALE2)
+            p_low = p.astype(BF16)
+            wide = p[:, :TOK]
+            for w in range(1, 2 * tiles):
+                wide = wide + p[:, w * TOK : (w + 1) * TOK]
+            total = jnp.sum(wide - hidden.astype(F32) * p[:, :TOK], axis=1, keepdims=True)
+            inv = 1.0 / total
+            o = (dot(p_low, v, 1, 0) * inv).astype(BF16)
+            do_wide = do.astype(F32)
+            delta = jnp.sum(do_wide * o.astype(F32), axis=1, keepdims=True) * inv
+            do_norm = (do_wide * inv).astype(BF16)
+            ds = p_low * (dot(do_norm, v, 1, 1) - delta).astype(BF16)
+            dq = (dot(ds, kz, 1, 0) * SCALE).astype(BF16)
+            for r in range(group_size):
+                at = slice((g + r) * HEAD, (g + r + 1) * HEAD)
+                o_now[:, at] = o[r * TOK : (r + 1) * TOK]
+                dq_now[:, at] = dq[r * TOK : (r + 1) * TOK]
+            dss.append(ds)
+            ps.append(p_low)
+            norms.append(do_norm)
+        ds, p_low, do_norm, q = [jnp.concatenate(x, 0) for x in (dss, ps, norms, qs)]
         place = lax.broadcasted_iota(jnp.int32, (HEAD, width), 1)
         shown = place >= hidden * TOK
         window = pl.ds(pl.multiple_of(index * TOK + KEYS - width, TOK), width)
@@ -196,7 +211,7 @@
     own = own_here.shape
     there = (TOK, 2 * half[1] + own[1])
     vmem = pl.BlockSpec(memory_space=pltpu.VMEM)
-    anywhere = pl.BlockSpec(memory_space=pl.ANY)
+    anywhere = pl.BlockSpec(memory_space=pltpu.HBM)
     return pl.pallas_call(
         attention_kernel,
         grid_spec=pltpu.PrefetchScalarGridSpec(
@@ -237,6 +252,29 @@
     )(where, offsets, queries, cotangent, q_there, do_there, seen, own_here, own_there)
 
 
+def theirs_kernel(where_ref, terms_ref, out_ref):
+    chip = where_ref[1]
+    for group in range(2):
+        total = terms_ref[group].astype(F32)
+        for j in range(1, RING // 2):
+            total += jnp.where(j > chip, 0.0, terms_ref[2 * j + group].astype(F32))
+        k_at, v_at = group * HEAD, (2 + group) * HEAD
+        out_ref[:, k_at : k_at + HEAD] = total[:, :HEAD].astype(BF16)
+        out_ref[:, v_at : v_at + HEAD] = total[:, HEAD:].astype(BF16)
+
+
+def theirs_sum(where, terms):
+    vmem = pl.BlockSpec(memory_space=pltpu.VMEM)
+    return pl.pallas_call(
+        theirs_kernel,
+        grid_spec=pltpu.PrefetchScalarGridSpec(
+            num_scalar_prefetch=1, grid=(1,), in_specs=[vmem], out_specs=vmem
+        ),
+        out_shape=jax.ShapeDtypeStruct((TOK, 4 * HEAD), BF16),
+        cost_estimate=pl.CostEstimate(flops=40_000_000_000, bytes_accessed=terms.size * 2, transcendentals=0),
+    )(where, terms)
+
+
 def ring_shift(block, rings):
     lanes, regions = lax.axis_size("uly"), lax.axis_size("blk")
     tokens = lanes * regions
@@ -294,18 +332,17 @@
         where, offsets, queries, cotangent, q_there, do_there, seen, heads_of(kv, core), own_there
     )
 
-    terms = within_ring(terms).reshape(RING // 2, 2, TOK, 2 * HEAD)
-
-    def picked(after):
-        return sum(
-            jnp.where((j > chip) == after, terms[j], jnp.zeros_like(terms[j])).astype(F32)
-            for j in range(RING // 2)
-        )
+    terms = within_ring(terms)
+    shifted = ring_shift(theirs_sum(where, terms), -1)
+    terms = terms.reshape(RING // 2, 2, TOK, 2 * HEAD)
 
     def side_by_side(a):
         return jnp.concatenate([a[0, :, :HEAD], a[1, :, :HEAD], a[0, :, HEAD:], a[1, :, HEAD:]], 1)
 
-    shifted = ring_shift(side_by_side(picked(False).astype(BF16)), -1)
+    after = sum(
+        jnp.where(j > chip, terms[j], jnp.zeros_like(terms[j])).astype(F32)
+        for j in range(1, RING // 2)
+    )
     back = to_sibling(there)
     half = o_here.shape[1]
 
@@ -318,7 +355,7 @@
         jnp.stack([mine_here, back[:, 2 * half :]]),
         jnp.stack([back[:, 2 * half :], mine_here]),
     )
-    ours = side_by_side(picked(True) + local.astype(F32))
+    ours = side_by_side(after + local.astype(F32))
     ours, attended, grad_q = lax.optimization_barrier((ours, attended, grad_q))
     total = (ours + shifted.astype(F32)).astype(BF16)
     return attended, grad_q, total[:, : 2 * HEAD], total[:, 2 * HEAD :]

time: 80.2 us -> 82.5 us (1.029)
  the two profiles are of different devices: /device:TPU:56 before, /device:TPU:8 now
where the time goes in v4:
time: 82.5 us; the launch traced here: 81.8 us
  starting transfers between devices  24.8 us (30%)
  waiting for transfers between devices  23 us (28%)
  Pallas kernels  18.7 us (23%)
  local copies, waits for them, and re-layouts  10.9 us (13%)
  other arithmetic  3.6 us (4%)
  between operations  0.85 us (1%)
    pallas_call x1, Pallas kernels, attention(): pl.pallas_call(attention_kernel, grid_spec=pltpu.PrefetchScalarGridSpec(n...  16.2 us
    all_to_all x2, waiting for transfers between devices, within_ring(): lax.all_to_all(blocks, 'uly', 0, 0, axis_index_groups=groups, tiled=True)  14.2 us
    ppermute x4, starting transfers between devices, to_sibling(): return lax.ppermute(block, 'uly', [(i, i ^ 1) for i in range(lanes)])  9 us
    ppermute x2, starting transfers between devices, ring_shift(): return lax.ppermute(block, ('uly', 'blk'), route)  8 us
    ppermute x2, waiting for transfers between devices, ring_shift(): return lax.ppermute(block, ('uly', 'blk'), route)  7.86 us
    all_to_all x2, starting transfers between devices, within_ring(): lax.all_to_all(blocks, 'uly', 0, 0, axis_index_groups=groups, tiled=True)  7.79 us
    unnamed x18, local copies, waits for them, and re-layouts  4.89 us
    pallas_call x1, Pallas kernels, theirs_sum(): pl.pallas_call(theirs_kernel, grid_spec=pltpu.PrefetchScalarGridSpec(num_...  2.45 us
  transfers between devices with their start and end apart: 8, of which 5 were waited for; matrix products, arithmetic and copies ran while one was open for 10% of the time, Pallas kernels for 3%

profile of v4, /device:TPU:8, one launch (start us, length us, event | category | flops | bytes accessed | tf_op | source)
XLA Modules:
  0.0 81.8 jit_solution(8031725363803725202)
XLA Ops:
  1.5 6.1 %collective-permute-start.2 = (bf16[128,512]{1,0:T(8,128)(2,1)S(1)}, bf16[128,512]{1,0:T(8,128)(2,1)S(1)}, u32[]{:S(2)}, u32[]{:S(2)}) collective-permute-start(bf16[128,512]{1,0:T(8,128)(2,1)S(1)} %pad_maximum_fusion.1), channel_id=1, source_target_pairs={{0,128},{16,144},{32,160},{48,176},{64,192},{80,208},{96,224},{112... | collective-permute-start | bytes 393224 | tf_op jit(solution)/shard_map/ppermute | solution.py:288
  7.6 2.3 %constant_dynamic-slice_fusion.2 = (bf16[128,2048]{1,0:T(8,128)(2,1)}, bf16[128,2048]{1,0:T(8,128)(2,1)}) fusion(bf16[128,4096]{1,0:T(8,128)(2,1)} %do_here_ref.1, s32[]{:T(128)S(6)} %select_n.62, bf16[128,4096]{1,0:T(8,128)(2,1)} %q_here_ref.1), kind=kLoop, calls=%fused_computation.22 | loop fusion | bytes 2097156 | tf_op jit(solution)/shard_map/dynamic_slice | solution.py:316
  10.0 1.9 %collective-permute-start = (bf16[128,2048]{1,0:T(8,128)(2,1)}, bf16[128,2048]{1,0:T(8,128)(2,1)S(1)}, u32[]{:S(2)}, u32[]{:S(2)}) collective-permute-start(bf16[128,2048]{1,0:T(8,128)(2,1)} %get-tuple-element.17), channel_id=1, source_target_pairs={{0,16},{16,0},{32,48},{48,32},{64,80},{80,64},{96,112},{112,96},{1... | collective-permute-start | bytes 1572872 | tf_op jit(solution)/shard_map/ppermute | solution.py:304
  11.9 2.4 %collective-permute-start.1 = (bf16[128,2048]{1,0:T(8,128)(2,1)}, bf16[128,2048]{1,0:T(8,128)(2,1)S(1)}, u32[]{:S(2)}, u32[]{:S(2)}) collective-permute-start(bf16[128,2048]{1,0:T(8,128)(2,1)} %get-tuple-element.18), channel_id=1, source_target_pairs={{0,16},{16,0},{32,48},{48,32},{64,80},{80,64},{96,112},{112,96},{1... | collective-permute-start | bytes 1572872 | tf_op jit(solution)/shard_map/ppermute | solution.py:304
  14.4 3.8 %collective-permute-done.2 = bf16[128,512]{1,0:T(8,128)(2,1)S(1)} collective-permute-done((bf16[128,512]{1,0:T(8,128)(2,1)S(1)}, bf16[128,512]{1,0:T(8,128)(2,1)S(1)}, u32[]{:S(2)}, u32[]{:S(2)}) %collective-permute-start.2) | collective-permute-done | bytes 131104 | tf_op jit(solution)/shard_map/ppermute | solution.py:288
  18.2 0.9 %bitcast_select_fusion = bf16[8,128,256]{2,1,0:T(8,128)(2,1)} fusion(pred[8]{0:T(512)(128)(4,1)S(1)} %fusion, bf16[2,128,256]{2,1,0:T(8,128)(2,1)S(1)} %copy.10, bf16[2,128,256]{2,1,0:T(8,128)(2,1)S(1)} %copy.9), kind=kLoop, calls=%fused_computation.2 | loop fusion | flops 262144 | bytes 786440 | tf_op jit(solution)/shard_map/jit(_where)/select_n | solution.py:325
  19.1 4.3 %all-to-all-start = ((bf16[8,128,256]{2,1,0:T(8,128)(2,1)}), bf16[8,128,256]{2,1,0:T(8,128)(2,1)S(1)}, u32[]{:S(2)}, u32[]{:S(2)}) async-start(bf16[8,128,256]{2,1,0:T(8,128)(2,1)} %bitcast_select_fusion), calls=%async_computation | async-start | bytes 1048576 | tf_op jit(solution)/shard_map/all_to_all | solution.py:294
  23.4 2.4 %collective-permute-start.3 = (bf16[128,256]{1,0:T(8,128)(2,1)S(1)}, bf16[128,256]{1,0:T(8,128)(2,1)S(1)}, u32[]{:S(2)}, u32[]{:S(2)}) collective-permute-start(bf16[128,256]{1,0:T(8,128)(2,1)S(1)} %get-tuple-element.19), channel_id=1, source_target_pairs={{0,16},{16,0},{32,48},{48,32},{64,80},{80,64},{96,112},{112,96},{1... | collective-permute-start | bytes 196616 | tf_op jit(solution)/shard_map/ppermute | solution.py:304
  25.9 0.9 %collective-permute-done.3.own_there_ref = bf16[128,256]{1,0:T(8,128)(2,1)S(1)} collective-permute-done((bf16[128,256]{1,0:T(8,128)(2,1)S(1)}, bf16[128,256]{1,0:T(8,128)(2,1)S(1)}, u32[]{:S(2)}, u32[]{:S(2)}) %collective-permute-start.3) | collective-permute-done | bytes 65568 | tf_op jit(solution)/shard_map/ppermute | solution.py:304
  27.5 6.3 %all-to-all-done.seen_ref = bf16[8,128,256]{2,1,0:T(8,128)(2,1)S(1)} async-done(((bf16[8,128,256]{2,1,0:T(8,128)(2,1)}), bf16[8,128,256]{2,1,0:T(8,128)(2,1)S(1)}, u32[]{:S(2)}, u32[]{:S(2)}) %all-to-all-start) | async-done | bytes 524320 | tf_op jit(solution)/shard_map/all_to_all | solution.py:294
  33.8 1.2 %copy-done.1 = bf16[128,4096]{1,0:T(8,128)(2,1)S(1)} copy-done((bf16[128,4096]{1,0:T(8,128)(2,1)S(1)}, bf16[128,4096]{1,0:T(8,128)(2,1)}, u32[]{:S(2)}) %copy-start.1) | copy-done | bytes 1048600
  35.0 1.0 %copy-done.5 = bf16[128,2048]{1,0:T(8,128)(2,1)S(1)} copy-done((bf16[128,2048]{1,0:T(8,128)(2,1)S(1)}, bf16[128,2048]{1,0:T(8,128)(2,1)}, u32[]{:S(2)}) %copy-start.5) | copy-done | bytes 524312
  36.1 16.2 %shard_map.84 = (bf16[128,2048]{1,0:T(8,128)(2,1)S(1)}, bf16[128,2048]{1,0:T(8,128)(2,1)S(1)}, bf16[128,4352]{1,0:T(8,128)(2,1)S(1)}, bf16[8,128,256]{2,1,0:T(8,128)(2,1)}, bf16[128,256]{1,0:T(8,128)(2,1)S(1)}) custom-call(s32[3]{0:T(128)S(1)} %pad_add_fusion.where_ref, s32[1,130]{1,0:T(1,128)S(1)} %bitcast.26, bf16[128,4096]{1,0:T(8,128)(2,1)S(1)} %copy-done, ...), custom_call_target="tpu_custom_call" | custom-call | flops 6442450944 | bytes 4194304 | tf_op jit(solution)/shard_map/pallas_call | solution.py:215
  52.3 1.0 %copy-done.3 = bf16[128,4352]{1,0:T(8,128)(2,1)} copy-done((bf16[128,4352]{1,0:T(8,128)(2,1)}, bf16[128,4352]{1,0:T(8,128)(2,1)S(1)}, u32[]{:S(2)}) %copy-start.3) | copy-done | bytes 1114136
  53.3 3.5 %all-to-all-start.1 = ((bf16[8,128,256]{2,1,0:T(8,128)(2,1)}), bf16[8,128,256]{2,1,0:T(8,128)(2,1)S(1)}, u32[]{:S(2)}, u32[]{:S(2)}) async-start(bf16[8,128,256]{2,1,0:T(8,128)(2,1)} %get-tuple-element.20), calls=%async_computation.1 | async-start | bytes 1048576 | tf_op jit(solution)/shard_map/all_to_all | solution.py:294
  56.8 2.3 %collective-permute-start.4 = (bf16[128,4352]{1,0:T(8,128)(2,1)}, bf16[128,4352]{1,0:T(8,128)(2,1)}, u32[]{:S(2)}, u32[]{:S(2)}) collective-permute-start(bf16[128,4352]{1,0:T(8,128)(2,1)} %copy-done.3), channel_id=1, source_target_pairs={{0,16},{16,0},{32,48},{48,32},{64,80},{80,64},{96,112},{112,96},{1... | collective-permute-start | bytes 3342344 | tf_op jit(solution)/shard_map/ppermute | solution.py:304
  59.1 8.0 %all-to-all-done.1.terms_ref = bf16[8,128,256]{2,1,0:T(8,128)(2,1)S(1)} async-done(((bf16[8,128,256]{2,1,0:T(8,128)(2,1)}), bf16[8,128,256]{2,1,0:T(8,128)(2,1)S(1)}, u32[]{:S(2)}, u32[]{:S(2)}) %all-to-all-start.1) | async-done | bytes 524320 | tf_op jit(solution)/shard_map/all_to_all | solution.py:294
  67.9 2.4 %shard_map.85 = bf16[128,512]{1,0:T(8,128)(2,1)} custom-call(s32[3]{0:T(128)} %copy-done.2, bf16[8,128,256]{2,1,0:T(8,128)(2,1)} %copy-done.7), custom_call_target="tpu_custom_call" | custom-call | flops 40000000000 | bytes 524288 | tf_op jit(solution)/shard_map/pallas_call | solution.py:268
  70.3 1.9 %collective-permute-start.5 = (bf16[128,512]{1,0:T(8,128)(2,1)}, bf16[128,512]{1,0:T(8,128)(2,1)S(1)}, u32[]{:S(2)}, u32[]{:S(2)}) collective-permute-start(bf16[128,512]{1,0:T(8,128)(2,1)} %shard_map.85), channel_id=1, source_target_pairs={{128,0},{144,16},{160,32},{176,48},{192,64},{208,80},{224,96},{240... | collective-permute-start | bytes 393224 | tf_op jit(solution)/shard_map/ppermute | solution.py:288
  72.3 1.3 %fusion.1 = (bf16[128,2048]{1,0:T(8,128)(2,1)S(1)}, bf16[128,2048]{1,0:T(8,128)(2,1)S(1)}) fusion(bf16[128,4352]{1,0:T(8,128)(2,1)} %collective-permute-done.4), kind=kLoop, calls=%fused_computation.26 | loop fusion | bytes 2097152 | tf_op jit(solution)/shard_map/slice | solution.py:352
  73.5 1.2 %maximum_select_fusion = bf16[128,4096]{1,0:T(8,128)(2,1)} fusion(bf16[128,2048]{1,0:T(8,128)(2,1)S(1)} %get-tuple-element.29, bf16[128,2048]{1,0:T(8,128)(2,1)S(1)} %get-tuple-element.23, pred[]{:T(512)S(6)} %eq.2), kind=kLoop, calls=%fused_computation | loop fusion | flops 4718592 | bytes 2097153 | tf_op jit(solution)/shard_map/jit(_where)/select_n | solution.py:350
  74.8 1.2 %maximum_select_fusion.1 = bf16[128,4096]{1,0:T(8,128)(2,1)} fusion(bf16[128,2048]{1,0:T(8,128)(2,1)S(1)} %get-tuple-element.28, bf16[128,2048]{1,0:T(8,128)(2,1)S(1)} %get-tuple-element.24, pred[]{:T(512)S(6)} %eq.2), kind=kLoop, calls=%fused_computation.1 | loop fusion | flops 4718592 | bytes 2097153 | tf_op jit(solution)/shard_map/jit(_where)/select_n | solution.py:350
  76.0 0.8 %slice_bitcast_fusion.4 = bf16[1,128,256]{2,1,0:T(8,128)(2,1)S(1)} fusion(bf16[128,4352]{1,0:T(8,128)(2,1)} %collective-permute-done.4), kind=kLoop, calls=%fused_computation.15 | loop fusion | bytes 131072 | tf_op jit(solution)/shard_map/stack | solution.py:355
  77.0 4.1 %collective-permute-done.5 = bf16[128,512]{1,0:T(8,128)(2,1)S(1)} collective-permute-done((bf16[128,512]{1,0:T(8,128)(2,1)}, bf16[128,512]{1,0:T(8,128)(2,1)S(1)}, u32[]{:S(2)}, u32[]{:S(2)}) %collective-permute-start.5) | collective-permute-done | bytes 131104 | tf_op jit(solution)/shard_map/ppermute | solution.py:288
  (32 shorter events, 3.5 us)
Async XLA Ops:
  1.5 16.7 %collective-permute-start.2 = (bf16[128,512]{1,0:T(8,128)(2,1)S(1)}, bf16[128,512]{1,0:T(8,128)(2,1)S(1)}, u32[]{:S(2)}, u32[]{:S(2)}) collective-permute-start(bf16[128,512]{1,0:T(8,128)(2,1)S(1)} %pad_maximum_fusion.1), channel_id=1, source_target_pairs={{0,128},{16,144},{32,160},{48,176},{64,192},{80,208},{96,224},{112... | collective-permute-start | bytes 393224 | tf_op jit(solution)/shard_map/ppermute | solution.py:288
  10.0 23.8 %copy-start.2 = (s32[3]{0:T(128)}, s32[3]{0:T(128)S(1)}, u32[]{:S(2)}) copy-start(s32[3]{0:T(128)S(1)} %pad_add_fusion.where_ref) | copy-start | bytes 40
  10.0 16.8 %collective-permute-start = (bf16[128,2048]{1,0:T(8,128)(2,1)}, bf16[128,2048]{1,0:T(8,128)(2,1)S(1)}, u32[]{:S(2)}, u32[]{:S(2)}) collective-permute-start(bf16[128,2048]{1,0:T(8,128)(2,1)} %get-tuple-element.17), channel_id=1, source_target_pairs={{0,16},{16,0},{32,48},{48,32},{64,80},{80,64},{96,112},{112,96},{1... | collective-permute-start | bytes 1572872 | tf_op jit(solution)/shard_map/ppermute | solution.py:304
  11.9 14.8 %collective-permute-start.1 = (bf16[128,2048]{1,0:T(8,128)(2,1)}, bf16[128,2048]{1,0:T(8,128)(2,1)S(1)}, u32[]{:S(2)}, u32[]{:S(2)}) collective-permute-start(bf16[128,2048]{1,0:T(8,128)(2,1)} %get-tuple-element.18), channel_id=1, source_target_pairs={{0,16},{16,0},{32,48},{48,32},{64,80},{80,64},{96,112},{112,96},{1... | collective-permute-start | bytes 1572872 | tf_op jit(solution)/shard_map/ppermute | solution.py:304
  18.2 15.6 %copy-start = (bf16[128,4096]{1,0:T(8,128)(2,1)S(1)}, bf16[128,4096]{1,0:T(8,128)(2,1)}, u32[]{:S(2)}) copy-start(bf16[128,4096]{1,0:T(8,128)(2,1)} %q_here_ref.1) | copy-start | bytes 3145732
  18.2 15.6 %copy-start.6 = (s32[130]{0:T(256)S(1)}, s32[130]{0:T(256)}, u32[]{:S(2)}) copy-start(s32[130]{0:T(256)} %param.9) | copy-start | bytes 1564
  19.1 14.6 %all-to-all-start = ((bf16[8,128,256]{2,1,0:T(8,128)(2,1)}), bf16[8,128,256]{2,1,0:T(8,128)(2,1)S(1)}, u32[]{:S(2)}, u32[]{:S(2)}) async-start(bf16[8,128,256]{2,1,0:T(8,128)(2,1)} %bitcast_select_fusion), calls=%async_computation | async-start | bytes 1048576 | tf_op jit(solution)/shard_map/all_to_all | solution.py:294
  23.4 3.3 %collective-permute-start.3 = (bf16[128,256]{1,0:T(8,128)(2,1)S(1)}, bf16[128,256]{1,0:T(8,128)(2,1)S(1)}, u32[]{:S(2)}, u32[]{:S(2)}) collective-permute-start(bf16[128,256]{1,0:T(8,128)(2,1)S(1)} %get-tuple-element.19), channel_id=1, source_target_pairs={{0,16},{16,0},{32,48},{48,32},{64,80},{80,64},{96,112},{112,96},{1... | collective-permute-start | bytes 196616 | tf_op jit(solution)/shard_map/ppermute | solution.py:304
  26.7 0.8 copy-start.4
  33.8 1.2 %copy-start.1 = (bf16[128,4096]{1,0:T(8,128)(2,1)S(1)}, bf16[128,4096]{1,0:T(8,128)(2,1)}, u32[]{:S(2)}) copy-start(bf16[128,4096]{1,0:T(8,128)(2,1)} %do_here_ref.1) | copy-start | bytes 3145732
  35.0 1.0 %copy-start.5 = (bf16[128,2048]{1,0:T(8,128)(2,1)S(1)}, bf16[128,2048]{1,0:T(8,128)(2,1)}, u32[]{:S(2)}) copy-start(bf16[128,2048]{1,0:T(8,128)(2,1)} %copy-done.4) | copy-start | bytes 1572868
  52.3 1.0 %copy-start.3 = (bf16[128,4352]{1,0:T(8,128)(2,1)}, bf16[128,4352]{1,0:T(8,128)(2,1)S(1)}, u32[]{:S(2)}) copy-start(bf16[128,4352]{1,0:T(8,128)(2,1)S(1)} %get-tuple-element.22) | copy-start | bytes 3342340
  53.3 13.8 %all-to-all-start.1 = ((bf16[8,128,256]{2,1,0:T(8,128)(2,1)}), bf16[8,128,256]{2,1,0:T(8,128)(2,1)S(1)}, u32[]{:S(2)}, u32[]{:S(2)}) async-start(bf16[8,128,256]{2,1,0:T(8,128)(2,1)} %get-tuple-element.20), calls=%async_computation.1 | async-start | bytes 1048576 | tf_op jit(solution)/shard_map/all_to_all | solution.py:294
  56.8 15.4 %collective-permute-start.4 = (bf16[128,4352]{1,0:T(8,128)(2,1)}, bf16[128,4352]{1,0:T(8,128)(2,1)}, u32[]{:S(2)}, u32[]{:S(2)}) collective-permute-start(bf16[128,4352]{1,0:T(8,128)(2,1)} %copy-done.3), channel_id=1, source_target_pairs={{0,16},{16,0},{32,48},{48,32},{64,80},{80,64},{96,112},{112,96},{1... | collective-permute-start | bytes 3342344 | tf_op jit(solution)/shard_map/ppermute | solution.py:304
  67.1 0.8 copy-start.7
  70.3 10.7 %collective-permute-start.5 = (bf16[128,512]{1,0:T(8,128)(2,1)}, bf16[128,512]{1,0:T(8,128)(2,1)S(1)}, u32[]{:S(2)}, u32[]{:S(2)}) collective-permute-start(bf16[128,512]{1,0:T(8,128)(2,1)} %shard_map.85), channel_id=1, source_target_pairs={{128,0},{144,16},{160,32},{176,48},{192,64},{208,80},{224,96},{240... | collective-permute-start | bytes 393224 | tf_op jit(solution)/shard_map/ppermute | solution.py:288
  74.8 2.1 %copy-start.8 = (bf16[8,128,256]{2,1,0:T(8,128)(2,1)S(1)}, bf16[8,128,256]{2,1,0:T(8,128)(2,1)}, u32[]{:S(2)}) copy-start(bf16[8,128,256]{2,1,0:T(8,128)(2,1)} %copy-done.7) | copy-start | bytes 1572868

commit v5 on v4

--- a/solution.py
+++ b/solution.py
@@ -44,13 +44,15 @@
     mine_here_ref,
     q_side,
     do_side,
-    own_now,
-    first_own,
+    seen_now,
+    own_side,
     k_fill,
     k_zero,
     v_zero,
-    o_now,
-    dq_now,
+    o_side,
+    dq_side,
+    terms_now,
+    own_out,
     dk_acc,
     dv_acc,
     sems,
@@ -58,7 +60,7 @@
     core, chip = where_ref[0], where_ref[1]
     side = pl.program_id(0)
     index = lax.rem(core + side, 2)
-    half = o_now.shape[1]
+    half = o_side.shape[2]
     first_token = where_ref[2] + index * TOK
     offsets = offsets_ref[...]
     start = jnp.max(jnp.where(offsets <= first_token, offsets, 0))
@@ -72,6 +74,9 @@
         [
             pltpu.make_async_copy(q_here_ref.at[:, mine], q_side.at[0], sems.at[0]),
             pltpu.make_async_copy(do_here_ref.at[:, mine], do_side.at[0], sems.at[1]),
+            pltpu.make_async_copy(seen_ref, seen_now, sems.at[10]),
+            pltpu.make_async_copy(own_here_ref, own_side.at[0], sems.at[11]),
+            pltpu.make_async_copy(own_there_ref, own_side.at[1], sems.at[12]),
         ],
         [
             pltpu.make_async_copy(q_there_ref, q_side.at[1], sems.at[2]),
@@ -79,33 +84,39 @@
         ],
     ]
 
+    own_cols = pl.ds(2 * half, 2 * HEAD)
+    sends = [
+        [
+            pltpu.make_async_copy(o_side.at[0], o_here_ref, sems.at[4]),
+            pltpu.make_async_copy(dq_side.at[0], dq_here_ref, sems.at[5]),
+        ],
+        [
+            pltpu.make_async_copy(o_side.at[1], there_ref.at[:, pl.ds(0, half)], sems.at[6]),
+            pltpu.make_async_copy(dq_side.at[1], there_ref.at[:, pl.ds(half, half)], sems.at[7]),
+            pltpu.make_async_copy(own_out, there_ref.at[:, own_cols], sems.at[8]),
+        ],
+    ]
+
     @pl.when(side == 0)
     def _():
-        for fetch in fetches[0] + fetches[1]:
+        for fetch in fetches[0][2:] + fetches[0][:2] + fetches[1]:
             fetch.start()
-        own_now[...] = own_here_ref[...]
         dk_acc[...] = jnp.zeros_like(dk_acc)
         dv_acc[...] = jnp.zeros_like(dv_acc)
 
-    @pl.when(side == 1)
-    def _():
-        own_now[...] = own_there_ref[...]
-
-    @pl.when(core == 0)
-    def _():
-        first_own[...] = own_here_ref[...]
-
-    @pl.when(core == 1)
-    def _():
-        first_own[...] = own_there_ref[...]
-
+    @pl.when(side == 0)
+    def _():
+        for fetch in fetches[0][2:]:
+            fetch.wait()
+
+    own_now = own_side.at[side]
     first = jnp.broadcast_to(own_now[0:1, :HEAD], (TOK, HEAD))
     zero = jnp.zeros((TOK, HEAD), BF16)
     for w in range(RING - 1):
         at = slice(w * TOK, (w + 1) * TOK)
-        block = seen_ref[slot(w + index)]
+        block = seen_now[slot(w + index)]
         if w == RING - 2:
-            block = jnp.where(index == 1, first_own[...], block)
+            block = jnp.where(index == 1, own_side[core], block)
         shown = RING - 1 - w <= before
         k_fill[at] = jnp.where(shown, block[:, :HEAD], first)
         k_zero[at] = jnp.where(shown, block[:, :HEAD], zero)
@@ -117,7 +128,7 @@
 
     @pl.when(side == 0)
     def _():
-        for fetch in fetches[0]:
+        for fetch in fetches[0][:2]:
             fetch.wait()
 
     @pl.when(side == 1)
@@ -136,15 +147,15 @@
         group_size = 8
         groups = range(0, heads, group_size)
 
-        def part(ref, g):
+        def rows_of(ref, g):
             at = ref.at[side]
             return jnp.concatenate([at[:, (g + r) * HEAD : (g + r + 1) * HEAD] for r in range(group_size)], 0)
 
-        qs = [part(q_side, g) for g in groups]
+        qs = [rows_of(q_side, g) for g in groups]
         scores = [dot(q, k, 1, 1) for q in qs]
         dss, ps, norms = [], [], []
         for g, s in zip(groups, scores):
-            do = part(do_side, g)
+            do = rows_of(do_side, g)
             s = jnp.concatenate(
                 [s[:, : width - TOK], s[:, width - TOK :] + jnp.concatenate([causal] * group_size, 0)], 1
             )
@@ -164,8 +175,8 @@
             dq = (dot(ds, kz, 1, 0) * SCALE).astype(BF16)
             for r in range(group_size):
                 at = slice((g + r) * HEAD, (g + r + 1) * HEAD)
-                o_now[:, at] = o[r * TOK : (r + 1) * TOK]
-                dq_now[:, at] = dq[r * TOK : (r + 1) * TOK]
+                o_side[side, :, at] = o[r * TOK : (r + 1) * TOK]
+                dq_side[side, :, at] = dq[r * TOK : (r + 1) * TOK]
             dss.append(ds)
             ps.append(p_low)
             norms.append(do_norm)
@@ -181,28 +192,36 @@
 
     @pl.when(side == 0)
     def _():
-        o_here_ref[...] = o_now[...]
-        dq_here_ref[...] = dq_now[...]
+        for send in sends[0]:
+            send.start()
 
     @pl.when(side == 1)
     def _():
-        there_ref[:, :half] = o_now[...]
-        there_ref[:, half : 2 * half] = dq_now[...]
+        for send in sends[1][:2]:
+            send.start()
+
+        def part(m):
+            return pltpu.make_async_copy(terms_now.at[slot(m)], terms_ref.at[slot(m)], sems.at[13 + m])
 
         def block(m):
             cols = slice(m * TOK, (m + 1) * TOK)
             return (dk_acc[:, cols] * SCALE).T.astype(BF16), dv_acc[:, cols].T.astype(BF16)
 
         for m in range(RING - 1):
-            terms_ref[slot(m), :, :HEAD], terms_ref[slot(m), :, HEAD:] = block(m)
-        terms_ref[2 * chip] = jnp.zeros((TOK, 2 * HEAD), BF16)
+            terms_now[slot(m), :, :HEAD], terms_now[slot(m), :, HEAD:] = block(m)
+            part(m).start()
+        terms_now[2 * chip] = jnp.zeros((TOK, 2 * HEAD), BF16)
+        part(RING - 1).start()
         even_k, even_v = block(RING - 1)
         odd_k, odd_v = block(RING)
         swap = core == 1
         mine_here_ref[:, :HEAD] = jnp.where(swap, odd_k, even_k)
         mine_here_ref[:, HEAD:] = jnp.where(swap, odd_v, even_v)
-        there_ref[:, 2 * half : 2 * half + HEAD] = jnp.where(swap, even_k, odd_k)
-        there_ref[:, 2 * half + HEAD :] = jnp.where(swap, even_v, odd_v)
+        own_out[:, :HEAD] = jnp.where(swap, even_k, odd_k)
+        own_out[:, HEAD:] = jnp.where(swap, even_v, odd_v)
+        sends[1][2].start()
+        for send in sends[0] + sends[1] + [part(m) for m in range(RING)]:
+            send.wait()
 
 
 def attention(where, offsets, queries, cotangent, q_there, do_there, seen, own_here, own_there):
@@ -211,27 +230,29 @@
     own = own_here.shape
     there = (TOK, 2 * half[1] + own[1])
     vmem = pl.BlockSpec(memory_space=pltpu.VMEM)
-    anywhere = pl.BlockSpec(memory_space=pltpu.HBM)
+    anywhere = pl.BlockSpec(memory_space=pl.ANY)
     return pl.pallas_call(
         attention_kernel,
         grid_spec=pltpu.PrefetchScalarGridSpec(
             num_scalar_prefetch=1,
             grid=(2,),
-            in_specs=[vmem] + [anywhere] * 4 + [vmem] * 3,
-            out_specs=[vmem] * 5,
+            in_specs=[vmem] + [anywhere] * 7,
+            out_specs=[anywhere] * 4 + [vmem],
             scratch_shapes=[
                 pltpu.VMEM((2, *half), BF16),
                 pltpu.VMEM((2, *half), BF16),
-                pltpu.VMEM(own, BF16),
-                pltpu.VMEM(own, BF16),
+                pltpu.VMEM(seen.shape, BF16),
+                pltpu.VMEM((2, *own), BF16),
                 pltpu.VMEM((KEYS, HEAD), BF16),
                 pltpu.VMEM((KEYS, HEAD), BF16),
                 pltpu.VMEM((KEYS, HEAD), BF16),
-                pltpu.VMEM(half, BF16),
-                pltpu.VMEM(half, BF16),
+                pltpu.VMEM((2, *half), BF16),
+                pltpu.VMEM((2, *half), BF16),
+                pltpu.VMEM(seen.shape, BF16),
+                pltpu.VMEM(own, BF16),
                 pltpu.VMEM((HEAD, SPAN), F32),
                 pltpu.VMEM((HEAD, SPAN), F32),
-                pltpu.SemaphoreType.DMA((4,)),
+                pltpu.SemaphoreType.DMA((13 + RING,)),
             ],
         ),
         out_shape=[
@@ -242,7 +263,7 @@
             jax.ShapeDtypeStruct(own, BF16),
         ],
         compiler_params=pltpu.CompilerParams(
-            vmem_limit_bytes=44 << 20, dimension_semantics=("arbitrary",)
+            vmem_limit_bytes=60 << 20, dimension_semantics=("arbitrary",)
         ),
         cost_estimate=pl.CostEstimate(
             flops=24 * rows * KEYS * HEAD,
@@ -271,6 +292,7 @@
             num_scalar_prefetch=1, grid=(1,), in_specs=[vmem], out_specs=vmem
         ),
         out_shape=jax.ShapeDtypeStruct((TOK, 4 * HEAD), BF16),
+        compiler_params=pltpu.CompilerParams(vmem_limit_bytes=6 << 20),
         cost_estimate=pl.CostEstimate(flops=40_000_000_000, bytes_accessed=terms.size * 2, transcendentals=0),
     )(where, terms)
 

time: 82.5 us -> 79 us (0.958)
  the two profiles are of different devices: /device:TPU:8 before, /device:TPU:40 now
where the time goes in v5:
time: 79 us; the launch traced here: 78.4 us
  waiting for transfers between devices  26 us (33%)
  starting transfers between devices  24.9 us (32%)
  Pallas kernels  17.9 us (23%)
  local copies, waits for them, and re-layouts  4.47 us (6%)
  other arithmetic  4.2 us (5%)
  between operations  0.87 us (1%)
    pallas_call x1, Pallas kernels, attention(): pl.pallas_call(attention_kernel, grid_spec=pltpu.PrefetchScalarGridSpec(n...  17.3 us
    all_to_all x2, waiting for transfers between devices, within_ring(): lax.all_to_all(blocks, 'uly', 0, 0, axis_index_groups=groups, tiled=True)  15 us
    ppermute x2, waiting for transfers between devices, ring_shift(): return lax.ppermute(block, ('uly', 'blk'), route)  10.1 us
    ppermute x4, starting transfers between devices, to_sibling(): return lax.ppermute(block, 'uly', [(i, i ^ 1) for i in range(lanes)])  9 us
    ppermute x2, starting transfers between devices, ring_shift(): return lax.ppermute(block, ('uly', 'blk'), route)  8.14 us
    all_to_all x2, starting transfers between devices, within_ring(): lax.all_to_all(blocks, 'uly', 0, 0, axis_index_groups=groups, tiled=True)  7.8 us
    select_n x2, other arithmetic, joined(): jnp.where(core == 0, jnp.concatenate([a, b], 1), jnp.concatenate([b, a], 1))  2.43 us
    dynamic_slice x2, local copies, waits for them, and re-layouts, heads_of(): return lax.dynamic_slice_in_dim(block, group * width, width, 1)  1.91 us
  transfers between devices with their start and end apart: 8, of which 5 were waited for; matrix products, arithmetic and copies ran while one was open for 8% of the time, Pallas kernels for 1%

profile of v5, /device:TPU:40, one launch (start us, length us, event | category | flops | bytes accessed | tf_op | source)
XLA Modules:
  0.0 78.4 jit_solution(11423661947844132957)
XLA Ops:
  0.6 0.8 %fusion.3 = (bf16[128,128]{1,0:T(8,128)(2,1)S(1)}, bf16[128,128]{1,0:T(8,128)(2,1)S(1)}, bf16[128,128]{1,0:T(8,128)(2,1)S(1)}, bf16[128,128]{1,0:T(8,128)(2,1)S(1)}) fusion(bf16[128,256]{1,0:T(8,128)(2,1)} %param.6, bf16[128,256]{1,0:T(8,128)(2,1)} %param.7), kind=kLoop, calls=%fused_computation.28 | loop fusion | bytes 262144 | tf_op jit(solution)/shard_map/slice | solution.py:345
  1.5 6.1 %collective-permute-start.2 = (bf16[128,512]{1,0:T(8,128)(2,1)S(1)}, bf16[128,512]{1,0:T(8,128)(2,1)S(1)}, u32[]{:S(2)}, u32[]{:S(2)}) collective-permute-start(bf16[128,512]{1,0:T(8,128)(2,1)S(1)} %pad_maximum_fusion.1), channel_id=1, source_target_pairs={{0,128},{16,144},{32,160},{48,176},{64,192},{80,208},{96,224},{112... | collective-permute-start | bytes 393224 | tf_op jit(solution)/shard_map/ppermute | solution.py:310
  7.6 0.6 constant_dynamic-slice_fusion
  8.2 1.3 %constant_dynamic-slice_fusion.2 = (bf16[128,2048]{1,0:T(8,128)(2,1)S(1)}, bf16[128,2048]{1,0:T(8,128)(2,1)S(1)}) fusion(bf16[128,4096]{1,0:T(8,128)(2,1)} %do_here_ref.1, s32[]{:T(128)S(6)} %select_n.62, bf16[128,4096]{1,0:T(8,128)(2,1)} %q_here_ref.1), kind=kLoop, calls=%fused_computation.22 | loop fusion | bytes 2097156 | tf_op jit(solution)/shard_map/dynamic_slice | solution.py:338
  9.5 0.7 pad_add_fusion.where_ref
  10.2 1.9 %collective-permute-start = (bf16[128,2048]{1,0:T(8,128)(2,1)S(1)}, bf16[128,2048]{1,0:T(8,128)(2,1)S(1)}, u32[]{:S(2)}, u32[]{:S(2)}) collective-permute-start(bf16[128,2048]{1,0:T(8,128)(2,1)S(1)} %get-tuple-element.17), channel_id=1, source_target_pairs={{0,16},{16,0},{32,48},{48,32},{64,80},{80,64},{96,112},{112,96},{1... | collective-permute-start | bytes 1572872 | tf_op jit(solution)/shard_map/ppermute | solution.py:326
  12.1 2.4 %collective-permute-start.1 = (bf16[128,2048]{1,0:T(8,128)(2,1)S(1)}, bf16[128,2048]{1,0:T(8,128)(2,1)S(1)}, u32[]{:S(2)}, u32[]{:S(2)}) collective-permute-start(bf16[128,2048]{1,0:T(8,128)(2,1)S(1)} %get-tuple-element.18), channel_id=1, source_target_pairs={{0,16},{16,0},{32,48},{48,32},{64,80},{80,64},{96,112},{112,96},{1... | collective-permute-start | bytes 1572872 | tf_op jit(solution)/shard_map/ppermute | solution.py:326
  14.6 4.1 %collective-permute-done.2 = bf16[128,512]{1,0:T(8,128)(2,1)S(1)} collective-permute-done((bf16[128,512]{1,0:T(8,128)(2,1)S(1)}, bf16[128,512]{1,0:T(8,128)(2,1)S(1)}, u32[]{:S(2)}, u32[]{:S(2)}) %collective-permute-start.2) | collective-permute-done | bytes 131104 | tf_op jit(solution)/shard_map/ppermute | solution.py:310
  18.7 0.9 %bitcast_select_fusion = bf16[8,128,256]{2,1,0:T(8,128)(2,1)} fusion(pred[8]{0:T(512)(128)(4,1)S(1)} %fusion, bf16[2,128,256]{2,1,0:T(8,128)(2,1)S(1)} %copy.10, bf16[2,128,256]{2,1,0:T(8,128)(2,1)S(1)} %copy.9), kind=kLoop, calls=%fused_computation.2 | loop fusion | flops 262144 | bytes 786440 | tf_op jit(solution)/shard_map/jit(_where)/select_n | solution.py:347
  19.6 4.3 %all-to-all-start = ((bf16[8,128,256]{2,1,0:T(8,128)(2,1)}), bf16[8,128,256]{2,1,0:T(8,128)(2,1)S(1)}, u32[]{:S(2)}, u32[]{:S(2)}) async-start(bf16[8,128,256]{2,1,0:T(8,128)(2,1)} %bitcast_select_fusion), calls=%async_computation | async-start | bytes 1048576 | tf_op jit(solution)/shard_map/all_to_all | solution.py:316
  23.9 2.4 %collective-permute-start.3 = (bf16[128,256]{1,0:T(8,128)(2,1)S(1)}, bf16[128,256]{1,0:T(8,128)(2,1)S(1)}, u32[]{:S(2)}, u32[]{:S(2)}) collective-permute-start(bf16[128,256]{1,0:T(8,128)(2,1)S(1)} %get-tuple-element.19), channel_id=1, source_target_pairs={{0,16},{16,0},{32,48},{48,32},{64,80},{80,64},{96,112},{112,96},{1... | collective-permute-start | bytes 196616 | tf_op jit(solution)/shard_map/ppermute | solution.py:326
  26.3 0.9 %collective-permute-done.3.own_there_ref = bf16[128,256]{1,0:T(8,128)(2,1)S(1)} collective-permute-done((bf16[128,256]{1,0:T(8,128)(2,1)S(1)}, bf16[128,256]{1,0:T(8,128)(2,1)S(1)}, u32[]{:S(2)}, u32[]{:S(2)}) %collective-permute-start.3) | collective-permute-done | bytes 65568 | tf_op jit(solution)/shard_map/ppermute | solution.py:326
  27.2 7.0 %all-to-all-done.seen_ref = bf16[8,128,256]{2,1,0:T(8,128)(2,1)S(1)} async-done(((bf16[8,128,256]{2,1,0:T(8,128)(2,1)}), bf16[8,128,256]{2,1,0:T(8,128)(2,1)S(1)}, u32[]{:S(2)}, u32[]{:S(2)}) %all-to-all-start) | async-done | bytes 524320 | tf_op jit(solution)/shard_map/all_to_all | solution.py:316
  34.3 0.8 %copy-done.3 = bf16[8,128,256]{2,1,0:T(8,128)(2,1)} copy-done((bf16[8,128,256]{2,1,0:T(8,128)(2,1)}, bf16[8,128,256]{2,1,0:T(8,128)(2,1)S(1)}, u32[]{:S(2)}) %copy-start.3) | copy-done | bytes 524312
  35.1 17.3 %shard_map.84 = (bf16[128,2048]{1,0:T(8,128)(2,1)}, bf16[128,2048]{1,0:T(8,128)(2,1)}, bf16[128,4352]{1,0:T(8,128)(2,1)}, bf16[8,128,256]{2,1,0:T(8,128)(2,1)}, bf16[128,256]{1,0:T(8,128)(2,1)}) custom-call(s32[3]{0:T(128)} %pad_add_fusion.where_ref, s32[1,130]{1,0:T(1,128)} %bitcast.28, bf16[128,4096]{1,0:T(8,128)(2,1)} %q_here_ref.1, ...), custom_call_target="tpu_custom_call" | custom-call | flops 6442450944 | bytes 4194304 | tf_op jit(solution)/shard_map/pallas_call | solution.py:234
  52.4 3.5 %all-to-all-start.1 = ((bf16[8,128,256]{2,1,0:T(8,128)(2,1)}), bf16[8,128,256]{2,1,0:T(8,128)(2,1)S(1)}, u32[]{:S(2)}, u32[]{:S(2)}) async-start(bf16[8,128,256]{2,1,0:T(8,128)(2,1)} %get-tuple-element.20), calls=%async_computation.1 | async-start | bytes 1048576 | tf_op jit(solution)/shard_map/all_to_all | solution.py:316
  55.9 2.3 %collective-permute-start.4 = (bf16[128,4352]{1,0:T(8,128)(2,1)}, bf16[128,4352]{1,0:T(8,128)(2,1)S(1)}, u32[]{:S(2)}, u32[]{:S(2)}) collective-permute-start(bf16[128,4352]{1,0:T(8,128)(2,1)} %get-tuple-element.22), channel_id=1, source_target_pairs={{0,16},{16,0},{32,48},{48,32},{64,80},{80,64},{96,112},{112,96},{1... | collective-permute-start | bytes 3342344 | tf_op jit(solution)/shard_map/ppermute | solution.py:326
  58.2 8.0 %all-to-all-done.1.terms_ref = bf16[8,128,256]{2,1,0:T(8,128)(2,1)S(1)} async-done(((bf16[8,128,256]{2,1,0:T(8,128)(2,1)}), bf16[8,128,256]{2,1,0:T(8,128)(2,1)S(1)}, u32[]{:S(2)}, u32[]{:S(2)}) %all-to-all-start.1) | async-done | bytes 524320 | tf_op jit(solution)/shard_map/all_to_all | solution.py:316
  66.2 0.6 shard_map.85
  66.8 2.1 %collective-permute-start.5 = (bf16[128,512]{1,0:T(8,128)(2,1)S(1)}, bf16[128,512]{1,0:T(8,128)(2,1)S(1)}, u32[]{:S(2)}, u32[]{:S(2)}) collective-permute-start(bf16[128,512]{1,0:T(8,128)(2,1)S(1)} %shard_map.85), channel_id=1, source_target_pairs={{128,0},{144,16},{160,32},{176,48},{192,64},{208,80},{224,96},{240... | collective-permute-start | bytes 393224 | tf_op jit(solution)/shard_map/ppermute | solution.py:310
  69.0 1.2 %maximum_select_fusion = bf16[128,4096]{1,0:T(8,128)(2,1)} fusion(bf16[128,2048]{1,0:T(8,128)(2,1)S(1)} %get-tuple-element.29, bf16[128,2048]{1,0:T(8,128)(2,1)S(1)} %copy-done.2, pred[]{:T(512)S(6)} %eq.2), kind=kLoop, calls=%fused_computation | loop fusion | flops 4718592 | bytes 2097153 | tf_op jit(solution)/shard_map/jit(_where)/select_n | solution.py:372
  70.3 1.2 %maximum_select_fusion.1 = bf16[128,4096]{1,0:T(8,128)(2,1)} fusion(bf16[128,2048]{1,0:T(8,128)(2,1)S(1)} %get-tuple-element.28, bf16[128,2048]{1,0:T(8,128)(2,1)S(1)} %copy-done.1, pred[]{:T(512)S(6)} %eq.2), kind=kLoop, calls=%fused_computation.1 | loop fusion | flops 4718592 | bytes 2097153 | tf_op jit(solution)/shard_map/jit(_where)/select_n | solution.py:372
  71.6 6.1 %collective-permute-done.5 = bf16[128,512]{1,0:T(8,128)(2,1)S(1)} collective-permute-done((bf16[128,512]{1,0:T(8,128)(2,1)S(1)}, bf16[128,512]{1,0:T(8,128)(2,1)S(1)}, u32[]{:S(2)}, u32[]{:S(2)}) %collective-permute-start.5) | collective-permute-done | bytes 131104 | tf_op jit(solution)/shard_map/ppermute | solution.py:310
  77.8 0.7 fusion.2
  (30 shorter events, 0.5 us)
Async XLA Ops:
  1.5 17.2 %collective-permute-start.2 = (bf16[128,512]{1,0:T(8,128)(2,1)S(1)}, bf16[128,512]{1,0:T(8,128)(2,1)S(1)}, u32[]{:S(2)}, u32[]{:S(2)}) collective-permute-start(bf16[128,512]{1,0:T(8,128)(2,1)S(1)} %pad_maximum_fusion.1), channel_id=1, source_target_pairs={{0,128},{16,144},{32,160},{48,176},{64,192},{80,208},{96,224},{112... | collective-permute-start | bytes 393224 | tf_op jit(solution)/shard_map/ppermute | solution.py:310
  10.2 17.0 %collective-permute-start = (bf16[128,2048]{1,0:T(8,128)(2,1)S(1)}, bf16[128,2048]{1,0:T(8,128)(2,1)S(1)}, u32[]{:S(2)}, u32[]{:S(2)}) collective-permute-start(bf16[128,2048]{1,0:T(8,128)(2,1)S(1)} %get-tuple-element.17), channel_id=1, source_target_pairs={{0,16},{16,0},{32,48},{48,32},{64,80},{80,64},{96,112},{112,96},{1... | collective-permute-start | bytes 1572872 | tf_op jit(solution)/shard_map/ppermute | solution.py:326
  12.1 15.1 %collective-permute-start.1 = (bf16[128,2048]{1,0:T(8,128)(2,1)S(1)}, bf16[128,2048]{1,0:T(8,128)(2,1)S(1)}, u32[]{:S(2)}, u32[]{:S(2)}) collective-permute-start(bf16[128,2048]{1,0:T(8,128)(2,1)S(1)} %get-tuple-element.18), channel_id=1, source_target_pairs={{0,16},{16,0},{32,48},{48,32},{64,80},{80,64},{96,112},{112,96},{1... | collective-permute-start | bytes 1572872 | tf_op jit(solution)/shard_map/ppermute | solution.py:326
  19.6 14.6 %all-to-all-start = ((bf16[8,128,256]{2,1,0:T(8,128)(2,1)}), bf16[8,128,256]{2,1,0:T(8,128)(2,1)S(1)}, u32[]{:S(2)}, u32[]{:S(2)}) async-start(bf16[8,128,256]{2,1,0:T(8,128)(2,1)} %bitcast_select_fusion), calls=%async_computation | async-start | bytes 1048576 | tf_op jit(solution)/shard_map/all_to_all | solution.py:316
  23.9 3.3 %collective-permute-start.3 = (bf16[128,256]{1,0:T(8,128)(2,1)S(1)}, bf16[128,256]{1,0:T(8,128)(2,1)S(1)}, u32[]{:S(2)}, u32[]{:S(2)}) collective-permute-start(bf16[128,256]{1,0:T(8,128)(2,1)S(1)} %get-tuple-element.19), channel_id=1, source_target_pairs={{0,16},{16,0},{32,48},{48,32},{64,80},{80,64},{96,112},{112,96},{1... | collective-permute-start | bytes 196616 | tf_op jit(solution)/shard_map/ppermute | solution.py:326
  27.2 7.1 %copy-start.7 = (bf16[128,256]{1,0:T(8,128)(2,1)}, bf16[128,256]{1,0:T(8,128)(2,1)S(1)}, u32[]{:S(2)}) copy-start(bf16[128,256]{1,0:T(8,128)(2,1)S(1)} %collective-permute-done.3.own_there_ref) | copy-start | bytes 196612
  27.2 7.1 %copy-start.5 = (bf16[128,2048]{1,0:T(8,128)(2,1)}, bf16[128,2048]{1,0:T(8,128)(2,1)S(1)}, u32[]{:S(2)}) copy-start(bf16[128,2048]{1,0:T(8,128)(2,1)S(1)} %collective-permute-done.q_there_ref) | copy-start | bytes 1572868
  27.2 7.1 %copy-start.6 = (bf16[128,2048]{1,0:T(8,128)(2,1)}, bf16[128,2048]{1,0:T(8,128)(2,1)S(1)}, u32[]{:S(2)}) copy-start(bf16[128,2048]{1,0:T(8,128)(2,1)S(1)} %collective-permute-done.1.do_there_ref) | copy-start | bytes 1572868
  34.3 0.8 %copy-start.3 = (bf16[8,128,256]{2,1,0:T(8,128)(2,1)}, bf16[8,128,256]{2,1,0:T(8,128)(2,1)S(1)}, u32[]{:S(2)}) copy-start(bf16[8,128,256]{2,1,0:T(8,128)(2,1)S(1)} %all-to-all-done.seen_ref) | copy-start | bytes 1572868
  35.1 31.1 %copy-start = (s32[3]{0:T(128)S(1)}, s32[3]{0:T(128)}, u32[]{:S(2)}) copy-start(s32[3]{0:T(128)} %pad_add_fusion.where_ref) | copy-start | bytes 40
  52.4 13.8 %all-to-all-start.1 = ((bf16[8,128,256]{2,1,0:T(8,128)(2,1)}), bf16[8,128,256]{2,1,0:T(8,128)(2,1)S(1)}, u32[]{:S(2)}, u32[]{:S(2)}) async-start(bf16[8,128,256]{2,1,0:T(8,128)(2,1)} %get-tuple-element.20), calls=%async_computation.1 | async-start | bytes 1048576 | tf_op jit(solution)/shard_map/all_to_all | solution.py:316
  55.9 13.0 %collective-permute-start.4 = (bf16[128,4352]{1,0:T(8,128)(2,1)}, bf16[128,4352]{1,0:T(8,128)(2,1)S(1)}, u32[]{:S(2)}, u32[]{:S(2)}) collective-permute-start(bf16[128,4352]{1,0:T(8,128)(2,1)} %get-tuple-element.22), channel_id=1, source_target_pairs={{0,16},{16,0},{32,48},{48,32},{64,80},{80,64},{96,112},{112,96},{1... | collective-permute-start | bytes 3342344 | tf_op jit(solution)/shard_map/ppermute | solution.py:326
  66.8 2.2 %copy-start.2 = (bf16[128,2048]{1,0:T(8,128)(2,1)S(1)}, bf16[128,2048]{1,0:T(8,128)(2,1)}, u32[]{:S(2)}) copy-start(bf16[128,2048]{1,0:T(8,128)(2,1)} %get-tuple-element.23) | copy-start | bytes 1572868
  66.8 10.9 %collective-permute-start.5 = (bf16[128,512]{1,0:T(8,128)(2,1)S(1)}, bf16[128,512]{1,0:T(8,128)(2,1)S(1)}, u32[]{:S(2)}, u32[]{:S(2)}) collective-permute-start(bf16[128,512]{1,0:T(8,128)(2,1)S(1)} %shard_map.85), channel_id=1, source_target_pairs={{128,0},{144,16},{160,32},{176,48},{192,64},{208,80},{224,96},{240... | collective-permute-start | bytes 393224 | tf_op jit(solution)/shard_map/ppermute | solution.py:310
  69.0 1.2 %copy-start.1 = (bf16[128,2048]{1,0:T(8,128)(2,1)S(1)}, bf16[128,2048]{1,0:T(8,128)(2,1)}, u32[]{:S(2)}) copy-start(bf16[128,2048]{1,0:T(8,128)(2,1)} %get-tuple-element.24) | copy-start | bytes 1572868
  70.3 1.2 %copy-start.4 = (bf16[128,256]{1,0:T(8,128)(2,1)S(1)}, bf16[128,256]{1,0:T(8,128)(2,1)}, u32[]{:S(2)}) copy-start(bf16[128,256]{1,0:T(8,128)(2,1)} %get-tuple-element.21) | copy-start | bytes 196612

commit v6 on v5

--- a/solution.py
+++ b/solution.py
@@ -17,6 +17,7 @@
 SCALE2 = SCALE * math.log2(math.e)
 F32 = jnp.float32
 BF16 = jnp.bfloat16
+STEP_ROWS = 2048
 
 
 def dot(a, b, ca, cb):
@@ -38,9 +39,10 @@
     own_here_ref,
     own_there_ref,
     o_here_ref,
-    dq_here_ref,
     there_ref,
     terms_ref,
+    ds_ref,
+    keys_ref,
     mine_here_ref,
     q_side,
     do_side,
@@ -50,7 +52,7 @@
     k_zero,
     v_zero,
     o_side,
-    dq_side,
+    ds_side,
     terms_now,
     own_out,
     dk_acc,
@@ -84,18 +86,22 @@
         ],
     ]
 
-    own_cols = pl.ds(2 * half, 2 * HEAD)
+    own_cols = pl.ds(half, 2 * HEAD)
+    rows = half // HEAD * TOK
     sends = [
         [
             pltpu.make_async_copy(o_side.at[0], o_here_ref, sems.at[4]),
-            pltpu.make_async_copy(dq_side.at[0], dq_here_ref, sems.at[5]),
         ],
         [
             pltpu.make_async_copy(o_side.at[1], there_ref.at[:, pl.ds(0, half)], sems.at[6]),
-            pltpu.make_async_copy(dq_side.at[1], there_ref.at[:, pl.ds(half, half)], sems.at[7]),
             pltpu.make_async_copy(own_out, there_ref.at[:, own_cols], sems.at[8]),
         ],
     ]
+
+    def keep(side, what):
+        if what == 0:
+            return pltpu.make_async_copy(ds_side.at[side], ds_ref.at[pl.ds(side * rows, rows)], sems.at[5 + 2 * side])
+        return pltpu.make_async_copy(k_zero.at[side], keys_ref.at[side], sems.at[9 + 12 * side])
 
     @pl.when(side == 0)
     def _():
@@ -119,11 +125,11 @@
             block = jnp.where(index == 1, own_side[core], block)
         shown = RING - 1 - w <= before
         k_fill[at] = jnp.where(shown, block[:, :HEAD], first)
-        k_zero[at] = jnp.where(shown, block[:, :HEAD], zero)
+        k_zero[side, at] = jnp.where(shown, block[:, :HEAD], zero)
         v_zero[at] = jnp.where(shown, block[:, HEAD:], zero)
     last = slice(KEYS - TOK, KEYS)
     k_fill[last] = own_now[:, :HEAD]
-    k_zero[last] = own_now[:, :HEAD]
+    k_zero[side, last] = own_now[:, :HEAD]
     v_zero[last] = own_now[:, HEAD:]
 
     @pl.when(side == 0)
@@ -135,6 +141,12 @@
     def _():
         for fetch in fetches[1]:
             fetch.wait()
+
+    def start_kept(n):
+        @pl.when(side == n)
+        def _():
+            keep(n, 0).start()
+            keep(n, 1).start()
 
     def attend(tiles):
         width = 2 * tiles * TOK
@@ -143,7 +155,7 @@
         row = lax.broadcasted_iota(jnp.int32, (TOK, TOK), 0)
         col = lax.broadcasted_iota(jnp.int32, (TOK, TOK), 1)
         causal = jnp.where(col <= row, 0.0, -1e30).astype(F32)
-        k, kz, v = k_fill[KEYS - width :], k_zero[KEYS - width :], v_zero[KEYS - width :]
+        k, v = k_fill[KEYS - width :], v_zero[KEYS - width :]
         group_size = 8
         groups = range(0, heads, group_size)
 
@@ -172,14 +184,18 @@
             delta = jnp.sum(do_wide * o.astype(F32), axis=1, keepdims=True) * inv
             do_norm = (do_wide * inv).astype(BF16)
             ds = p_low * (dot(do_norm, v, 1, 1) - delta).astype(BF16)
-            dq = (dot(ds, kz, 1, 0) * SCALE).astype(BF16)
             for r in range(group_size):
                 at = slice((g + r) * HEAD, (g + r + 1) * HEAD)
                 o_side[side, :, at] = o[r * TOK : (r + 1) * TOK]
-                dq_side[side, :, at] = dq[r * TOK : (r + 1) * TOK]
+            at = pl.ds(g * TOK, group_size * TOK)
+            ds_side[side, at, KEYS - width :] = ds
+            if width < KEYS:
+                ds_side[side, at, : KEYS - width] = jnp.zeros((group_size * TOK, KEYS - width), BF16)
             dss.append(ds)
             ps.append(p_low)
             norms.append(do_norm)
+        for n in range(2):
+            start_kept(n)
         ds, p_low, do_norm, q = [jnp.concatenate(x, 0) for x in (dss, ps, norms, qs)]
         place = lax.broadcasted_iota(jnp.int32, (HEAD, width), 1)
         shown = place >= hidden * TOK
@@ -197,8 +213,7 @@
 
     @pl.when(side == 1)
     def _():
-        for send in sends[1][:2]:
-            send.start()
+        sends[1][0].start()
 
         def part(m):
             return pltpu.make_async_copy(terms_now.at[slot(m)], terms_ref.at[slot(m)], sems.at[13 + m])
@@ -219,8 +234,9 @@
         mine_here_ref[:, HEAD:] = jnp.where(swap, odd_v, even_v)
         own_out[:, :HEAD] = jnp.where(swap, even_k, odd_k)
         own_out[:, HEAD:] = jnp.where(swap, even_v, odd_v)
-        sends[1][2].start()
-        for send in sends[0] + sends[1] + [part(m) for m in range(RING)]:
+        sends[1][1].start()
+        kept = [keep(n, what) for n in range(2) for what in range(2)]
+        for send in sends[0] + sends[1] + kept + [part(m) for m in range(RING)]:
             send.wait()
 
 
@@ -228,7 +244,7 @@
     half = q_there.shape
     rows = half[1] // HEAD * TOK
     own = own_here.shape
-    there = (TOK, 2 * half[1] + own[1])
+    there = (TOK, half[1] + own[1])
     vmem = pl.BlockSpec(memory_space=pltpu.VMEM)
     anywhere = pl.BlockSpec(memory_space=pl.ANY)
     return pl.pallas_call(
@@ -237,29 +253,30 @@
             num_scalar_prefetch=1,
             grid=(2,),
             in_specs=[vmem] + [anywhere] * 7,
-            out_specs=[anywhere] * 4 + [vmem],
+            out_specs=[anywhere] * 5 + [vmem],
             scratch_shapes=[
                 pltpu.VMEM((2, *half), BF16),
                 pltpu.VMEM((2, *half), BF16),
                 pltpu.VMEM(seen.shape, BF16),
                 pltpu.VMEM((2, *own), BF16),
                 pltpu.VMEM((KEYS, HEAD), BF16),
-                pltpu.VMEM((KEYS, HEAD), BF16),
+                pltpu.VMEM((2, KEYS, HEAD), BF16),
                 pltpu.VMEM((KEYS, HEAD), BF16),
                 pltpu.VMEM((2, *half), BF16),
-                pltpu.VMEM((2, *half), BF16),
+                pltpu.VMEM((2, rows, KEYS), BF16),
                 pltpu.VMEM(seen.shape, BF16),
                 pltpu.VMEM(own, BF16),
                 pltpu.VMEM((HEAD, SPAN), F32),
                 pltpu.VMEM((HEAD, SPAN), F32),
-                pltpu.SemaphoreType.DMA((13 + RING,)),
+                pltpu.SemaphoreType.DMA((14 + RING,)),
             ],
         ),
         out_shape=[
-            jax.ShapeDtypeStruct(half, BF16),
             jax.ShapeDtypeStruct(half, BF16),
             jax.ShapeDtypeStruct(there, BF16),
             jax.ShapeDtypeStruct(seen.shape, BF16),
+            jax.ShapeDtypeStruct((2 * rows, KEYS), BF16),
+            jax.ShapeDtypeStruct((2, KEYS, HEAD), BF16),
             jax.ShapeDtypeStruct(own, BF16),
         ],
         compiler_params=pltpu.CompilerParams(
@@ -271,6 +288,47 @@
             transcendentals=2 * rows * KEYS,
         ),
     )(where, offsets, queries, cotangent, q_there, do_there, seen, own_here, own_there)
+
+
+def queries_kernel(ds_ref, keys_ref, dq_here_ref, dq_there_ref):
+    dq = (dot(ds_ref[...], keys_ref[0], 1, 0) * SCALE).astype(BF16)
+    steps = pl.num_programs(0) // 2
+
+    def put(ref):
+        for r in range(dq.shape[0] // TOK):
+            ref[:, r * HEAD : (r + 1) * HEAD] = dq[r * TOK : (r + 1) * TOK]
+
+    @pl.when(pl.program_id(0) < steps)
+    def _():
+        put(dq_here_ref)
+
+    @pl.when(pl.program_id(0) >= steps)
+    def _():
+        put(dq_there_ref)
+
+
+def queries_gradient(ds, keys, half):
+    steps = ds.shape[0] // 2 // STEP_ROWS
+    block = (TOK, half[1] // steps)
+    return pl.pallas_call(
+        queries_kernel,
+        grid=(2 * steps,),
+        in_specs=[
+            pl.BlockSpec((STEP_ROWS, KEYS), lambda i: (i, 0)),
+            pl.BlockSpec((1, KEYS, HEAD), lambda i: (i // steps, 0, 0)),
+        ],
+        out_specs=[
+            pl.BlockSpec(block, lambda i: (0, jnp.minimum(i, steps - 1))),
+            pl.BlockSpec(block, lambda i: (0, jnp.maximum(i - steps, 0))),
+        ],
+        out_shape=[jax.ShapeDtypeStruct(half, BF16)] * 2,
+        compiler_params=pltpu.CompilerParams(
+            vmem_limit_bytes=40 << 20, dimension_semantics=("arbitrary",)
+        ),
+        cost_estimate=pl.CostEstimate(
+            flops=2 * ds.size * HEAD, bytes_accessed=2 * ds.size, transcendentals=0
+        ),
+    )(ds, keys)
 
 
 def theirs_kernel(where_ref, terms_ref, out_ref):
@@ -350,7 +408,7 @@
     seen = within_ring(send)
     q_there, do_there, own_there = [to_sibling(a) for a in halves]
     offsets = doc_offsets.reshape(1, -1)
-    o_here, dq_here, there, terms, mine_here = attention(
+    o_here, there, terms, ds, kept_keys, mine_here = attention(
         where, offsets, queries, cotangent, q_there, do_there, seen, heads_of(kv, core), own_there
     )
 
@@ -365,17 +423,18 @@
         jnp.where(j > chip, terms[j], jnp.zeros_like(terms[j])).astype(F32)
         for j in range(1, RING // 2)
     )
-    back = to_sibling(there)
+    dq_here, dq_there = queries_gradient(ds, kept_keys, o_here.shape)
+    back, dq_back = to_sibling(there), to_sibling(dq_there)
     half = o_here.shape[1]
 
     def joined(a, b):
         return jnp.where(core == 0, jnp.concatenate([a, b], 1), jnp.concatenate([b, a], 1))
 
-    attended, grad_q = joined(o_here, back[:, :half]), joined(dq_here, back[:, half : 2 * half])
+    attended, grad_q = joined(o_here, back[:, :half]), joined(dq_here, dq_back)
     local = jnp.where(
         core == 0,
-        jnp.stack([mine_here, back[:, 2 * half :]]),
-        jnp.stack([back[:, 2 * half :], mine_here]),
+        jnp.stack([mine_here, back[:, half:]]),
+        jnp.stack([back[:, half:], mine_here]),
     )
     ours = side_by_side(after + local.astype(F32))
     ours, attended, grad_q = lax.optimization_barrier((ours, attended, grad_q))

time: 79 us -> 80 us (1.013)
  the two profiles are of different devices: /device:TPU:40 before, /device:TPU:56 now
where the time goes in v6:
time: 80 us; the launch traced here: 79 us
  starting transfers between devices  27 us (34%)
  Pallas kernels  19.5 us (24%)
  waiting for transfers between devices  18.6 us (23%)
  local copies, waits for them, and re-layouts  8.81 us (11%)
  other arithmetic  4.14 us (5%)
  between operations  0.9 us (1%)
    pallas_call x1, Pallas kernels, attention(): pl.pallas_call(attention_kernel, grid_spec=pltpu.PrefetchScalarGridSpec(n...  16.1 us
    ppermute x5, starting transfers between devices, to_sibling(): return lax.ppermute(block, 'uly', [(i, i ^ 1) for i in range(lanes)])  11 us
    ppermute x2, waiting for transfers between devices, ring_shift(): return lax.ppermute(block, ('uly', 'blk'), route)  10.7 us
    ppermute x2, starting transfers between devices, ring_shift(): return lax.ppermute(block, ('uly', 'blk'), route)  8.14 us
    all_to_all x2, starting transfers between devices, within_ring(): lax.all_to_all(blocks, 'uly', 0, 0, axis_index_groups=groups, tiled=True)  7.8 us
    all_to_all x2, waiting for transfers between devices, within_ring(): lax.all_to_all(blocks, 'uly', 0, 0, axis_index_groups=groups, tiled=True)  7.04 us
    unnamed x20, local copies, waits for them, and re-layouts  5.24 us
    pallas_call x1, Pallas kernels, queries_gradient(): pl.pallas_call(queries_kernel, grid=(2 * steps,), in_specs=[pl.BlockSpec(...  2.81 us
  transfers between devices with their start and end apart: 9, of which 4 were waited for; matrix products, arithmetic and copies ran while one was open for 8% of the time, Pallas kernels for 4%

profile of v6, /device:TPU:56, one launch (start us, length us, event | category | flops | bytes accessed | tf_op | source)
XLA Modules:
  0.0 79.0 jit_solution(10970391293279137463)
XLA Ops:
  0.6 0.8 %fusion.2 = (bf16[128,128]{1,0:T(8,128)(2,1)S(1)}, bf16[128,128]{1,0:T(8,128)(2,1)S(1)}, bf16[128,128]{1,0:T(8,128)(2,1)S(1)}, bf16[128,128]{1,0:T(8,128)(2,1)S(1)}) fusion(bf16[128,256]{1,0:T(8,128)(2,1)} %param.6, bf16[128,256]{1,0:T(8,128)(2,1)} %param.7), kind=kLoop, calls=%fused_computation.27 | loop fusion | bytes 262144 | tf_op jit(solution)/shard_map/slice | solution.py:403
  1.5 6.1 %collective-permute-start.2 = (bf16[128,512]{1,0:T(8,128)(2,1)S(1)}, bf16[128,512]{1,0:T(8,128)(2,1)S(1)}, u32[]{:S(2)}, u32[]{:S(2)}) collective-permute-start(bf16[128,512]{1,0:T(8,128)(2,1)S(1)} %pad_maximum_fusion.1), channel_id=1, source_target_pairs={{0,128},{16,144},{32,160},{48,176},{64,192},{80,208},{96,224},{112... | collective-permute-start | bytes 393224 | tf_op jit(solution)/shard_map/ppermute | solution.py:368
  8.2 1.3 %constant_dynamic-slice_fusion.2 = (bf16[128,2048]{1,0:T(8,128)(2,1)S(1)}, bf16[128,2048]{1,0:T(8,128)(2,1)S(1)}) fusion(bf16[128,4096]{1,0:T(8,128)(2,1)} %do_here_ref.1, s32[]{:T(128)S(6)} %select_n.62, bf16[128,4096]{1,0:T(8,128)(2,1)} %q_here_ref.1), kind=kLoop, calls=%fused_computation.22 | loop fusion | bytes 2097156 | tf_op jit(solution)/shard_map/dynamic_slice | solution.py:396
  10.1 1.9 %collective-permute-start = (bf16[128,2048]{1,0:T(8,128)(2,1)S(1)}, bf16[128,2048]{1,0:T(8,128)(2,1)S(1)}, u32[]{:S(2)}, u32[]{:S(2)}) collective-permute-start(bf16[128,2048]{1,0:T(8,128)(2,1)S(1)} %get-tuple-element.20), channel_id=1, source_target_pairs={{0,16},{16,0},{32,48},{48,32},{64,80},{80,64},{96,112},{112,96},{1... | collective-permute-start | bytes 1572872 | tf_op jit(solution)/shard_map/ppermute | solution.py:384
  12.0 2.4 %collective-permute-start.1 = (bf16[128,2048]{1,0:T(8,128)(2,1)S(1)}, bf16[128,2048]{1,0:T(8,128)(2,1)S(1)}, u32[]{:S(2)}, u32[]{:S(2)}) collective-permute-start(bf16[128,2048]{1,0:T(8,128)(2,1)S(1)} %get-tuple-element.21), channel_id=1, source_target_pairs={{0,16},{16,0},{32,48},{48,32},{64,80},{80,64},{96,112},{112,96},{1... | collective-permute-start | bytes 1572872 | tf_op jit(solution)/shard_map/ppermute | solution.py:384
  14.5 4.1 %collective-permute-done.2 = bf16[128,512]{1,0:T(8,128)(2,1)S(1)} collective-permute-done((bf16[128,512]{1,0:T(8,128)(2,1)S(1)}, bf16[128,512]{1,0:T(8,128)(2,1)S(1)}, u32[]{:S(2)}, u32[]{:S(2)}) %collective-permute-start.2) | collective-permute-done | bytes 131104 | tf_op jit(solution)/shard_map/ppermute | solution.py:368
  18.7 0.9 %bitcast_select_fusion = bf16[8,128,256]{2,1,0:T(8,128)(2,1)} fusion(pred[8]{0:T(512)(128)(4,1)S(1)} %fusion, bf16[2,128,256]{2,1,0:T(8,128)(2,1)S(1)} %copy.10, bf16[2,128,256]{2,1,0:T(8,128)(2,1)S(1)} %copy.9), kind=kLoop, calls=%fused_computation.2 | loop fusion | flops 262144 | bytes 786440 | tf_op jit(solution)/shard_map/jit(_where)/select_n | solution.py:405
  19.6 4.3 %all-to-all-start = ((bf16[8,128,256]{2,1,0:T(8,128)(2,1)}), bf16[8,128,256]{2,1,0:T(8,128)(2,1)S(1)}, u32[]{:S(2)}, u32[]{:S(2)}) async-start(bf16[8,128,256]{2,1,0:T(8,128)(2,1)} %bitcast_select_fusion), calls=%async_computation | async-start | bytes 1048576 | tf_op jit(solution)/shard_map/all_to_all | solution.py:374
  23.9 2.4 %collective-permute-start.3 = (bf16[128,256]{1,0:T(8,128)(2,1)S(1)}, bf16[128,256]{1,0:T(8,128)(2,1)S(1)}, u32[]{:S(2)}, u32[]{:S(2)}) collective-permute-start(bf16[128,256]{1,0:T(8,128)(2,1)S(1)} %get-tuple-element.22), channel_id=1, source_target_pairs={{0,16},{16,0},{32,48},{48,32},{64,80},{80,64},{96,112},{112,96},{1... | collective-permute-start | bytes 196616 | tf_op jit(solution)/shard_map/ppermute | solution.py:384
  26.3 0.9 %collective-permute-done.3.own_there_ref = bf16[128,256]{1,0:T(8,128)(2,1)S(1)} collective-permute-done((bf16[128,256]{1,0:T(8,128)(2,1)S(1)}, bf16[128,256]{1,0:T(8,128)(2,1)S(1)}, u32[]{:S(2)}, u32[]{:S(2)}) %collective-permute-start.3) | collective-permute-done | bytes 65568 | tf_op jit(solution)/shard_map/ppermute | solution.py:384
  27.2 7.0 %all-to-all-done.seen_ref = bf16[8,128,256]{2,1,0:T(8,128)(2,1)S(1)} async-done(((bf16[8,128,256]{2,1,0:T(8,128)(2,1)}), bf16[8,128,256]{2,1,0:T(8,128)(2,1)S(1)}, u32[]{:S(2)}, u32[]{:S(2)}) %all-to-all-start) | async-done | bytes 524320 | tf_op jit(solution)/shard_map/all_to_all | solution.py:374
  34.3 0.8 %copy-done.4 = bf16[8,128,256]{2,1,0:T(8,128)(2,1)} copy-done((bf16[8,128,256]{2,1,0:T(8,128)(2,1)}, bf16[8,128,256]{2,1,0:T(8,128)(2,1)S(1)}, u32[]{:S(2)}) %copy-start.4) | copy-done | bytes 524312
  35.1 16.1 %shard_map.84 = (bf16[128,2048]{1,0:T(8,128)(2,1)}, bf16[128,2304]{1,0:T(8,128)(2,1)}, bf16[8,128,256]{2,1,0:T(8,128)(2,1)}, bf16[4096,1024]{1,0:T(8,128)(2,1)},...) custom-call(s32[3]{0:T(128)} %pad_add_fusion.where_ref, s32[1,130]{1,0:T(1,128)} %bitcast.28, ...), custom_call_target="tpu_custom_call" | custom-call | flops 6442450944 | bytes 4194304 | tf_op jit(solution)/shard_map/pallas_call | solution.py:250
  51.1 3.5 %all-to-all-start.1 = ((bf16[8,128,256]{2,1,0:T(8,128)(2,1)}), bf16[8,128,256]{2,1,0:T(8,128)(2,1)S(1)}, u32[]{:S(2)}, u32[]{:S(2)}) async-start(bf16[8,128,256]{2,1,0:T(8,128)(2,1)} %get-tuple-element.23), calls=%async_computation.1 | async-start | bytes 1048576 | tf_op jit(solution)/shard_map/all_to_all | solution.py:374
  54.7 3.4 %copy-done = bf16[4096,1024]{1,0:T(8,128)(2,1)S(1)} copy-done((bf16[4096,1024]{1,0:T(8,128)(2,1)S(1)}, bf16[4096,1024]{1,0:T(8,128)(2,1)}, u32[]{:S(2)}) %copy-start) | copy-done | bytes 8388632
  58.1 1.0 %copy-done.1 = bf16[2,1024,128]{2,1,0:T(8,128)(2,1)S(1)} copy-done((bf16[2,1024,128]{2,1,0:T(8,128)(2,1)S(1)}, bf16[2,1024,128]{2,1,0:T(8,128)(2,1)}, u32[]{:S(2)}) %copy-start.1) | copy-done | bytes 524312
  59.1 2.8 %shard_map.85 = (bf16[128,2048]{1,0:T(8,128)(2,1)S(1)}, bf16[128,2048]{1,0:T(8,128)(2,1)S(1)}) custom-call(bf16[4096,1024]{1,0:T(8,128)(2,1)S(1)} %copy-done, bf16[2,1024,128]{2,1,0:T(8,128)(2,1)S(1)} %copy-done.1), custom_call_target="tpu_custom_call" | custom-call | flops 1073741824 | bytes 8388608 | tf_op jit(solution)/shard_map/pallas_call | solution.py:313
  61.9 2.3 %collective-permute-start.5 = (bf16[128,2048]{1,0:T(8,128)(2,1)S(1)}, bf16[128,2048]{1,0:T(8,128)(2,1)S(1)}, u32[]{:S(2)}, u32[]{:S(2)}) collective-permute-start(bf16[128,2048]{1,0:T(8,128)(2,1)S(1)} %get-tuple-element.30), channel_id=1, source_target_pairs={{0,16},{16,0},{32,48},{48,32},{64,80},{80,64},{96,112},{112,96},{1... | collective-permute-start | bytes 1572872 | tf_op jit(solution)/shard_map/ppermute | solution.py:384
  64.2 2.0 %collective-permute-start.4 = (bf16[128,2304]{1,0:T(8,128)(2,1)S(1)}, bf16[128,2304]{1,0:T(8,128)(2,1)S(1)}, u32[]{:S(2)}, u32[]{:S(2)}) collective-permute-start(bf16[128,2304]{1,0:T(8,128)(2,1)S(1)} %copy-done.6), channel_id=1, source_target_pairs={{0,16},{16,0},{32,48},{48,32},{64,80},{80,64},{96,112},{112,96},{1... | collective-permute-start | bytes 1769480 | tf_op jit(solution)/shard_map/ppermute | solution.py:384
  66.9 2.1 %collective-permute-start.6 = (bf16[128,512]{1,0:T(8,128)(2,1)S(1)}, bf16[128,512]{1,0:T(8,128)(2,1)S(1)}, u32[]{:S(2)}, u32[]{:S(2)}) collective-permute-start(bf16[128,512]{1,0:T(8,128)(2,1)S(1)} %shard_map.86), channel_id=1, source_target_pairs={{128,0},{144,16},{160,32},{176,48},{192,64},{208,80},{224,96},{240... | collective-permute-start | bytes 393224 | tf_op jit(solution)/shard_map/ppermute | solution.py:368
  69.0 1.2 %maximum_select_fusion.1 = bf16[128,4096]{1,0:T(8,128)(2,1)} fusion(bf16[128,2048]{1,0:T(8,128)(2,1)S(1)} %collective-permute-done.5, bf16[128,2048]{1,0:T(8,128)(2,1)S(1)} %get-tuple-element.29, pred[]{:T(512)S(6)} %eq.2), kind=kLoop, calls=%fused_computation.1 | loop fusion | flops 4718592 | bytes 2097153 | tf_op jit(solution)/shard_map/jit(_where)/select_n | solution.py:431
  70.3 1.2 %maximum_select_fusion = bf16[128,4096]{1,0:T(8,128)(2,1)} fusion(bf16[128,2048]{1,0:T(8,128)(2,1)S(1)} %slice.72, bf16[128,2048]{1,0:T(8,128)(2,1)S(1)} %copy-done.3, pred[]{:T(512)S(6)} %eq.2), kind=kLoop, calls=%fused_computation | loop fusion | flops 4718592 | bytes 2097153 | tf_op jit(solution)/shard_map/jit(_where)/select_n | solution.py:431
  71.7 6.6 %collective-permute-done.6 = bf16[128,512]{1,0:T(8,128)(2,1)S(1)} collective-permute-done((bf16[128,512]{1,0:T(8,128)(2,1)S(1)}, bf16[128,512]{1,0:T(8,128)(2,1)S(1)}, u32[]{:S(2)}, u32[]{:S(2)}) %collective-permute-start.6) | collective-permute-done | bytes 131104 | tf_op jit(solution)/shard_map/ppermute | solution.py:368
  78.3 0.7 fusion.1
  (37 shorter events, 2.3 us)
Async XLA Ops:
  1.5 17.2 %collective-permute-start.2 = (bf16[128,512]{1,0:T(8,128)(2,1)S(1)}, bf16[128,512]{1,0:T(8,128)(2,1)S(1)}, u32[]{:S(2)}, u32[]{:S(2)}) collective-permute-start(bf16[128,512]{1,0:T(8,128)(2,1)S(1)} %pad_maximum_fusion.1), channel_id=1, source_target_pairs={{0,128},{16,144},{32,160},{48,176},{64,192},{80,208},{96,224},{112... | collective-permute-start | bytes 393224 | tf_op jit(solution)/shard_map/ppermute | solution.py:368
  10.1 17.1 %collective-permute-start = (bf16[128,2048]{1,0:T(8,128)(2,1)S(1)}, bf16[128,2048]{1,0:T(8,128)(2,1)S(1)}, u32[]{:S(2)}, u32[]{:S(2)}) collective-permute-start(bf16[128,2048]{1,0:T(8,128)(2,1)S(1)} %get-tuple-element.20), channel_id=1, source_target_pairs={{0,16},{16,0},{32,48},{48,32},{64,80},{80,64},{96,112},{112,96},{1... | collective-permute-start | bytes 1572872 | tf_op jit(solution)/shard_map/ppermute | solution.py:384
  12.0 15.2 %collective-permute-start.1 = (bf16[128,2048]{1,0:T(8,128)(2,1)S(1)}, bf16[128,2048]{1,0:T(8,128)(2,1)S(1)}, u32[]{:S(2)}, u32[]{:S(2)}) collective-permute-start(bf16[128,2048]{1,0:T(8,128)(2,1)S(1)} %get-tuple-element.21), channel_id=1, source_target_pairs={{0,16},{16,0},{32,48},{48,32},{64,80},{80,64},{96,112},{112,96},{1... | collective-permute-start | bytes 1572872 | tf_op jit(solution)/shard_map/ppermute | solution.py:384
  19.6 14.6 %all-to-all-start = ((bf16[8,128,256]{2,1,0:T(8,128)(2,1)}), bf16[8,128,256]{2,1,0:T(8,128)(2,1)S(1)}, u32[]{:S(2)}, u32[]{:S(2)}) async-start(bf16[8,128,256]{2,1,0:T(8,128)(2,1)} %bitcast_select_fusion), calls=%async_computation | async-start | bytes 1048576 | tf_op jit(solution)/shard_map/all_to_all | solution.py:374
  23.9 3.3 %collective-permute-start.3 = (bf16[128,256]{1,0:T(8,128)(2,1)S(1)}, bf16[128,256]{1,0:T(8,128)(2,1)S(1)}, u32[]{:S(2)}, u32[]{:S(2)}) collective-permute-start(bf16[128,256]{1,0:T(8,128)(2,1)S(1)} %get-tuple-element.22), channel_id=1, source_target_pairs={{0,16},{16,0},{32,48},{48,32},{64,80},{80,64},{96,112},{112,96},{1... | collective-permute-start | bytes 196616 | tf_op jit(solution)/shard_map/ppermute | solution.py:384
  27.2 7.1 %copy-start.9 = (bf16[128,256]{1,0:T(8,128)(2,1)}, bf16[128,256]{1,0:T(8,128)(2,1)S(1)}, u32[]{:S(2)}) copy-start(bf16[128,256]{1,0:T(8,128)(2,1)S(1)} %collective-permute-done.3.own_there_ref) | copy-start | bytes 196612
  27.2 7.1 %copy-start.7 = (bf16[128,2048]{1,0:T(8,128)(2,1)}, bf16[128,2048]{1,0:T(8,128)(2,1)S(1)}, u32[]{:S(2)}) copy-start(bf16[128,2048]{1,0:T(8,128)(2,1)S(1)} %collective-permute-done.q_there_ref) | copy-start | bytes 1572868
  27.2 7.1 %copy-start.8 = (bf16[128,2048]{1,0:T(8,128)(2,1)}, bf16[128,2048]{1,0:T(8,128)(2,1)S(1)}, u32[]{:S(2)}) copy-start(bf16[128,2048]{1,0:T(8,128)(2,1)S(1)} %collective-permute-done.1.do_there_ref) | copy-start | bytes 1572868
  34.3 0.8 %copy-start.4 = (bf16[8,128,256]{2,1,0:T(8,128)(2,1)}, bf16[8,128,256]{2,1,0:T(8,128)(2,1)S(1)}, u32[]{:S(2)}) copy-start(bf16[8,128,256]{2,1,0:T(8,128)(2,1)S(1)} %all-to-all-done.seen_ref) | copy-start | bytes 1572868
  51.1 15.1 %all-to-all-start.1 = ((bf16[8,128,256]{2,1,0:T(8,128)(2,1)}), bf16[8,128,256]{2,1,0:T(8,128)(2,1)S(1)}, u32[]{:S(2)}, u32[]{:S(2)}) async-start(bf16[8,128,256]{2,1,0:T(8,128)(2,1)} %get-tuple-element.23), calls=%async_computation.1 | async-start | bytes 1048576 | tf_op jit(solution)/shard_map/all_to_all | solution.py:374
  54.7 3.4 %copy-start = (bf16[4096,1024]{1,0:T(8,128)(2,1)S(1)}, bf16[4096,1024]{1,0:T(8,128)(2,1)}, u32[]{:S(2)}) copy-start(bf16[4096,1024]{1,0:T(8,128)(2,1)} %get-tuple-element.27.ds_ref) | copy-start | bytes 25165828
  58.0 1.0 %copy-start.1 = (bf16[2,1024,128]{2,1,0:T(8,128)(2,1)S(1)}, bf16[2,1024,128]{2,1,0:T(8,128)(2,1)}, u32[]{:S(2)}) copy-start(bf16[2,1024,128]{2,1,0:T(8,128)(2,1)} %get-tuple-element.28.keys_ref) | copy-start | bytes 1572868
  59.1 5.1 %copy-start.6 = (bf16[128,2304]{1,0:T(8,128)(2,1)S(1)}, bf16[128,2304]{1,0:T(8,128)(2,1)}, u32[]{:S(2)}) copy-start(bf16[128,2304]{1,0:T(8,128)(2,1)} %get-tuple-element.25) | copy-start | bytes 1769476
  59.1 7.2 %copy-start.2 = (s32[3]{0:T(128)S(1)}, s32[3]{0:T(128)}, u32[]{:S(2)}) copy-start(s32[3]{0:T(128)} %pad_add_fusion.where_ref) | copy-start | bytes 40
  61.9 7.1 %collective-permute-start.5 = (bf16[128,2048]{1,0:T(8,128)(2,1)S(1)}, bf16[128,2048]{1,0:T(8,128)(2,1)S(1)}, u32[]{:S(2)}, u32[]{:S(2)}) collective-permute-start(bf16[128,2048]{1,0:T(8,128)(2,1)S(1)} %get-tuple-element.30), channel_id=1, source_target_pairs={{0,16},{16,0},{32,48},{48,32},{64,80},{80,64},{96,112},{112,96},{1... | collective-permute-start | bytes 1572872 | tf_op jit(solution)/shard_map/ppermute | solution.py:384
  64.2 6.0 %collective-permute-start.4 = (bf16[128,2304]{1,0:T(8,128)(2,1)S(1)}, bf16[128,2304]{1,0:T(8,128)(2,1)S(1)}, u32[]{:S(2)}, u32[]{:S(2)}) collective-permute-start(bf16[128,2304]{1,0:T(8,128)(2,1)S(1)} %copy-done.6), channel_id=1, source_target_pairs={{0,16},{16,0},{32,48},{48,32},{64,80},{80,64},{96,112},{112,96},{1... | collective-permute-start | bytes 1769480 | tf_op jit(solution)/shard_map/ppermute | solution.py:384
  66.9 3.4 %copy-start.3 = (bf16[128,2048]{1,0:T(8,128)(2,1)S(1)}, bf16[128,2048]{1,0:T(8,128)(2,1)}, u32[]{:S(2)}) copy-start(bf16[128,2048]{1,0:T(8,128)(2,1)} %get-tuple-element.26) | copy-start | bytes 1572868
  66.9 11.3 %collective-permute-start.6 = (bf16[128,512]{1,0:T(8,128)(2,1)S(1)}, bf16[128,512]{1,0:T(8,128)(2,1)S(1)}, u32[]{:S(2)}, u32[]{:S(2)}) collective-permute-start(bf16[128,512]{1,0:T(8,128)(2,1)S(1)} %shard_map.86), channel_id=1, source_target_pairs={{128,0},{144,16},{160,32},{176,48},{192,64},{208,80},{224,96},{240... | collective-permute-start | bytes 393224 | tf_op jit(solution)/shard_map/ppermute | solution.py:368
  70.2 1.3 %copy-start.5 = (bf16[128,256]{1,0:T(8,128)(2,1)S(1)}, bf16[128,256]{1,0:T(8,128)(2,1)}, u32[]{:S(2)}) copy-start(bf16[128,256]{1,0:T(8,128)(2,1)} %get-tuple-element.24) | copy-start | bytes 196612

commit v7 on v5

--- a/solution.py
+++ b/solution.py
@@ -136,6 +136,12 @@
         for fetch in fetches[1]:
             fetch.wait()
 
+    def start_sends(n):
+        @pl.when(side == n)
+        def _():
+            for send in sends[n][:2]:
+                send.start()
+
     def attend(tiles):
         width = 2 * tiles * TOK
         heads = half // HEAD
@@ -180,6 +186,8 @@
             dss.append(ds)
             ps.append(p_low)
             norms.append(do_norm)
+        for n in range(2):
+            start_sends(n)
         ds, p_low, do_norm, q = [jnp.concatenate(x, 0) for x in (dss, ps, norms, qs)]
         place = lax.broadcasted_iota(jnp.int32, (HEAD, width), 1)
         shown = place >= hidden * TOK
@@ -190,16 +198,8 @@
     for tiles in range(1, RING // 2 + 1):
         pl.when(lax.shift_right_logical(before, 1) == tiles - 1)(functools.partial(attend, tiles))
 
-    @pl.when(side == 0)
-    def _():
-        for send in sends[0]:
-            send.start()
-
     @pl.when(side == 1)
     def _():
-        for send in sends[1][:2]:
-            send.start()
-
         def part(m):
             return pltpu.make_async_copy(terms_now.at[slot(m)], terms_ref.at[slot(m)], sems.at[13 + m])
 
@@ -263,7 +263,7 @@
             jax.ShapeDtypeStruct(own, BF16),
         ],
         compiler_params=pltpu.CompilerParams(
-            vmem_limit_bytes=60 << 20, dimension_semantics=("arbitrary",)
+            vmem_limit_bytes=62 << 20, dimension_semantics=("arbitrary",)
         ),
         cost_estimate=pl.CostEstimate(
             flops=24 * rows * KEYS * HEAD,

time: 79 us -> 80.2 us (1.015)
  the two profiles are of different devices: /device:TPU:40 before, /device:TPU:56 now
where the time goes in v7:
time: 80.2 us; the launch traced here: 79.7 us
  waiting for transfers between devices  25.9 us (32%)
  starting transfers between devices  24.9 us (31%)
  Pallas kernels  19.3 us (24%)
  local copies, waits for them, and re-layouts  4.47 us (6%)
  other arithmetic  4.2 us (5%)
  between operations  0.87 us (1%)
    pallas_call x1, Pallas kernels, attention(): pl.pallas_call(attention_kernel, grid_spec=pltpu.PrefetchScalarGridSpec(n...  18.6 us
    all_to_all x2, waiting for transfers between devices, within_ring(): lax.all_to_all(blocks, 'uly', 0, 0, axis_index_groups=groups, tiled=True)  15 us
    ppermute x2, waiting for transfers between devices, ring_shift(): return lax.ppermute(block, ('uly', 'blk'), route)  10.1 us
    ppermute x4, starting transfers between devices, to_sibling(): return lax.ppermute(block, 'uly', [(i, i ^ 1) for i in range(lanes)])  9 us
    ppermute x2, starting transfers between devices, ring_shift(): return lax.ppermute(block, ('uly', 'blk'), route)  8.14 us
    all_to_all x2, starting transfers between devices, within_ring(): lax.all_to_all(blocks, 'uly', 0, 0, axis_index_groups=groups, tiled=True)  7.8 us
    select_n x2, other arithmetic, joined(): jnp.where(core == 0, jnp.concatenate([a, b], 1), jnp.concatenate([b, a], 1))  2.43 us
    dynamic_slice x2, local copies, waits for them, and re-layouts, heads_of(): return lax.dynamic_slice_in_dim(block, group * width, width, 1)  1.91 us
  transfers between devices with their start and end apart: 8, of which 5 were waited for; matrix products, arithmetic and copies ran while one was open for 8% of the time, Pallas kernels for 1%

profile of v7, /device:TPU:56, one launch (start us, length us, event | category | flops | bytes accessed | tf_op | source)
XLA Modules:
  0.0 79.7 jit_solution(4207589068007201188)
XLA Ops:
  0.6 0.8 %fusion.3 = (bf16[128,128]{1,0:T(8,128)(2,1)S(1)}, bf16[128,128]{1,0:T(8,128)(2,1)S(1)}, bf16[128,128]{1,0:T(8,128)(2,1)S(1)}, bf16[128,128]{1,0:T(8,128)(2,1)S(1)}) fusion(bf16[128,256]{1,0:T(8,128)(2,1)} %param.6, bf16[128,256]{1,0:T(8,128)(2,1)} %param.7), kind=kLoop, calls=%fused_computation.28 | loop fusion | bytes 262144 | tf_op jit(solution)/shard_map/slice | solution.py:345
  1.5 6.1 %collective-permute-start.2 = (bf16[128,512]{1,0:T(8,128)(2,1)S(1)}, bf16[128,512]{1,0:T(8,128)(2,1)S(1)}, u32[]{:S(2)}, u32[]{:S(2)}) collective-permute-start(bf16[128,512]{1,0:T(8,128)(2,1)S(1)} %pad_maximum_fusion.1), channel_id=1, source_target_pairs={{0,128},{16,144},{32,160},{48,176},{64,192},{80,208},{96,224},{112... | collective-permute-start | bytes 393224 | tf_op jit(solution)/shard_map/ppermute | solution.py:310
  7.6 0.6 constant_dynamic-slice_fusion
  8.2 1.3 %constant_dynamic-slice_fusion.2 = (bf16[128,2048]{1,0:T(8,128)(2,1)S(1)}, bf16[128,2048]{1,0:T(8,128)(2,1)S(1)}) fusion(bf16[128,4096]{1,0:T(8,128)(2,1)} %do_here_ref.1, s32[]{:T(128)S(6)} %select_n.62, bf16[128,4096]{1,0:T(8,128)(2,1)} %q_here_ref.1), kind=kLoop, calls=%fused_computation.22 | loop fusion | bytes 2097156 | tf_op jit(solution)/shard_map/dynamic_slice | solution.py:338
  9.5 0.7 pad_add_fusion.where_ref
  10.2 1.9 %collective-permute-start = (bf16[128,2048]{1,0:T(8,128)(2,1)S(1)}, bf16[128,2048]{1,0:T(8,128)(2,1)S(1)}, u32[]{:S(2)}, u32[]{:S(2)}) collective-permute-start(bf16[128,2048]{1,0:T(8,128)(2,1)S(1)} %get-tuple-element.17), channel_id=1, source_target_pairs={{0,16},{16,0},{32,48},{48,32},{64,80},{80,64},{96,112},{112,96},{1... | collective-permute-start | bytes 1572872 | tf_op jit(solution)/shard_map/ppermute | solution.py:326
  12.1 2.4 %collective-permute-start.1 = (bf16[128,2048]{1,0:T(8,128)(2,1)S(1)}, bf16[128,2048]{1,0:T(8,128)(2,1)S(1)}, u32[]{:S(2)}, u32[]{:S(2)}) collective-permute-start(bf16[128,2048]{1,0:T(8,128)(2,1)S(1)} %get-tuple-element.18), channel_id=1, source_target_pairs={{0,16},{16,0},{32,48},{48,32},{64,80},{80,64},{96,112},{112,96},{1... | collective-permute-start | bytes 1572872 | tf_op jit(solution)/shard_map/ppermute | solution.py:326
  14.6 4.1 %collective-permute-done.2 = bf16[128,512]{1,0:T(8,128)(2,1)S(1)} collective-permute-done((bf16[128,512]{1,0:T(8,128)(2,1)S(1)}, bf16[128,512]{1,0:T(8,128)(2,1)S(1)}, u32[]{:S(2)}, u32[]{:S(2)}) %collective-permute-start.2) | collective-permute-done | bytes 131104 | tf_op jit(solution)/shard_map/ppermute | solution.py:310
  18.7 0.9 %bitcast_select_fusion = bf16[8,128,256]{2,1,0:T(8,128)(2,1)} fusion(pred[8]{0:T(512)(128)(4,1)S(1)} %fusion, bf16[2,128,256]{2,1,0:T(8,128)(2,1)S(1)} %copy.10, bf16[2,128,256]{2,1,0:T(8,128)(2,1)S(1)} %copy.9), kind=kLoop, calls=%fused_computation.2 | loop fusion | flops 262144 | bytes 786440 | tf_op jit(solution)/shard_map/jit(_where)/select_n | solution.py:347
  19.6 4.3 %all-to-all-start = ((bf16[8,128,256]{2,1,0:T(8,128)(2,1)}), bf16[8,128,256]{2,1,0:T(8,128)(2,1)S(1)}, u32[]{:S(2)}, u32[]{:S(2)}) async-start(bf16[8,128,256]{2,1,0:T(8,128)(2,1)} %bitcast_select_fusion), calls=%async_computation | async-start | bytes 1048576 | tf_op jit(solution)/shard_map/all_to_all | solution.py:316
  23.9 2.4 %collective-permute-start.3 = (bf16[128,256]{1,0:T(8,128)(2,1)S(1)}, bf16[128,256]{1,0:T(8,128)(2,1)S(1)}, u32[]{:S(2)}, u32[]{:S(2)}) collective-permute-start(bf16[128,256]{1,0:T(8,128)(2,1)S(1)} %get-tuple-element.19), channel_id=1, source_target_pairs={{0,16},{16,0},{32,48},{48,32},{64,80},{80,64},{96,112},{112,96},{1... | collective-permute-start | bytes 196616 | tf_op jit(solution)/shard_map/ppermute | solution.py:326
  26.3 0.9 %collective-permute-done.3.own_there_ref = bf16[128,256]{1,0:T(8,128)(2,1)S(1)} collective-permute-done((bf16[128,256]{1,0:T(8,128)(2,1)S(1)}, bf16[128,256]{1,0:T(8,128)(2,1)S(1)}, u32[]{:S(2)}, u32[]{:S(2)}) %collective-permute-start.3) | collective-permute-done | bytes 65568 | tf_op jit(solution)/shard_map/ppermute | solution.py:326
  27.2 7.0 %all-to-all-done.seen_ref = bf16[8,128,256]{2,1,0:T(8,128)(2,1)S(1)} async-done(((bf16[8,128,256]{2,1,0:T(8,128)(2,1)}), bf16[8,128,256]{2,1,0:T(8,128)(2,1)S(1)}, u32[]{:S(2)}, u32[]{:S(2)}) %all-to-all-start) | async-done | bytes 524320 | tf_op jit(solution)/shard_map/all_to_all | solution.py:316
  34.3 0.8 copy-done.3
  35.1 18.6 %shard_map.84 = (bf16[128,2048]{1,0:T(8,128)(2,1)}, bf16[128,2048]{1,0:T(8,128)(2,1)}, bf16[128,4352]{1,0:T(8,128)(2,1)}, bf16[8,128,256]{2,1,0:T(8,128)(2,1)}, bf16[128,256]{1,0:T(8,128)(2,1)}) custom-call(s32[3]{0:T(128)} %pad_add_fusion.where_ref, s32[1,130]{1,0:T(1,128)} %bitcast.28, bf16[128,4096]{1,0:T(8,128)(2,1)} %q_here_ref.1, ...), custom_call_target="tpu_custom_call" | custom-call | flops 6442450944 | bytes 4194304 | tf_op jit(solution)/shard_map/pallas_call | solution.py:234
  53.7 3.5 %all-to-all-start.1 = ((bf16[8,128,256]{2,1,0:T(8,128)(2,1)}), bf16[8,128,256]{2,1,0:T(8,128)(2,1)S(1)}, u32[]{:S(2)}, u32[]{:S(2)}) async-start(bf16[8,128,256]{2,1,0:T(8,128)(2,1)} %get-tuple-element.20), calls=%async_computation.1 | async-start | bytes 1048576 | tf_op jit(solution)/shard_map/all_to_all | solution.py:316
  57.2 2.3 %collective-permute-start.4 = (bf16[128,4352]{1,0:T(8,128)(2,1)}, bf16[128,4352]{1,0:T(8,128)(2,1)S(1)}, u32[]{:S(2)}, u32[]{:S(2)}) collective-permute-start(bf16[128,4352]{1,0:T(8,128)(2,1)} %get-tuple-element.22), channel_id=1, source_target_pairs={{0,16},{16,0},{32,48},{48,32},{64,80},{80,64},{96,112},{112,96},{1... | collective-permute-start | bytes 3342344 | tf_op jit(solution)/shard_map/ppermute | solution.py:326
  59.5 8.0 %all-to-all-done.1.terms_ref = bf16[8,128,256]{2,1,0:T(8,128)(2,1)S(1)} async-done(((bf16[8,128,256]{2,1,0:T(8,128)(2,1)}), bf16[8,128,256]{2,1,0:T(8,128)(2,1)S(1)}, u32[]{:S(2)}, u32[]{:S(2)}) %all-to-all-start.1) | async-done | bytes 524320 | tf_op jit(solution)/shard_map/all_to_all | solution.py:316
  67.5 0.6 shard_map.85
  68.2 2.1 %collective-permute-start.5 = (bf16[128,512]{1,0:T(8,128)(2,1)S(1)}, bf16[128,512]{1,0:T(8,128)(2,1)S(1)}, u32[]{:S(2)}, u32[]{:S(2)}) collective-permute-start(bf16[128,512]{1,0:T(8,128)(2,1)S(1)} %shard_map.85), channel_id=1, source_target_pairs={{128,0},{144,16},{160,32},{176,48},{192,64},{208,80},{224,96},{240... | collective-permute-start | bytes 393224 | tf_op jit(solution)/shard_map/ppermute | solution.py:310
  70.4 1.2 %maximum_select_fusion = bf16[128,4096]{1,0:T(8,128)(2,1)} fusion(bf16[128,2048]{1,0:T(8,128)(2,1)S(1)} %get-tuple-element.29, bf16[128,2048]{1,0:T(8,128)(2,1)S(1)} %copy-done.2, pred[]{:T(512)S(6)} %eq.2), kind=kLoop, calls=%fused_computation | loop fusion | flops 4718592 | bytes 2097153 | tf_op jit(solution)/shard_map/jit(_where)/select_n | solution.py:372
  71.6 1.2 %maximum_select_fusion.1 = bf16[128,4096]{1,0:T(8,128)(2,1)} fusion(bf16[128,2048]{1,0:T(8,128)(2,1)S(1)} %get-tuple-element.28, bf16[128,2048]{1,0:T(8,128)(2,1)S(1)} %copy-done.1, pred[]{:T(512)S(6)} %eq.2), kind=kLoop, calls=%fused_computation.1 | loop fusion | flops 4718592 | bytes 2097153 | tf_op jit(solution)/shard_map/jit(_where)/select_n | solution.py:372
  73.0 6.0 %collective-permute-done.5 = bf16[128,512]{1,0:T(8,128)(2,1)S(1)} collective-permute-done((bf16[128,512]{1,0:T(8,128)(2,1)S(1)}, bf16[128,512]{1,0:T(8,128)(2,1)S(1)}, u32[]{:S(2)}, u32[]{:S(2)}) %collective-permute-start.5) | collective-permute-done | bytes 131104 | tf_op jit(solution)/shard_map/ppermute | solution.py:310
  79.0 0.7 fusion.2
  (30 shorter events, 0.5 us)
Async XLA Ops:
  1.5 17.2 %collective-permute-start.2 = (bf16[128,512]{1,0:T(8,128)(2,1)S(1)}, bf16[128,512]{1,0:T(8,128)(2,1)S(1)}, u32[]{:S(2)}, u32[]{:S(2)}) collective-permute-start(bf16[128,512]{1,0:T(8,128)(2,1)S(1)} %pad_maximum_fusion.1), channel_id=1, source_target_pairs={{0,128},{16,144},{32,160},{48,176},{64,192},{80,208},{96,224},{112... | collective-permute-start | bytes 393224 | tf_op jit(solution)/shard_map/ppermute | solution.py:310
  10.2 17.0 %collective-permute-start = (bf16[128,2048]{1,0:T(8,128)(2,1)S(1)}, bf16[128,2048]{1,0:T(8,128)(2,1)S(1)}, u32[]{:S(2)}, u32[]{:S(2)}) collective-permute-start(bf16[128,2048]{1,0:T(8,128)(2,1)S(1)} %get-tuple-element.17), channel_id=1, source_target_pairs={{0,16},{16,0},{32,48},{48,32},{64,80},{80,64},{96,112},{112,96},{1... | collective-permute-start | bytes 1572872 | tf_op jit(solution)/shard_map/ppermute | solution.py:326
  12.1 15.1 %collective-permute-start.1 = (bf16[128,2048]{1,0:T(8,128)(2,1)S(1)}, bf16[128,2048]{1,0:T(8,128)(2,1)S(1)}, u32[]{:S(2)}, u32[]{:S(2)}) collective-permute-start(bf16[128,2048]{1,0:T(8,128)(2,1)S(1)} %get-tuple-element.18), channel_id=1, source_target_pairs={{0,16},{16,0},{32,48},{48,32},{64,80},{80,64},{96,112},{112,96},{1... | collective-permute-start | bytes 1572872 | tf_op jit(solution)/shard_map/ppermute | solution.py:326
  19.6 14.6 %all-to-all-start = ((bf16[8,128,256]{2,1,0:T(8,128)(2,1)}), bf16[8,128,256]{2,1,0:T(8,128)(2,1)S(1)}, u32[]{:S(2)}, u32[]{:S(2)}) async-start(bf16[8,128,256]{2,1,0:T(8,128)(2,1)} %bitcast_select_fusion), calls=%async_computation | async-start | bytes 1048576 | tf_op jit(solution)/shard_map/all_to_all | solution.py:316
  23.9 3.3 %collective-permute-start.3 = (bf16[128,256]{1,0:T(8,128)(2,1)S(1)}, bf16[128,256]{1,0:T(8,128)(2,1)S(1)}, u32[]{:S(2)}, u32[]{:S(2)}) collective-permute-start(bf16[128,256]{1,0:T(8,128)(2,1)S(1)} %get-tuple-element.19), channel_id=1, source_target_pairs={{0,16},{16,0},{32,48},{48,32},{64,80},{80,64},{96,112},{112,96},{1... | collective-permute-start | bytes 196616 | tf_op jit(solution)/shard_map/ppermute | solution.py:326
  27.2 7.1 %copy-start.7 = (bf16[128,256]{1,0:T(8,128)(2,1)}, bf16[128,256]{1,0:T(8,128)(2,1)S(1)}, u32[]{:S(2)}) copy-start(bf16[128,256]{1,0:T(8,128)(2,1)S(1)} %collective-permute-done.3.own_there_ref) | copy-start | bytes 196612
  27.2 7.1 %copy-start.5 = (bf16[128,2048]{1,0:T(8,128)(2,1)}, bf16[128,2048]{1,0:T(8,128)(2,1)S(1)}, u32[]{:S(2)}) copy-start(bf16[128,2048]{1,0:T(8,128)(2,1)S(1)} %collective-permute-done.q_there_ref) | copy-start | bytes 1572868
  27.2 7.1 %copy-start.6 = (bf16[128,2048]{1,0:T(8,128)(2,1)}, bf16[128,2048]{1,0:T(8,128)(2,1)S(1)}, u32[]{:S(2)}) copy-start(bf16[128,2048]{1,0:T(8,128)(2,1)S(1)} %collective-permute-done.1.do_there_ref) | copy-start | bytes 1572868
  34.3 0.8 %copy-start.3 = (bf16[8,128,256]{2,1,0:T(8,128)(2,1)}, bf16[8,128,256]{2,1,0:T(8,128)(2,1)S(1)}, u32[]{:S(2)}) copy-start(bf16[8,128,256]{2,1,0:T(8,128)(2,1)S(1)} %all-to-all-done.seen_ref) | copy-start | bytes 1572868
  35.1 32.4 %copy-start = (s32[3]{0:T(128)S(1)}, s32[3]{0:T(128)}, u32[]{:S(2)}) copy-start(s32[3]{0:T(128)} %pad_add_fusion.where_ref) | copy-start | bytes 40
  53.7 13.8 %all-to-all-start.1 = ((bf16[8,128,256]{2,1,0:T(8,128)(2,1)}), bf16[8,128,256]{2,1,0:T(8,128)(2,1)S(1)}, u32[]{:S(2)}, u32[]{:S(2)}) async-start(bf16[8,128,256]{2,1,0:T(8,128)(2,1)} %get-tuple-element.20), calls=%async_computation.1 | async-start | bytes 1048576 | tf_op jit(solution)/shard_map/all_to_all | solution.py:316
  57.2 13.0 %collective-permute-start.4 = (bf16[128,4352]{1,0:T(8,128)(2,1)}, bf16[128,4352]{1,0:T(8,128)(2,1)S(1)}, u32[]{:S(2)}, u32[]{:S(2)}) collective-permute-start(bf16[128,4352]{1,0:T(8,128)(2,1)} %get-tuple-element.22), channel_id=1, source_target_pairs={{0,16},{16,0},{32,48},{48,32},{64,80},{80,64},{96,112},{112,96},{1... | collective-permute-start | bytes 3342344 | tf_op jit(solution)/shard_map/ppermute | solution.py:326
  68.1 2.2 %copy-start.2 = (bf16[128,2048]{1,0:T(8,128)(2,1)S(1)}, bf16[128,2048]{1,0:T(8,128)(2,1)}, u32[]{:S(2)}) copy-start(bf16[128,2048]{1,0:T(8,128)(2,1)} %get-tuple-element.23) | copy-start | bytes 1572868
  68.2 10.8 %collective-permute-start.5 = (bf16[128,512]{1,0:T(8,128)(2,1)S(1)}, bf16[128,512]{1,0:T(8,128)(2,1)S(1)}, u32[]{:S(2)}, u32[]{:S(2)}) collective-permute-start(bf16[128,512]{1,0:T(8,128)(2,1)S(1)} %shard_map.85), channel_id=1, source_target_pairs={{128,0},{144,16},{160,32},{176,48},{192,64},{208,80},{224,96},{240... | collective-permute-start | bytes 393224 | tf_op jit(solution)/shard_map/ppermute | solution.py:310
  70.4 1.2 %copy-start.1 = (bf16[128,2048]{1,0:T(8,128)(2,1)S(1)}, bf16[128,2048]{1,0:T(8,128)(2,1)}, u32[]{:S(2)}) copy-start(bf16[128,2048]{1,0:T(8,128)(2,1)} %get-tuple-element.24) | copy-start | bytes 1572868
  71.6 1.2 %copy-start.4 = (bf16[128,256]{1,0:T(8,128)(2,1)S(1)}, bf16[128,256]{1,0:T(8,128)(2,1)}, u32[]{:S(2)}) copy-start(bf16[128,256]{1,0:T(8,128)(2,1)} %get-tuple-element.21) | copy-start | bytes 196612
